TPU v7x, 256 devices: a whole 4x4x8 slice. The times are simulated.
256 devices in a mesh: section: 4 (over z_lo, core), seq: 64 (over z_hi, x, y).
Axes of the slice: x: 4, y: 4, z: 8 (z_hi: 4, z_lo: 2; z = z_hi * 2 + z_lo), core: 2. Of those that a mesh axis runs over, the one named last changes fastest.
Arguments:
- queries: bfloat16 [4, 16384, 3072], P('section', 'seq'), may hold values from -0.75 to 0.75
- out_grads: bfloat16 [4, 16384, 3072], P('section', 'seq'), may hold values from -0.59765625 to 0.59765625
- logsumexp: float32 [4, 24, 16384], P('section', None, 'seq'), may hold values from 3.5 to 5.5
- shared_keys: bfloat16 [1024, 1024], P('seq'), may hold values from -48 to 48
- shared_values: bfloat16 [1024, 1024], P('seq'), may hold values from -6 to 6
- query_starts: int32 [64], P('seq'), may hold values from 0 to 16383, as said below
- slab_starts: int32 [64], P('seq'), may hold values from 0 to 16383, as said below
Outputs:
- query_grads: float32 [4, 16384, 3072], P('section', 'seq')
- key_grads: float32 [1024, 1024], P('seq', 'section')
- value_grads: float32 [1024, 1024], P('seq', 'section')
Inputs may be any that keep to these rules, and one draw needn't show every extreme that they name: s * 256 <= query_starts[s] < (s + 1) * 256. j * 256 <= slab_starts[j] < (j + 1) * 256.
All inputs are finite; a program needn't handle non-finite values.
Results may differ from a plain program's by a relative error of at most 0.004.
Values may be sent and summed in bfloat16 or wider, within the bound.
No kernel may reach another device: no remote copies, remote signals or barrier semaphores. Data moves between devices by JAX's collectives and lax.ppermute only.
A program may use at most 128 MiB of HBM per device.

v0:
```python
import jax
import jax.numpy as jnp
from jax import lax
from jax.sharding import PartitionSpec as P

Q_HEADS = 24
KV_HEADS = 8
HEAD_DIM = 128


def per_device(
    queries, out_grads, logsumexp, shared_keys, shared_values, query_starts, slab_starts
):
    score_scale = HEAD_DIM ** (-0.5)
    group_size = Q_HEADS // KV_HEADS
    kv_width = KV_HEADS * HEAD_DIM
    row_count = queries.shape[1]
    slab_rows = shared_keys.shape[0]
    all_keys, all_values, all_starts = (
        lax.all_gather(shared_keys, "seq", axis=0, tiled=True),
        lax.all_gather(shared_values, "seq", axis=0, tiled=True),
        lax.all_gather(slab_starts, "seq", axis=0, tiled=True),
    )
    total_keys = all_keys.shape[0]
    key_pos = (all_starts[:, None] + jnp.arange(slab_rows, dtype=jnp.int32)[None, :]).reshape(-1)
    query_pos = query_starts[0] + jnp.arange(row_count, dtype=jnp.int32)
    visible = key_pos[None, :] <= query_pos[:, None]
    key_total = jnp.zeros((total_keys, kv_width), jnp.float32)
    value_total = jnp.zeros((total_keys, kv_width), jnp.float32)
    layer_queries = queries[0]
    layer_outs = out_grads[0]
    layer_lse = logsumexp[0]

    def head_step(head_index, carried):
        query_acc, key_acc, value_acc = carried
        col_begin = head_index * group_size * HEAD_DIM
        query_group = lax.dynamic_slice_in_dim(
            layer_queries, col_begin, group_size * HEAD_DIM, 1
        ).reshape(row_count, group_size, HEAD_DIM)
        grad_group = lax.dynamic_slice_in_dim(
            layer_outs, col_begin, group_size * HEAD_DIM, 1
        ).reshape(row_count, group_size, HEAD_DIM)
        saved = lax.dynamic_slice_in_dim(layer_lse, head_index * group_size, group_size, 0)
        key_head = lax.dynamic_slice_in_dim(all_keys, head_index * HEAD_DIM, HEAD_DIM, 1)
        value_head = lax.dynamic_slice_in_dim(all_values, head_index * HEAD_DIM, HEAD_DIM, 1)
        scores = (
            jnp.einsum("rhd,kd->hrk", query_group, key_head, preferred_element_type=jnp.float32)
            * score_scale
        )
        probs = jnp.where(visible[None], jnp.exp(scores - saved[:, :, None]), 0.0)
        grad_probs = jnp.einsum(
            "rhd,kd->hrk", grad_group, value_head, preferred_element_type=jnp.float32
        )
        row_delta = jnp.sum(probs * grad_probs, axis=2, keepdims=True)
        grad_scores = probs * (grad_probs - row_delta)
        probs_half = probs.astype(jnp.bfloat16)
        scores_half = grad_scores.astype(jnp.bfloat16)
        value_piece = jnp.einsum(
            "hrk,rhd->kd", probs_half, grad_group, preferred_element_type=jnp.float32
        )
        key_piece = (
            jnp.einsum("hrk,rhd->kd", scores_half, query_group, preferred_element_type=jnp.float32)
            * score_scale
        )
        query_piece = (
            jnp.einsum("hrk,kd->rhd", scores_half, key_head, preferred_element_type=jnp.float32)
            * score_scale
        )
        query_acc = lax.dynamic_update_slice_in_dim(
            query_acc, query_piece.reshape(row_count, group_size * HEAD_DIM), col_begin, 1
        )
        key_old = lax.dynamic_slice_in_dim(key_acc, head_index * HEAD_DIM, HEAD_DIM, 1)
        key_acc = lax.dynamic_update_slice_in_dim(
            key_acc, key_old + key_piece, head_index * HEAD_DIM, 1
        )
        value_old = lax.dynamic_slice_in_dim(value_acc, head_index * HEAD_DIM, HEAD_DIM, 1)
        value_acc = lax.dynamic_update_slice_in_dim(
            value_acc, value_old + value_piece, head_index * HEAD_DIM, 1
        )
        return (query_acc, key_acc, value_acc)

    query_start = jnp.zeros((row_count, Q_HEADS * HEAD_DIM), jnp.float32)
    query_done, key_total, value_total = lax.fori_loop(
        0, KV_HEADS, head_step, (query_start, key_total, value_total)
    )
    layer_grads = [query_done]
    key_share, value_share = (
        lax.psum_scatter(key_total, "seq", scatter_dimension=0, tiled=True),
        lax.psum_scatter(value_total, "seq", scatter_dimension=0, tiled=True),
    )
    key_grads, value_grads = (
        lax.psum_scatter(key_share, "section", scatter_dimension=1, tiled=True),
        lax.psum_scatter(value_share, "section", scatter_dimension=1, tiled=True),
    )
    return (jnp.stack(layer_grads), key_grads, value_grads)


def solution(mesh):
    return jax.shard_map(
        per_device,
        mesh=mesh,
        in_specs=(
            P("section", "seq", None),
            P("section", "seq", None),
            P("section", None, "seq"),
            P("seq", None),
            P("seq", None),
            P("seq"),
            P("seq"),
        ),
        out_specs=(P("section", "seq", None), P("seq", "section"), P("seq", "section")),
        check_vma=False,
    )
```

profile of v0, /device:TPU:32, one launch (start us, length us, event | category | flops | bytes accessed | tf_op | source)
XLA Modules:
  0.0 1133.3 jit_solution(17633379529952931863)
XLA Ops:
  12.0 27.4 %all-reduce = s32[64]{0:T(128)S(1)} all-reduce(s32[64]{0:T(128)S(1)} %dynamic-update-slice), channel_id=1, replica_groups=mesh['section'=4,'seq'=64] {'seq'}, use_global_device_ids=true, to_apply=%add | all-reduce | flops 64 | bytes 512
  43.0 48.4 %all-gather.3.cloned.1.call-done = bf16[1024,1024]{1,0:T(8,128)(2,1)} async-done(((bf16[16,1024]{1,0:T(8,128)(2,1)}), bf16[1024,1024]{1,0:T(8,128)(2,1)}) %all-gather.3.cloned.1.call-update) | async-done | bytes 2097168 | tf_op jit(solution)/shard_map/all_gather | solution.py:20
  91.4 79.8 %all-gather.5.cloned.1.call-done = bf16[1024,1024]{1,0:T(8,128)(2,1)} async-done(((bf16[16,1024]{1,0:T(8,128)(2,1)}), bf16[1024,1024]{1,0:T(8,128)(2,1)}) %all-gather.5.cloned.1.call-update) | async-done | bytes 2097168 | tf_op jit(solution)/shard_map/all_gather | solution.py:21
  178.3 133.7 %while.20 = (s32[]{:T(128)}, f32[256,3072]{1,0:T(8,128)}, f32[1024,1024]{1,0:T(8,128)}, f32[1024,1024]{1,0:T(8,128)}, bf16[1024,1024]{1,0:T(8,128)(2,1)}, /*inde...) while((s32[]{:T(128)}, f32[256,3072]{1,0:T(8,128)}, ...), condition=%wide.region_2.3_spmd.clone, body=%wide.region_0.2_spmd.clone.sunk | while | flops 1014463744 | bytes 69882400 | solution.py:83
  189.0 2.6 fusion.64
  191.6 2.6 fusion.63
  205.7 2.6 fusion.64
  208.3 2.6 fusion.63
  222.4 2.6 fusion.64
  225.0 2.6 fusion.63
  239.1 2.6 fusion.64
  241.7 2.6 fusion.63
  255.8 2.6 fusion.64
  258.5 2.7 fusion.63
  272.6 2.6 fusion.64
  275.2 2.6 fusion.63
  289.4 2.6 fusion.64
  291.9 2.6 fusion.63
  306.0 2.6 fusion.64
  308.6 2.6 fusion.63
  312.6 387.9 %reduce-scatter.9.cloned.1.call-done = f32[16,1024]{1,0:T(8,128)} async-done(((f32[1024,1024]{1,0:T(8,128)}), f32[16,1024]{1,0:T(8,128)}) %reduce-scatter.9.cloned.1.call-update) | async-done | bytes 65552 | tf_op jit(solution)/shard_map/reduce_scatter | solution.py:89
  700.6 387.3 %reduce-scatter.5.cloned.1.call-done = f32[16,1024]{1,0:T(8,128)} async-done(((f32[1024,1024]{1,0:T(8,128)}), f32[16,1024]{1,0:T(8,128)}) %reduce-scatter.5.cloned.1.call-update) | async-done | bytes 65552 | tf_op jit(solution)/shard_map/reduce_scatter | solution.py:88
  1087.9 15.7 %reduce-scatter.11.cloned.1.call-done = f32[16,256]{1,0:T(8,128)} async-done(((f32[16,1024]{1,0:T(8,128)}), f32[16,256]{1,0:T(8,128)}) %reduce-scatter.11.cloned.1.call-update) | async-done | bytes 16400 | tf_op jit(solution)/shard_map/reduce_scatter | solution.py:93
  1103.7 22.8 %reduce-scatter.7.cloned.1.call-done = f32[16,256]{1,0:T(8,128)} async-done(((f32[16,1024]{1,0:T(8,128)}), f32[16,256]{1,0:T(8,128)}) %reduce-scatter.7.cloned.1.call-update) | async-done | bytes 16400 | tf_op jit(solution)/shard_map/reduce_scatter | solution.py:92
  (207 shorter events, 106.3 us)
Async XLA Ops:
  7.2 84.3 %all-gather.3.cloned.1.call-start = ((), (), s32[]{:S(2)}) async-start(), calls=%async_computation.4 | async-start | bytes 2129920 | tf_op jit(solution)/shard_map/all_gather | solution.py:20
  7.9 163.3 %all-gather.5.cloned.1.call-start = ((), (), s32[]{:S(2)}) async-start(), calls=%async_computation.5 | async-start | bytes 2129920 | tf_op jit(solution)/shard_map/all_gather | solution.py:21
  8.6 691.9 %reduce-scatter.9.cloned.1.call-start = ((), (), s32[]{:S(2)}) async-start(), calls=%async_computation.8 | async-start | bytes 4259840 | tf_op jit(solution)/shard_map/reduce_scatter | solution.py:89
  189.0 5.2 copy-start.2
  205.7 5.2 copy-start.2
  208.3 3.4 copy-start.4
  208.3 3.4 copy-start.6
  222.4 5.2 copy-start.2
  225.0 3.4 copy-start.4
  225.0 3.4 copy-start.6
  239.1 5.2 copy-start.2
  241.7 3.4 copy-start.4
  241.7 3.4 copy-start.6
  255.8 5.3 copy-start.2
  258.5 3.4 copy-start.4
  258.5 3.4 copy-start.6
  272.6 5.2 copy-start.2
  275.2 3.4 copy-start.4
  275.2 3.4 copy-start.6
  289.3 5.2 copy-start.2
  306.0 5.2 copy-start.2
  312.0 775.9 %reduce-scatter.5.cloned.1.call-start = ((), (), s32[]{:S(2)}) async-start(), calls=%async_computation.6 | async-start | bytes 4259840 | tf_op jit(solution)/shard_map/reduce_scatter | solution.py:88
  312.6 791.1 %reduce-scatter.11.cloned.1.call-start = ((), (), s32[]{:S(2)}) async-start(), calls=%async_computation.9 | async-start | bytes 81920 | tf_op jit(solution)/shard_map/reduce_scatter | solution.py:93
  700.6 425.9 %reduce-scatter.7.cloned.1.call-start = ((), (), s32[]{:S(2)}) async-start(), calls=%async_computation.7 | async-start | bytes 81920 | tf_op jit(solution)/shard_map/reduce_scatter | solution.py:92
  (38 other events, 72.5 us)
Sparse Core Ops, SparseCore 0:
  11.3 80.0 all-gather.2
  94.7 76.4 all-gather.4
  312.1 388.3 reduce-scatter.8
  703.1 384.7 reduce-scatter.4
  1090.8 12.7 reduce-scatter.10
  1106.7 19.6 reduce-scatter.6
where the time goes:
time: 1140 us; the launch traced here: 1130 us
  waiting for transfers between devices  944 us (83%)
  matrix products  86 us (8%)
  local copies, waits for them, and re-layouts  54.2 us (5%)
  blocking collectives  27.4 us (2%)
  between operations  15.4 us (1%)
    reduce_scatter x1, waiting for transfers between devices, per_device(): lax.psum_scatter(value_total, 'seq', scatter_dimension=0, tiled=True)  388 us
    reduce_scatter x1, waiting for transfers between devices, per_device(): lax.psum_scatter(key_total, 'seq', scatter_dimension=0, tiled=True)  387 us
    all_gather x1, waiting for transfers between devices, per_device(): lax.all_gather(shared_values, 'seq', axis=0, tiled=True)  79.8 us
    all_gather x1, waiting for transfers between devices, per_device(): lax.all_gather(shared_keys, 'seq', axis=0, tiled=True)  48.4 us
    unnamed x1, blocking collectives  27.4 us
  transfers between devices with their start and end apart: 6, of which 6 were waited for; matrix products, arithmetic and copies ran while one was open for 0% of the time, Pallas kernels for 0%

commit v1 on v0

v1 whole, which is shorter than its diff:
```python
import jax
import jax.numpy as jnp
from jax import lax
from jax.experimental import pallas as pl
from jax.experimental.pallas import tpu as pltpu
from jax.sharding import Mesh
from jax.sharding import PartitionSpec as P

KV_HEADS = 8
GROUP = 3
HEAD_DIM = 128
ROWS = 256
SLAB = 16
SCALE = HEAD_DIM**-0.5
LOG2E = 1.4426950408889634
WIDE = GROUP * ROWS
MINE = KV_HEADS // 2
COLS = MINE * HEAD_DIM
KEYS = 1024
BLOCK = 256
AXES = ("zl", "core", "zh", "x", "y")


def attention_kernel(
    meta, q_own, g_own, lse_own, q_oth, g_oth, lse_oth, kv0, kv1, kv2, kv3,
    dq_own, dq_oth, out0, out1, out2, out3,
    key_s, val_s, pos_s, rows_q, rows_g, prob_s, gp_s, half_s, ds_s, dk_s, dv_s,
):
    step = pl.program_id(0)
    core, a0, b0, z0, first = (meta[i] for i in range(5))
    a_step = jnp.where(core == 0, 1, 4)
    b_step = jnp.where(core == 0, 4, 1)

    @pl.when(step == 0)
    def _():
        row = lax.broadcasted_iota(jnp.int32, (SLAB, 128), 0).astype(jnp.float32)
        for a, piece in enumerate((kv0, kv1, kv2, kv3)):
            for b in range(4):
                for z in range(4):
                    slab = ((z0 - z) & 3) * 16 + ((a0 - a) & 3) * a_step + ((b0 - b) & 3) * b_step
                    src = pl.ds((b * 4 + z) * SLAB, SLAB)
                    dst = pl.ds(pl.multiple_of(slab * SLAB, SLAB), SLAB)
                    for h in range(MINE):
                        key_s[h, dst, :] = piece[src, h * 128:(h + 1) * 128]
                        val_s[h, dst, :] = piece[src, COLS + h * 128:COLS + (h + 1) * 128]
                    pos_s[dst, :] = (
                        piece[src, 2 * COLS:2 * COLS + 128].astype(jnp.float32)
                        + row + (slab * 256).astype(jnp.float32)
                    )

    lane = lax.broadcasted_iota(jnp.int32, (1, 128), 1)
    q_pos = [(first + lane + c * 128).astype(jnp.float32) for c in range(2)]

    for layer, (q_ref, g_ref, l_ref, dq_ref) in enumerate(
        ((q_own, g_own, lse_own, dq_own), (q_oth, g_oth, lse_oth, dq_oth))
    ):
        for h in range(GROUP):
            rows_q[layer, h * ROWS:(h + 1) * ROWS, :] = q_ref[:, h * 128:(h + 1) * 128]
            rows_g[layer, h * ROWS:(h + 1) * ROWS, :] = g_ref[:, h * 128:(h + 1) * 128]
        queries = rows_q[layer]
        grads = rows_g[layer]
        lse = l_ref[0] * LOG2E
        delta = jnp.zeros((1, WIDE), jnp.float32)
        for kb in range(KEYS // BLOCK):
            sl = slice(kb * BLOCK, (kb + 1) * BLOCK)
            score = lax.dot_general(
                key_s[step, sl, :], queries, (((1,), (1,)), ((), ())),
                preferred_element_type=jnp.float32,
            )
            prob = jnp.exp2(score * (SCALE * LOG2E) - lse)
            k_pos = pos_s[sl, :]
            seen = jnp.concatenate([k_pos <= q_pos[0], k_pos <= q_pos[1]] * GROUP, axis=1)
            prob = jnp.where(seen, prob, 0.0)
            grad_prob = lax.dot_general(
                val_s[step, sl, :], grads, (((1,), (1,)), ((), ())),
                preferred_element_type=jnp.float32,
            )
            delta = delta + jnp.sum(prob * grad_prob, axis=0, keepdims=True)
            prob_s[layer, sl, :] = prob
            gp_s[layer, sl, :] = grad_prob
            half_s[layer, sl, :] = prob.astype(jnp.bfloat16)
        for kb in range(KEYS // BLOCK):
            sl = slice(kb * BLOCK, (kb + 1) * BLOCK)
            ds_s[layer, sl, :] = (prob_s[layer, sl, :] * (gp_s[layer, sl, :] - delta)).astype(jnp.bfloat16)
        dv = jnp.dot(half_s[layer], grads, preferred_element_type=jnp.float32)
        dk = jnp.dot(ds_s[layer], queries, preferred_element_type=jnp.float32)
        if layer == 0:
            dv_s[...] = dv
            dk_s[...] = dk
        else:
            dv_s[...] += dv
            dk_s[...] = (dk_s[...] + dk) * SCALE
        dq_t = lax.dot_general(
            key_s[step], ds_s[layer], (((0,), (0,)), ((), ())),
            preferred_element_type=jnp.float32,
        ) * SCALE
        for h in range(GROUP):
            dq_ref[:, h * 128:(h + 1) * 128] = dq_t[:, h * ROWS:(h + 1) * ROWS].T

    for a, out in enumerate((out0, out1, out2, out3)):
        for b in range(4):
            for z in range(4):
                slab = z * 16 + ((a0 + a) & 3) * a_step + ((b0 + b) & 3) * b_step
                src = pl.ds(pl.multiple_of(slab * SLAB, SLAB), SLAB)
                dst = pl.ds((b * 4 + z) * SLAB, SLAB)
                out[0, dst, :] = dk_s[src, :].astype(out.dtype)
                out[1, dst, :] = dv_s[src, :].astype(out.dtype)


def attention(meta, q_own, g_own, lse_own, q_oth, g_oth, lse_oth, kv):
    def head(g, m):
        return (g // 2) * 4 + m[0] * 2 + g % 2

    f32, bf16 = jnp.float32, jnp.bfloat16
    width = GROUP * HEAD_DIM
    own = pl.BlockSpec((ROWS, width), lambda g, m: (0, head(g, m)))
    oth = pl.BlockSpec((ROWS, width), lambda g, m: (0, g))
    part = pl.BlockSpec((BLOCK, kv[0].shape[1]), lambda g, m: (0, 0))
    out = pl.BlockSpec((2, BLOCK, HEAD_DIM), lambda g, m: (0, 0, g))
    return pl.pallas_call(
        attention_kernel,
        grid_spec=pltpu.PrefetchScalarGridSpec(
            num_scalar_prefetch=1,
            grid=(MINE,),
            in_specs=[
                own, own, pl.BlockSpec((1, 1, WIDE), lambda g, m: (head(g, m), 0, 0)),
                oth, oth, pl.BlockSpec((1, 1, WIDE), lambda g, m: (g, 0, 0)),
                part, part, part, part,
            ],
            out_specs=[own, oth, out, out, out, out],
            scratch_shapes=[
                pltpu.VMEM((MINE, KEYS, HEAD_DIM), bf16),
                pltpu.VMEM((MINE, KEYS, HEAD_DIM), bf16),
                pltpu.VMEM((KEYS, 128), f32),
                pltpu.VMEM((2, WIDE, HEAD_DIM), bf16),
                pltpu.VMEM((2, WIDE, HEAD_DIM), bf16),
                pltpu.VMEM((2, KEYS, WIDE), f32),
                pltpu.VMEM((2, KEYS, WIDE), f32),
                pltpu.VMEM((2, KEYS, WIDE), bf16),
                pltpu.VMEM((2, KEYS, WIDE), bf16),
                pltpu.VMEM((KEYS, HEAD_DIM), f32),
                pltpu.VMEM((KEYS, HEAD_DIM), f32),
            ],
        ),
        out_shape=[
            jax.ShapeDtypeStruct((ROWS, KV_HEADS * width), f32),
            jax.ShapeDtypeStruct((ROWS, MINE * width), f32),
            jax.ShapeDtypeStruct((2, BLOCK, COLS), f32),
        ] + [jax.ShapeDtypeStruct((2, BLOCK, COLS), bf16)] * 3,
        compiler_params=pltpu.CompilerParams(vmem_limit_bytes=50 * 2**20),
        cost_estimate=pl.CostEstimate(
            flops=8 * 10**9, bytes_accessed=16 * 2**20, transcendentals=6 * 10**6
        ),
        name="attention_backward",
    )(meta, q_own, g_own, lse_own, q_oth, g_oth, lse_oth, *kv)


def shift(value, axis, by):
    return lax.ppermute(value, axis, [(i, (i + by) % 4) for i in range(4)])


def plane_shift(value, by, x_core):
    pairs = []
    for core in range(2):
        for x in range(4):
            for y in range(4):
                to = ((x + by) % 4, y) if core == x_core else (x, (y + by) % 4)
                pairs.append((core * 16 + x * 4 + y, core * 16 + to[0] * 4 + to[1]))
    return lax.ppermute(value, ("core", "x", "y"), pairs)


def swap(value):
    return lax.ppermute(value, "core", [(0, 1), (1, 0)])


def per_device(
    queries, out_grads, logsumexp, shared_keys, shared_values, query_starts, slab_starts
):
    core, zh, x, y = (lax.axis_index(n) for n in ("core", "zh", "x", "y"))
    other = 1 - core
    seq = zh * 16 + x * 4 + y
    queries, out_grads = queries[0], out_grads[0]

    def halves(value, which, width, axis=1):
        return jnp.concatenate(
            [
                lax.dynamic_slice_in_dim(value, which * width, width, axis),
                lax.dynamic_slice_in_dim(value, (2 + which) * width, width, axis),
            ],
            axis,
        )

    with jax.named_scope("gather_keys"):
        offset = (slab_starts[0] - seq * 256).astype(jnp.bfloat16)
        payload = jnp.concatenate(
            [
                halves(shared_keys, core, 256),
                halves(shared_values, core, 256),
                jnp.broadcast_to(offset, (SLAB, 128)),
            ],
            1,
        )
        block = jnp.concatenate([payload] + [shift(payload, "zh", r) for r in (1, 2, 3)], 0)
    with jax.named_scope("swap_queries"):
        lse = logsumexp[0].reshape(KV_HEADS, WIDE)
        q_oth = swap(halves(queries, other, 768))
        g_oth = swap(halves(out_grads, other, 768))
        lse_oth = swap(halves(lse, other, 2, 0))
    with jax.named_scope("gather_keys"):
        block = jnp.concatenate([block] + [plane_shift(block, r, 0) for r in (1, 2, 3)], 0)
        pieces = [block] + [plane_shift(block, r, 1) for r in (1, 2, 3)]

    a0 = jnp.where(core == 0, y, x)
    b0 = jnp.where(core == 0, x, y)
    meta = jnp.stack([core, a0, b0, zh, query_starts[0]]).astype(jnp.int32)
    dq, dq_oth, part0, *parts = attention(
        meta, queries, out_grads, lse[:, None], q_oth, g_oth, lse_oth[:, None], pieces
    )

    with jax.named_scope("scatter_grads"):
        total = part0
        for r, part in enumerate(parts):
            total = total + plane_shift(part, r + 1, 1).astype(jnp.float32)
    with jax.named_scope("swap_query_grads"):
        back = swap(dq_oth)
        dq = lax.dynamic_update_slice(dq, back[:, :768], (0, other * 768))
        dq = lax.dynamic_update_slice(dq, back[:, 768:], (0, (2 + other) * 768))
    with jax.named_scope("scatter_grads"):
        small = total[:, :64]
        for r in (1, 2, 3):
            piece = total[:, r * 64:(r + 1) * 64].astype(jnp.bfloat16)
            small = small + plane_shift(piece, r, 0).astype(jnp.float32)
        small = small.reshape(2, 4, SLAB, 2, 256).transpose(3, 1, 0, 2, 4).reshape(8, 2, SLAB, 256)
        got = lax.all_to_all(small, ("zl", "zh"), 0, 0)
        grads = jnp.sum(got, 0)
    return dq[None], grads[0], grads[1]


def solution(mesh):
    fine = Mesh(mesh.devices.reshape(2, 2, 4, 4, 4), AXES)
    section, seq = ("zl", "core"), ("zh", "x", "y")
    return jax.shard_map(
        per_device,
        mesh=fine,
        in_specs=(
            P(section, seq, None),
            P(section, seq, None),
            P(section, None, seq),
            P(seq, None),
            P(seq, None),
            P(seq),
            P(seq),
        ),
        out_specs=(P(section, seq, None), P(seq, section), P(seq, section)),
        check_vma=False,
    )
```

time: 1140 us -> 126 us (0.11)
  waiting for transfers between devices: 944 us -> 48.4 us
  matrix products: 86 us -> 0 us
  local copies, waits for them, and re-layouts: 54.2 us -> 8.7 us
  Pallas kernels: 0 us -> 23.8 us
  starting transfers between devices: 0.23 us -> 24 us
  between operations: 15.4 us -> 2.1 us
  blocking collectives: 27.4 us -> 15.4 us
    reduce_scatter x4 -> x0, waiting for transfers between devices: 814 us -> none  [the longest x1 388 us: per_device(): lax.psum_scatter(value_total, 'seq', scatter_dimension=0, tiled=True)]
    all_gather x2 -> x0, waiting for transfers between devices: 128 us -> none  [the longest x1 79.8 us: per_device(): lax.all_gather(shared_values, 'seq', axis=0, tiled=True)]
    dot_general x40 -> x0, matrix products: 86 us -> none  [the longest x8 20.8 us: head_step(): jnp.einsum('hrk,rhd->kd', scores_half, query_group, preferred_element_typ...]
    ppermute x0 -> x19, waiting for transfers between devices: none -> 48.4 us  [the longest x12 48.4 us: plane_shift(): return lax.ppermute(value, ('core', 'x', 'y'), pairs)]
    unnamed x1 -> x0, blocking collectives: 27.4 us -> none
    ppermute x0 -> x19, starting transfers between devices: none -> 24 us  [the longest x12 14.1 us: plane_shift(): return lax.ppermute(value, ('core', 'x', 'y'), pairs)]
    pallas_call x0 -> x1, Pallas kernels: none -> 23.8 us  [attention(): pl.pallas_call(attention_kernel, grid_spec=pltpu.PrefetchScalarGridSpec(n...]
    dynamic_update_slice x16 -> x2, local copies, waits for them, and re-layouts: 21.4 us -> 1.86 us  [the longest x1 0.93 us: per_device(): dq = lax.dynamic_update_slice(dq, back[:, :768], (0, other * 768))]
  transfers between devices with their start and end apart: 6 -> 19, of which waited for: 6 -> 9; matrix products, arithmetic and copies ran while one was open for 0% -> 5% of each run, Pallas kernels for 0% -> 0%
where the time goes in v1:
time: 126 us; the launch traced here: 125 us
  waiting for transfers between devices  48.4 us (38%)
  starting transfers between devices  24 us (19%)
  Pallas kernels  23.8 us (19%)
  blocking collectives  15.4 us (12%)
  local copies, waits for them, and re-layouts  8.7 us (7%)
  other arithmetic  2.64 us (2%)
  between operations  2.1 us (2%)
    ppermute x12, waiting for transfers between devices, plane_shift(): return lax.ppermute(value, ('core', 'x', 'y'), pairs)  48.4 us
    pallas_call x1, Pallas kernels, attention(): pl.pallas_call(attention_kernel, grid_spec=pltpu.PrefetchScalarGridSpec(n...  23.8 us
    all_to_all x1, blocking collectives, per_device(): got = lax.all_to_all(small, ('zl', 'zh'), 0, 0)  15.4 us
    ppermute x12, starting transfers between devices, plane_shift(): return lax.ppermute(value, ('core', 'x', 'y'), pairs)  14.1 us
    ppermute x3, starting transfers between devices, shift(): return lax.ppermute(value, axis, [(i, (i + by) % 4) for i in range(4)])  9.21 us
    unnamed x13, local copies, waits for them, and re-layouts  3.63 us
  transfers between devices with their start and end apart: 19, of which 9 were waited for; matrix products, arithmetic and copies ran while one was open for 5% of the time, Pallas kernels for 0%

profile of v1, /device:TPU:32, one launch (start us, length us, event | category | flops | bytes accessed | tf_op | source)
XLA Modules:
  0.0 125.0 jit_solution(18028410176999663749)
XLA Ops:
  4.2 5.4 %collective-permute-start.5 = (bf16[16,1152]{1,0:T(8,128)(2,1)S(1)}, bf16[16,1152]{1,0:T(8,128)(2,1)S(1)}, u32[]{:S(2)}, u32[]{:S(2)}) collective-permute-start(bf16[16,1152]{1,0:T(8,128)(2,1)S(1)} %constant_dynamic-update-slice_fusion), channel_id=1, source_target_pairs={{0,48},{16,0},{32,16},{48,32},{1,49},{17,1},{33,17},{49,33},{2,50}... | collective-permute-start | bytes 110600 | tf_op jit(solution)/shard_map/gather_keys/ppermute | solution.py:159
  9.6 1.4 %collective-permute-start.4 = (bf16[16,1152]{1,0:T(8,128)(2,1)S(1)}, bf16[16,1152]{1,0:T(8,128)(2,1)S(1)}, u32[]{:S(2)}, u32[]{:S(2)}) collective-permute-start(bf16[16,1152]{1,0:T(8,128)(2,1)S(1)} %constant_dynamic-update-slice_fusion), channel_id=1, source_target_pairs={{0,32},{16,48},{32,0},{48,16},{1,33},{17,49},{33,1},{49,17},{2,34}... | collective-permute-start | bytes 110600 | tf_op jit(solution)/shard_map/gather_keys/ppermute | solution.py:159
  11.0 2.4 %collective-permute-start.3 = (bf16[16,1152]{1,0:T(8,128)(2,1)S(1)}, bf16[16,1152]{1,0:T(8,128)(2,1)S(1)}, u32[]{:S(2)}, u32[]{:S(2)}) collective-permute-start(bf16[16,1152]{1,0:T(8,128)(2,1)S(1)} %constant_dynamic-update-slice_fusion), channel_id=1, source_target_pairs={{0,16},{16,32},{32,48},{48,0},{1,17},{17,33},{33,49},{49,1},{2,18}... | collective-permute-start | bytes 110600 | tf_op jit(solution)/shard_map/gather_keys/ppermute | solution.py:159
  14.3 1.5 %dynamic-slice_bitcast_fusion.1 = (bf16[256,768]{1,0:T(8,128)(2,1)S(1)}, bf16[256,768]{1,0:T(8,128)(2,1)S(1)}, bf16[256,768]{1,0:T(8,128)(2,1)S(1)}, bf16[256,768]{1,0:T(8,128)(2,1)S(1)}) fusion(bf16[1,256,3072]{2,1,0:T(8,128)(2,1)} %param.8, s32[]{:T(128)S(6)} %select_n.33, s32[]{:T(128)S(6)} %select_n.34, bf16[1,256,3072]{2,1,0:T(8,128)(2,1)} %param.7), kind=kLoop, calls=%fused_computation.8 | loop fusion | bytes 3145736 | tf_op jit(solution)/shard_map/swap_queries/dynamic_slice | solution.py:187
  17.1 0.9 pad_maximum_fusion.1
  18.1 2.8 %collective-permute-start.8 = (bf16[64,1152]{1,0:T(8,128)(2,1)S(1)}, bf16[64,1152]{1,0:T(8,128)(2,1)S(1)}, u32[]{:S(2)}, u32[]{:S(2)}) collective-permute-start(bf16[64,1152]{1,0:T(8,128)(2,1)S(1)} %pad_maximum_fusion.2), channel_id=1, source_target_pairs={{0,12},{1,13},{2,14},{3,15},{4,0},{5,1},{6,2},{7,3},{8,4},{9,5},{1... | collective-permute-start | bytes 442376 | tf_op jit(solution)/shard_map/gather_keys/ppermute | solution.py:169
  20.9 6.3 %collective-permute-done.6 = bf16[64,1152]{1,0:T(8,128)(2,1)S(1)} collective-permute-done((bf16[64,1152]{1,0:T(8,128)(2,1)S(1)}, bf16[64,1152]{1,0:T(8,128)(2,1)S(1)}, u32[]{:S(2)}, u32[]{:S(2)}) %collective-permute-start.6) | collective-permute-done | bytes 147488 | tf_op jit(solution)/shard_map/gather_keys/ppermute | solution.py:169
  27.3 6.6 %collective-permute-done.7 = bf16[64,1152]{1,0:T(8,128)(2,1)S(1)} collective-permute-done((bf16[64,1152]{1,0:T(8,128)(2,1)S(1)}, bf16[64,1152]{1,0:T(8,128)(2,1)S(1)}, u32[]{:S(2)}, u32[]{:S(2)}) %collective-permute-start.7) | collective-permute-done | bytes 147488 | tf_op jit(solution)/shard_map/gather_keys/ppermute | solution.py:169
  34.0 3.1 %collective-permute-start.11 = (bf16[256,1152]{1,0:T(8,128)(2,1)S(1)}, bf16[256,1152]{1,0:T(8,128)(2,1)S(1)}, u32[]{:S(2)}, u32[]{:S(2)}) collective-permute-start(bf16[256,1152]{1,0:T(8,128)(2,1)S(1)} %constant_dynamic-update-slice_fusion.5.kv0), channel_id=1, source_target_pairs={{0,3},{1,0},{2,1},{3,2},{4,7},{5,4},{6,5},{7,6},{8,11},{9,8},{10,9... | collective-permute-start | bytes 1769480 | tf_op jit(solution)/shard_map/gather_keys/ppermute | solution.py:169
  37.7 1.0 collective-permute-start.9
  39.4 11.3 %collective-permute-done.11.kv3 = bf16[256,1152]{1,0:T(8,128)(2,1)S(1)} collective-permute-done((bf16[256,1152]{1,0:T(8,128)(2,1)S(1)}, bf16[256,1152]{1,0:T(8,128)(2,1)S(1)}, u32[]{:S(2)}, u32[]{:S(2)}) %collective-permute-start.11) | collective-permute-done | bytes 589856 | tf_op jit(solution)/shard_map/gather_keys/ppermute | solution.py:169
  50.8 4.0 %collective-permute-done.9.kv1 = bf16[256,1152]{1,0:T(8,128)(2,1)S(1)} collective-permute-done((bf16[256,1152]{1,0:T(8,128)(2,1)S(1)}, bf16[256,1152]{1,0:T(8,128)(2,1)S(1)}, u32[]{:S(2)}, u32[]{:S(2)}) %collective-permute-start.9) | collective-permute-done | bytes 589856 | tf_op jit(solution)/shard_map/gather_keys/ppermute | solution.py:169
  54.8 23.8 %attention_backward.1 = (f32[256,3072]{1,0:T(8,128)}, f32[256,1536]{1,0:T(8,128)}, f32[2,256,512]{2,1,0:T(8,128)}, bf16[2,256,512]{2,1,0:T(8,128)(2,1)S(1)}, bf1...) custom-call(s32[5]{0:T(128)S(1)} %stack.19.meta, bf16[256,3072]{1,0:T(8,128)(2,1)} %bitcast.33, ...), custom_call_target="tpu_custom_call" | custom-call | flops 8000000000 | bytes 16777216 | tf_op jit(solution)/shard_map/attention_backward/pallas_call | solution.py:120
  78.5 2.1 %collective-permute-start.14 = (bf16[2,256,512]{2,1,0:T(8,128)(2,1)S(1)}, bf16[2,256,512]{2,1,0:T(8,128)(2,1)S(1)}, u32[]{:S(2)}, u32[]{:S(2)}) collective-permute-start(bf16[2,256,512]{2,1,0:T(8,128)(2,1)S(1)} %get-tuple-element.13), channel_id=1, source_target_pairs={{0,2},{1,3},{2,0},{3,1},{4,6},{5,7},{6,4},{7,5},{8,10},{9,11},{10,... | collective-permute-start | bytes 1572872 | tf_op jit(solution)/shard_map/scatter_grads/ppermute | solution.py:169
  80.6 1.2 collective-permute-start.15
  81.8 12.7 %collective-permute-done.13 = bf16[2,256,512]{2,1,0:T(8,128)(2,1)S(1)} collective-permute-done((bf16[2,256,512]{2,1,0:T(8,128)(2,1)S(1)}, bf16[2,256,512]{2,1,0:T(8,128)(2,1)S(1)}, u32[]{:S(2)}, u32[]{:S(2)}) %collective-permute-start.13) | collective-permute-done | bytes 524320 | tf_op jit(solution)/shard_map/scatter_grads/ppermute | solution.py:169
  95.5 1.5 %fusion.4 = (bf16[2,256,512]{2,1,0:T(8,128)(2,1)S(1)}, f32[2,256,512]{2,1,0:T(8,128)S(1)}) fusion(bf16[2,256,512]{2,1,0:T(8,128)(2,1)S(1)} %collective-permute-done.15, bf16[2,256,512]{2,1,0:T(8,128)(2,1)S(1)} %collective-permute-done.14, f32[2,256,512]{2,1,0:T(8,128)} %get-tuple-element.11, bf16[2,256,512]{2,1,0:T(8,128)(2,1)S(1)} %collective-permute-done.13), kind=kLoop, calls=%fused_computation.36 | loop fusion | flops 1835008 | bytes 4194304 | tf_op jit(solution)/shard_map/convert.2
  97.1 3.2 %collective-permute-start.18 = (bf16[2,64,512]{2,1,0:T(8,128)(2,1)S(1)}, bf16[2,64,512]{2,1,0:T(8,128)(2,1)S(1)}, u32[]{:S(2)}, u32[]{:S(2)}) collective-permute-start(bf16[2,64,512]{2,1,0:T(8,128)(2,1)S(1)} %get-tuple-element.22), channel_id=1, source_target_pairs={{0,12},{1,13},{2,14},{3,15},{4,0},{5,1},{6,2},{7,3},{8,4},{9,5},{1... | collective-permute-start | bytes 393224 | tf_op jit(solution)/shard_map/scatter_grads/ppermute | solution.py:169
  100.4 2.9 %collective-permute-done.16 = bf16[2,64,512]{2,1,0:T(8,128)(2,1)S(1)} collective-permute-done((bf16[2,64,512]{2,1,0:T(8,128)(2,1)S(1)}, bf16[2,64,512]{2,1,0:T(8,128)(2,1)S(1)}, u32[]{:S(2)}, u32[]{:S(2)}) %collective-permute-start.16) | collective-permute-done | bytes 131104 | tf_op jit(solution)/shard_map/scatter_grads/ppermute | solution.py:169
  103.3 1.0 collective-permute-done.18
  104.3 2.5 %collective-permute-done.17 = bf16[2,64,512]{2,1,0:T(8,128)(2,1)S(1)} collective-permute-done((bf16[2,64,512]{2,1,0:T(8,128)(2,1)S(1)}, bf16[2,64,512]{2,1,0:T(8,128)(2,1)S(1)}, u32[]{:S(2)}, u32[]{:S(2)}) %collective-permute-start.17) | collective-permute-done | bytes 131104 | tf_op jit(solution)/shard_map/scatter_grads/ppermute | solution.py:169
  107.1 15.4 %all_to_all.5 = f32[8,2,16,256]{3,2,1,0:T(8,128)S(1)} all-to-all(f32[8,2,16,256]{3,2,1,0:T(8,128)S(1)} %bitcast.32), channel_id=1, replica_groups=mesh['zl'=2,'core'=2,'zh'=4,'x'=4,'y'=4] {'zl','zh'}, dimensions={0} | all-to-all | bytes 524288 | tf_op jit(solution)/shard_map/scatter_grads/all_to_all | solution.py:234
  123.1 0.9 fusion.1
  124.1 0.9 fusion
  (50 shorter events, 7.9 us)
Async XLA Ops:
  4.2 13.9 %collective-permute-start.5 = (bf16[16,1152]{1,0:T(8,128)(2,1)S(1)}, bf16[16,1152]{1,0:T(8,128)(2,1)S(1)}, u32[]{:S(2)}, u32[]{:S(2)}) collective-permute-start(bf16[16,1152]{1,0:T(8,128)(2,1)S(1)} %constant_dynamic-update-slice_fusion), channel_id=1, source_target_pairs={{0,48},{16,0},{32,16},{48,32},{1,49},{17,1},{33,17},{49,33},{2,50}... | collective-permute-start | bytes 110600 | tf_op jit(solution)/shard_map/gather_keys/ppermute | solution.py:159
  9.6 8.5 %collective-permute-start.4 = (bf16[16,1152]{1,0:T(8,128)(2,1)S(1)}, bf16[16,1152]{1,0:T(8,128)(2,1)S(1)}, u32[]{:S(2)}, u32[]{:S(2)}) collective-permute-start(bf16[16,1152]{1,0:T(8,128)(2,1)S(1)} %constant_dynamic-update-slice_fusion), channel_id=1, source_target_pairs={{0,32},{16,48},{32,0},{48,16},{1,33},{17,49},{33,1},{49,17},{2,34}... | collective-permute-start | bytes 110600 | tf_op jit(solution)/shard_map/gather_keys/ppermute | solution.py:159
  11.0 7.0 %collective-permute-start.3 = (bf16[16,1152]{1,0:T(8,128)(2,1)S(1)}, bf16[16,1152]{1,0:T(8,128)(2,1)S(1)}, u32[]{:S(2)}, u32[]{:S(2)}) collective-permute-start(bf16[16,1152]{1,0:T(8,128)(2,1)S(1)} %constant_dynamic-update-slice_fusion), channel_id=1, source_target_pairs={{0,16},{16,32},{32,48},{48,0},{1,17},{17,33},{33,49},{49,1},{2,18}... | collective-permute-start | bytes 110600 | tf_op jit(solution)/shard_map/gather_keys/ppermute | solution.py:159
  14.2 23.5 %collective-permute-start.2 = (f32[4,768]{1,0:T(4,128)S(1)}, f32[4,768]{1,0:T(4,128)S(1)}, u32[]{:S(2)}, u32[]{:S(2)}) collective-permute-start(f32[4,768]{1,0:T(4,128)S(1)} %pad_maximum_fusion.3), channel_id=1, source_target_pairs={{0,64},{64,0},{1,65},{65,1},{2,66},{66,2},{3,67},{67,3},{4,68},{68... | collective-permute-start | bytes 36872 | tf_op jit(solution)/shard_map/swap_queries/ppermute | solution.py:173
  15.8 22.9 %copy-start = (f32[1,24,256]{2,1,0:T(8,128)S(1)}, f32[1,24,256]{2,1,0:T(8,128)}, u32[]{:S(2)}) copy-start(f32[1,24,256]{2,1,0:T(8,128)} %param.9) | copy-start | bytes 73732
  15.8 39.0 %collective-permute-start = (bf16[256,1536]{1,0:T(8,128)(2,1)S(1)}, bf16[256,1536]{1,0:T(8,128)(2,1)}, u32[]{:S(2)}, u32[]{:S(2)}) collective-permute-start(bf16[256,1536]{1,0:T(8,128)(2,1)S(1)} %pad_maximum_fusion), channel_id=1, source_target_pairs={{0,64},{64,0},{1,65},{65,1},{2,66},{66,2},{3,67},{67,3},{4,68},{68... | collective-permute-start | bytes 2359304 | tf_op jit(solution)/shard_map/swap_queries/ppermute | solution.py:173
  18.0 36.8 %collective-permute-start.1 = (bf16[256,1536]{1,0:T(8,128)(2,1)}, bf16[256,1536]{1,0:T(8,128)(2,1)}, u32[]{:S(2)}, u32[]{:S(2)}) collective-permute-start(bf16[256,1536]{1,0:T(8,128)(2,1)} %pad_maximum_fusion.1), channel_id=1, source_target_pairs={{0,64},{64,0},{1,65},{65,1},{2,66},{66,2},{3,67},{67,3},{4,68},{68... | collective-permute-start | bytes 2359304 | tf_op jit(solution)/shard_map/swap_queries/ppermute | solution.py:173
  18.1 15.9 %collective-permute-start.8 = (bf16[64,1152]{1,0:T(8,128)(2,1)S(1)}, bf16[64,1152]{1,0:T(8,128)(2,1)S(1)}, u32[]{:S(2)}, u32[]{:S(2)}) collective-permute-start(bf16[64,1152]{1,0:T(8,128)(2,1)S(1)} %pad_maximum_fusion.2), channel_id=1, source_target_pairs={{0,12},{1,13},{2,14},{3,15},{4,0},{5,1},{6,2},{7,3},{8,4},{9,5},{1... | collective-permute-start | bytes 442376 | tf_op jit(solution)/shard_map/gather_keys/ppermute | solution.py:169
  20.9 6.4 %collective-permute-start.6 = (bf16[64,1152]{1,0:T(8,128)(2,1)S(1)}, bf16[64,1152]{1,0:T(8,128)(2,1)S(1)}, u32[]{:S(2)}, u32[]{:S(2)}) collective-permute-start(bf16[64,1152]{1,0:T(8,128)(2,1)S(1)} %pad_maximum_fusion.2), channel_id=1, source_target_pairs={{0,4},{1,5},{2,6},{3,7},{4,8},{5,9},{6,10},{7,11},{8,12},{9,13},{1... | collective-permute-start | bytes 442376 | tf_op jit(solution)/shard_map/gather_keys/ppermute | solution.py:169
  27.3 6.6 %collective-permute-start.7 = (bf16[64,1152]{1,0:T(8,128)(2,1)S(1)}, bf16[64,1152]{1,0:T(8,128)(2,1)S(1)}, u32[]{:S(2)}, u32[]{:S(2)}) collective-permute-start(bf16[64,1152]{1,0:T(8,128)(2,1)S(1)} %pad_maximum_fusion.2), channel_id=1, source_target_pairs={{0,8},{1,9},{2,10},{3,11},{4,12},{5,13},{6,14},{7,15},{8,0},{9,1},... | collective-permute-start | bytes 442376 | tf_op jit(solution)/shard_map/gather_keys/ppermute | solution.py:169
  34.0 16.8 %collective-permute-start.11 = (bf16[256,1152]{1,0:T(8,128)(2,1)S(1)}, bf16[256,1152]{1,0:T(8,128)(2,1)S(1)}, u32[]{:S(2)}, u32[]{:S(2)}) collective-permute-start(bf16[256,1152]{1,0:T(8,128)(2,1)S(1)} %constant_dynamic-update-slice_fusion.5.kv0), channel_id=1, source_target_pairs={{0,3},{1,0},{2,1},{3,2},{4,7},{5,4},{6,5},{7,6},{8,11},{9,8},{10,9... | collective-permute-start | bytes 1769480 | tf_op jit(solution)/shard_map/gather_keys/ppermute | solution.py:169
  37.1 13.7 %collective-permute-start.10 = (bf16[256,1152]{1,0:T(8,128)(2,1)S(1)}, bf16[256,1152]{1,0:T(8,128)(2,1)S(1)}, u32[]{:S(2)}, u32[]{:S(2)}) collective-permute-start(bf16[256,1152]{1,0:T(8,128)(2,1)S(1)} %constant_dynamic-update-slice_fusion.5.kv0), channel_id=1, source_target_pairs={{0,2},{1,3},{2,0},{3,1},{4,6},{5,7},{6,4},{7,5},{8,10},{9,11},{10,... | collective-permute-start | bytes 1769480 | tf_op jit(solution)/shard_map/gather_keys/ppermute | solution.py:169
  37.7 17.1 %collective-permute-start.9 = (bf16[256,1152]{1,0:T(8,128)(2,1)S(1)}, bf16[256,1152]{1,0:T(8,128)(2,1)S(1)}, u32[]{:S(2)}, u32[]{:S(2)}) collective-permute-start(bf16[256,1152]{1,0:T(8,128)(2,1)S(1)} %constant_dynamic-update-slice_fusion.5.kv0), channel_id=1, source_target_pairs={{0,1},{1,2},{2,3},{3,0},{4,5},{5,6},{6,7},{7,4},{8,9},{9,10},{10,1... | collective-permute-start | bytes 1769480 | tf_op jit(solution)/shard_map/gather_keys/ppermute | solution.py:169
  78.5 16.0 %collective-permute-start.13 = (bf16[2,256,512]{2,1,0:T(8,128)(2,1)S(1)}, bf16[2,256,512]{2,1,0:T(8,128)(2,1)S(1)}, u32[]{:S(2)}, u32[]{:S(2)}) collective-permute-start(bf16[2,256,512]{2,1,0:T(8,128)(2,1)S(1)} %get-tuple-element.12), channel_id=1, source_target_pairs={{0,1},{1,2},{2,3},{3,0},{4,5},{5,6},{6,7},{7,4},{8,9},{9,10},{10,1... | collective-permute-start | bytes 1572872 | tf_op jit(solution)/shard_map/scatter_grads/ppermute | solution.py:169
  78.5 16.0 %collective-permute-start.14 = (bf16[2,256,512]{2,1,0:T(8,128)(2,1)S(1)}, bf16[2,256,512]{2,1,0:T(8,128)(2,1)S(1)}, u32[]{:S(2)}, u32[]{:S(2)}) collective-permute-start(bf16[2,256,512]{2,1,0:T(8,128)(2,1)S(1)} %get-tuple-element.13), channel_id=1, source_target_pairs={{0,2},{1,3},{2,0},{3,1},{4,6},{5,7},{6,4},{7,5},{8,10},{9,11},{10,... | collective-permute-start | bytes 1572872 | tf_op jit(solution)/shard_map/scatter_grads/ppermute | solution.py:169
  80.6 14.8 %collective-permute-start.15 = (bf16[2,256,512]{2,1,0:T(8,128)(2,1)S(1)}, bf16[2,256,512]{2,1,0:T(8,128)(2,1)S(1)}, u32[]{:S(2)}, u32[]{:S(2)}) collective-permute-start(bf16[2,256,512]{2,1,0:T(8,128)(2,1)S(1)} %get-tuple-element.14), channel_id=1, source_target_pairs={{0,3},{1,0},{2,1},{3,2},{4,7},{5,4},{6,5},{7,6},{8,11},{9,8},{10,9... | collective-permute-start | bytes 1572872 | tf_op jit(solution)/shard_map/scatter_grads/ppermute | solution.py:169
  81.8 41.3 %collective-permute-start.12 = (f32[256,1536]{1,0:T(8,128)}, f32[256,1536]{1,0:T(8,128)S(1)}, u32[]{:S(2)}, u32[]{:S(2)}) collective-permute-start(f32[256,1536]{1,0:T(8,128)} %get-tuple-element.10), channel_id=1, source_target_pairs={{0,64},{64,0},{1,65},{65,1},{2,66},{66,2},{3,67},{67,3},{4,68},{68... | collective-permute-start | bytes 4718600 | tf_op jit(solution)/shard_map/swap_query_grads/ppermute | solution.py:173
  97.0 6.3 %collective-permute-start.16 = (bf16[2,64,512]{2,1,0:T(8,128)(2,1)S(1)}, bf16[2,64,512]{2,1,0:T(8,128)(2,1)S(1)}, u32[]{:S(2)}, u32[]{:S(2)}) collective-permute-start(bf16[2,64,512]{2,1,0:T(8,128)(2,1)S(1)} %get-tuple-element.21), channel_id=1, source_target_pairs={{0,4},{1,5},{2,6},{3,7},{4,8},{5,9},{6,10},{7,11},{8,12},{9,13},{1... | collective-permute-start | bytes 393224 | tf_op jit(solution)/shard_map/scatter_grads/ppermute | solution.py:169
  97.1 7.1 %collective-permute-start.18 = (bf16[2,64,512]{2,1,0:T(8,128)(2,1)S(1)}, bf16[2,64,512]{2,1,0:T(8,128)(2,1)S(1)}, u32[]{:S(2)}, u32[]{:S(2)}) collective-permute-start(bf16[2,64,512]{2,1,0:T(8,128)(2,1)S(1)} %get-tuple-element.22), channel_id=1, source_target_pairs={{0,12},{1,13},{2,14},{3,15},{4,0},{5,1},{6,2},{7,3},{8,4},{9,5},{1... | collective-permute-start | bytes 393224 | tf_op jit(solution)/shard_map/scatter_grads/ppermute | solution.py:169
  100.4 6.5 %collective-permute-start.17 = (bf16[2,64,512]{2,1,0:T(8,128)(2,1)S(1)}, bf16[2,64,512]{2,1,0:T(8,128)(2,1)S(1)}, u32[]{:S(2)}, u32[]{:S(2)}) collective-permute-start(bf16[2,64,512]{2,1,0:T(8,128)(2,1)S(1)} %get-tuple-element.23), channel_id=1, source_target_pairs={{0,8},{1,9},{2,10},{3,11},{4,12},{5,13},{6,14},{7,15},{8,0},{9,1},... | collective-permute-start | bytes 393224 | tf_op jit(solution)/shard_map/scatter_grads/ppermute | solution.py:169

commit v2 on v1

--- a/solution.py
+++ b/solution.py
@@ -27,7 +27,7 @@
     key_s, val_s, pos_s, rows_q, rows_g, prob_s, gp_s, half_s, ds_s, dk_s, dv_s,
 ):
     step = pl.program_id(0)
-    core, a0, b0, z0, first = (meta[i] for i in range(5))
+    core, a0, first = (meta[i] for i in range(3))
     a_step = jnp.where(core == 0, 1, 4)
     b_step = jnp.where(core == 0, 4, 1)
 
@@ -37,7 +37,7 @@
         for a, piece in enumerate((kv0, kv1, kv2, kv3)):
             for b in range(4):
                 for z in range(4):
-                    slab = ((z0 - z) & 3) * 16 + ((a0 - a) & 3) * a_step + ((b0 - b) & 3) * b_step
+                    slab = z * 16 + ((a0 - a) & 3) * a_step + b * b_step
                     src = pl.ds((b * 4 + z) * SLAB, SLAB)
                     dst = pl.ds(pl.multiple_of(slab * SLAB, SLAB), SLAB)
                     for h in range(MINE):
@@ -100,11 +100,10 @@
     for a, out in enumerate((out0, out1, out2, out3)):
         for b in range(4):
             for z in range(4):
-                slab = z * 16 + ((a0 + a) & 3) * a_step + ((b0 + b) & 3) * b_step
+                slab = z * 16 + ((a0 + a) & 3) * a_step + b * b_step
                 src = pl.ds(pl.multiple_of(slab * SLAB, SLAB), SLAB)
-                dst = pl.ds((b * 4 + z) * SLAB, SLAB)
-                out[0, dst, :] = dk_s[src, :].astype(out.dtype)
-                out[1, dst, :] = dv_s[src, :].astype(out.dtype)
+                out[b, 0, z, 0] = dk_s[src, :].astype(out.dtype)
+                out[b, 0, z, 1] = dv_s[src, :].astype(out.dtype)
 
 
 def attention(meta, q_own, g_own, lse_own, q_oth, g_oth, lse_oth, kv):
@@ -114,20 +113,20 @@
     f32, bf16 = jnp.float32, jnp.bfloat16
     width = GROUP * HEAD_DIM
     own = pl.BlockSpec((ROWS, width), lambda g, m: (0, head(g, m)))
-    oth = pl.BlockSpec((ROWS, width), lambda g, m: (0, g))
+    back = pl.BlockSpec((ROWS, width), lambda g, m: (0, g))
     part = pl.BlockSpec((BLOCK, kv[0].shape[1]), lambda g, m: (0, 0))
-    out = pl.BlockSpec((2, BLOCK, HEAD_DIM), lambda g, m: (0, 0, g))
+    lse = pl.BlockSpec((1, 1, WIDE), lambda g, m: (head(g, m), 0, 0))
+    out_dims = (4, 2, 4, 2, SLAB, 2 * HEAD_DIM)
+    out = pl.BlockSpec(
+        (4, 1, 4, 2, SLAB, HEAD_DIM), lambda g, m: (0, g // 2, 0, 0, 0, g % 2)
+    )
     return pl.pallas_call(
         attention_kernel,
         grid_spec=pltpu.PrefetchScalarGridSpec(
             num_scalar_prefetch=1,
             grid=(MINE,),
-            in_specs=[
-                own, own, pl.BlockSpec((1, 1, WIDE), lambda g, m: (head(g, m), 0, 0)),
-                oth, oth, pl.BlockSpec((1, 1, WIDE), lambda g, m: (g, 0, 0)),
-                part, part, part, part,
-            ],
-            out_specs=[own, oth, out, out, out, out],
+            in_specs=[own, own, lse, own, own, lse, part, part, part, part],
+            out_specs=[own, back, out, out, out, out],
             scratch_shapes=[
                 pltpu.VMEM((MINE, KEYS, HEAD_DIM), bf16),
                 pltpu.VMEM((MINE, KEYS, HEAD_DIM), bf16),
@@ -145,8 +144,8 @@
         out_shape=[
             jax.ShapeDtypeStruct((ROWS, KV_HEADS * width), f32),
             jax.ShapeDtypeStruct((ROWS, MINE * width), f32),
-            jax.ShapeDtypeStruct((2, BLOCK, COLS), f32),
-        ] + [jax.ShapeDtypeStruct((2, BLOCK, COLS), bf16)] * 3,
+            jax.ShapeDtypeStruct(out_dims, f32),
+        ] + [jax.ShapeDtypeStruct(out_dims, bf16)] * 3,
         compiler_params=pltpu.CompilerParams(vmem_limit_bytes=50 * 2**20),
         cost_estimate=pl.CostEstimate(
             flops=8 * 10**9, bytes_accessed=16 * 2**20, transcendentals=6 * 10**6
@@ -155,8 +154,42 @@
     )(meta, q_own, g_own, lse_own, q_oth, g_oth, lse_oth, *kv)
 
 
-def shift(value, axis, by):
-    return lax.ppermute(value, axis, [(i, (i + by) % 4) for i in range(4)])
+def pack_kernel(meta, keys, values, out):
+    core, offset = meta[0], meta[1]
+    tail = jnp.full((SLAB, 128), offset, jnp.int32).astype(jnp.float32).astype(jnp.bfloat16)
+    cols = [pl.ds(pl.multiple_of(n * 512 + core * 256, 128), 256) for n in range(2)]
+    for to in range(4):
+        for n in range(2):
+            out[to, :, n * 256:(n + 1) * 256] = keys[:, cols[n]]
+            out[to, :, COLS + n * 256:COLS + (n + 1) * 256] = values[:, cols[n]]
+        out[to, :, 2 * COLS:] = tail
+
+
+def pack(meta, keys, values):
+    return pl.pallas_call(
+        pack_kernel,
+        in_specs=[
+            pl.BlockSpec(memory_space=pltpu.SMEM),
+            pl.BlockSpec(memory_space=pltpu.VMEM),
+            pl.BlockSpec(memory_space=pltpu.VMEM),
+        ],
+        out_specs=pl.BlockSpec(memory_space=pltpu.VMEM),
+        out_shape=jax.ShapeDtypeStruct((4, SLAB, 2 * COLS + 128), jnp.bfloat16),
+        name="pack_keys_values",
+    )(meta, keys, values)
+
+
+def finish_kernel(got, dk, dv):
+    for n, out in enumerate((dk, dv)):
+        total = got[0, n].astype(jnp.float32)
+        for i in range(1, 8):
+            total = total + got[i, n].astype(jnp.float32)
+        out[...] = total
+
+
+def finish(got):
+    shape = jax.ShapeDtypeStruct((SLAB, 2 * HEAD_DIM), jnp.float32)
+    return pl.pallas_call(finish_kernel, out_shape=[shape, shape], name="add_last")(got)
 
 
 def plane_shift(value, by, x_core):
@@ -169,6 +202,24 @@
     return lax.ppermute(value, ("core", "x", "y"), pairs)
 
 
+def plane_exchange(value, x_core):
+    groups = []
+    for core in range(2):
+        for line in range(4):
+            if core == x_core:
+                groups.append([core * 16 + i * 4 + line for i in range(4)])
+            else:
+                groups.append([core * 16 + line * 4 + i for i in range(4)])
+    return lax.all_to_all(value, ("core", "x", "y"), 0, 0, axis_index_groups=groups)
+
+
+def add(terms):
+    total = terms[0].astype(jnp.float32)
+    for term in terms[1:]:
+        total = total + term.astype(jnp.float32)
+    return total.astype(jnp.bfloat16)
+
+
 def swap(value):
     return lax.ppermute(value, "core", [(0, 1), (1, 0)])
 
@@ -179,61 +230,37 @@
     core, zh, x, y = (lax.axis_index(n) for n in ("core", "zh", "x", "y"))
     other = 1 - core
     seq = zh * 16 + x * 4 + y
-    queries, out_grads = queries[0], out_grads[0]
-
-    def halves(value, which, width, axis=1):
-        return jnp.concatenate(
-            [
-                lax.dynamic_slice_in_dim(value, which * width, width, axis),
-                lax.dynamic_slice_in_dim(value, (2 + which) * width, width, axis),
-            ],
-            axis,
-        )
+    queries, out_grads, lse = queries[0], out_grads[0], logsumexp[0]
 
     with jax.named_scope("gather_keys"):
-        offset = (slab_starts[0] - seq * 256).astype(jnp.bfloat16)
-        payload = jnp.concatenate(
-            [
-                halves(shared_keys, core, 256),
-                halves(shared_values, core, 256),
-                jnp.broadcast_to(offset, (SLAB, 128)),
-            ],
-            1,
-        )
-        block = jnp.concatenate([payload] + [shift(payload, "zh", r) for r in (1, 2, 3)], 0)
+        offset = slab_starts[0] - seq * 256
+        payload = pack(jnp.stack([core, offset]).astype(jnp.int32), shared_keys, shared_values)
+        block = lax.all_to_all(payload, "zh", 0, 0)
+        block = plane_exchange(jnp.broadcast_to(block, (4, *block.shape)), 0)
+        block = block.reshape(BLOCK, 2 * COLS + 128)
+        pieces = [block] + [plane_shift(block, r, 1) for r in (1, 2, 3)]
     with jax.named_scope("swap_queries"):
-        lse = logsumexp[0].reshape(KV_HEADS, WIDE)
-        q_oth = swap(halves(queries, other, 768))
-        g_oth = swap(halves(out_grads, other, 768))
-        lse_oth = swap(halves(lse, other, 2, 0))
-    with jax.named_scope("gather_keys"):
-        block = jnp.concatenate([block] + [plane_shift(block, r, 0) for r in (1, 2, 3)], 0)
-        pieces = [block] + [plane_shift(block, r, 1) for r in (1, 2, 3)]
+        q_oth, g_oth, lse_oth = (swap(v) for v in (queries, out_grads, lse))
 
     a0 = jnp.where(core == 0, y, x)
-    b0 = jnp.where(core == 0, x, y)
-    meta = jnp.stack([core, a0, b0, zh, query_starts[0]]).astype(jnp.int32)
+    meta = jnp.stack([core, a0, query_starts[0]]).astype(jnp.int32)
+    wide = (KV_HEADS, 1, WIDE)
     dq, dq_oth, part0, *parts = attention(
-        meta, queries, out_grads, lse[:, None], q_oth, g_oth, lse_oth[:, None], pieces
+        meta, queries, out_grads, lse.reshape(wide), q_oth, g_oth, lse_oth.reshape(wide), pieces
     )
 
     with jax.named_scope("scatter_grads"):
-        total = part0
-        for r, part in enumerate(parts):
-            total = total + plane_shift(part, r + 1, 1).astype(jnp.float32)
+        parts = [plane_shift(part, r + 1, 1) for r, part in enumerate(parts)]
     with jax.named_scope("swap_query_grads"):
         back = swap(dq_oth)
         dq = lax.dynamic_update_slice(dq, back[:, :768], (0, other * 768))
         dq = lax.dynamic_update_slice(dq, back[:, 768:], (0, (2 + other) * 768))
     with jax.named_scope("scatter_grads"):
-        small = total[:, :64]
-        for r in (1, 2, 3):
-            piece = total[:, r * 64:(r + 1) * 64].astype(jnp.bfloat16)
-            small = small + plane_shift(piece, r, 0).astype(jnp.float32)
-        small = small.reshape(2, 4, SLAB, 2, 256).transpose(3, 1, 0, 2, 4).reshape(8, 2, SLAB, 256)
-        got = lax.all_to_all(small, ("zl", "zh"), 0, 0)
-        grads = jnp.sum(got, 0)
-    return dq[None], grads[0], grads[1]
+        parts[0], dq = lax.optimization_barrier((parts[0], dq))
+        got = plane_exchange(add([part0, *parts]), 0)
+        small = add([got[i] for i in range(4)]).reshape(8, 2, SLAB, 2 * HEAD_DIM)
+        dk, dv = finish(lax.all_to_all(small, ("zl", "zh"), 0, 0))
+    return dq[None], dk, dv
 
 
 def solution(mesh):

time: 126 us -> 121 us (0.960)
  blocking collectives: 15.4 us -> 39.8 us
  waiting for transfers between devices: 48.4 us -> 29 us
  starting transfers between devices: 24 us -> 17.6 us
  local copies, waits for them, and re-layouts: 8.7 us -> 3.57 us
  Pallas kernels: 23.8 us -> 27 us
  other arithmetic: 2.64 us -> 1.17 us
    ppermute x12 -> x6, waiting for transfers between devices: 48.4 us -> 20.6 us  [plane_shift(): return lax.ppermute(value, ('core', 'x', 'y'), pairs)]
    all_to_all x1 -> x3, blocking collectives: 15.4 us -> 39.8 us  [the longest x1 17 us: per_device(): block = lax.all_to_all(payload, 'zh', 0, 0)]
    ppermute x3 -> x0, starting transfers between devices: 9.21 us -> none  [shift(): return lax.ppermute(value, axis, [(i, (i + by) % 4) for i in range(4)])]
    all_to_all x0 -> x1, waiting for transfers between devices: none -> 8.43 us  [plane_exchange(): lax.all_to_all(value, ('core', 'x', 'y'), 0, 0, axis_index_groups=groups)]
    all_to_all x0 -> x1, starting transfers between devices: none -> 4.29 us  [plane_exchange(): lax.all_to_all(value, ('core', 'x', 'y'), 0, 0, axis_index_groups=groups)]
    pallas_call x0 -> x2, Pallas kernels: none -> 2.99 us  [the longest x1 1.53 us: finish(): pl.pallas_call(finish_kernel, out_shape=[shape, shape], name='add_last')]
    unnamed x13 -> x6, local copies, waits for them, and re-layouts: 3.63 us -> 0.8 us
    dynamic_slice x2 -> x0, local copies, waits for them, and re-layouts: 1.48 us -> none  [halves(): lax.dynamic_slice_in_dim(value, which * width, width, axis)]
  transfers between devices with their start and end apart: 19 -> 11, of which waited for: 9 -> 6; matrix products, arithmetic and copies ran while one was open for 5% -> 3% of each run, Pallas kernels for 0% -> 1%
where the time goes in v2:
time: 121 us; the launch traced here: 120 us
  blocking collectives  39.8 us (33%)
  waiting for transfers between devices  29 us (24%)
  Pallas kernels  27 us (22%)
  starting transfers between devices  17.6 us (15%)
  local copies, waits for them, and re-layouts  3.57 us (3%)
  between operations  2 us (2%)
    pallas_call x1, Pallas kernels, attention(): pl.pallas_call(attention_kernel, grid_spec=pltpu.PrefetchScalarGridSpec(n...  24 us
    ppermute x6, waiting for transfers between devices, plane_shift(): return lax.ppermute(value, ('core', 'x', 'y'), pairs)  20.6 us
    all_to_all x1, blocking collectives, per_device(): block = lax.all_to_all(payload, 'zh', 0, 0)  17 us
    ppermute x6, starting transfers between devices, plane_shift(): return lax.ppermute(value, ('core', 'x', 'y'), pairs)  12.7 us
    all_to_all x1, blocking collectives, per_device(): dk, dv = finish(lax.all_to_all(small, ('zl', 'zh'), 0, 0))  12.3 us
    all_to_all x1, blocking collectives, plane_exchange(): lax.all_to_all(value, ('core', 'x', 'y'), 0, 0, axis_index_groups=groups)  10.5 us
    all_to_all x1, waiting for transfers between devices, plane_exchange(): lax.all_to_all(value, ('core', 'x', 'y'), 0, 0, axis_index_groups=groups)  8.43 us
    all_to_all x1, starting transfers between devices, plane_exchange(): lax.all_to_all(value, ('core', 'x', 'y'), 0, 0, axis_index_groups=groups)  4.29 us
  transfers between devices with their start and end apart: 11, of which 6 were waited for; matrix products, arithmetic and copies ran while one was open for 3% of the time, Pallas kernels for 1%

profile of v2, /device:TPU:32, one launch (start us, length us, event | category | flops | bytes accessed | tf_op | source)
XLA Modules:
  0.0 120.2 jit_solution(13692296532669980760)
XLA Ops:
  0.7 0.5 collective-permute-start.1
  1.9 0.7 pad_add_fusion.1.meta
  2.6 1.5 %pack_keys_values.1 = bf16[4,16,1152]{2,1,0:T(8,128)(2,1)} custom-call(s32[2]{0:T(128)} %pad_add_fusion.1.meta, bf16[16,1024]{1,0:T(8,128)(2,1)} %keys.1, bf16[16,1024]{1,0:T(8,128)(2,1)} %values.1), custom_call_target="tpu_custom_call" | custom-call | tf_op jit(solution)/shard_map/gather_keys/pack_keys_values/pallas_call | solution.py:169
  4.0 17.0 %all_to_all.20 = bf16[4,16,1152]{2,1,0:T(8,128)(2,1)S(1)} all-to-all(bf16[4,16,1152]{2,1,0:T(8,128)(2,1)} %pack_keys_values.1), channel_id=1, replica_groups=mesh['zl'=2,'core'=2,'zh'=4,'x'=4,'y'=4] {'zh'}, dimensions={0} | all-to-all | bytes 294912 | tf_op jit(solution)/shard_map/gather_keys/all_to_all | solution.py:238
  21.0 0.9 broadcast_in_dim.6
  21.9 4.3 %all-to-all-start.1 = ((bf16[4,4,16,1152]{3,2,1,0:T(8,128)(2,1)}), bf16[4,4,16,1152]{3,2,1,0:T(8,128)(2,1)S(1)}, u32[]{:S(2)}, u32[]{:S(2)}) async-start(bf16[4,4,16,1152]{3,2,1,0:T(8,128)(2,1)} %broadcast_in_dim.6), calls=%async_computation.1 | async-start | bytes 1179648 | tf_op jit(solution)/shard_map/gather_keys/all_to_all | solution.py:213
  26.2 8.4 %all-to-all-done.1 = bf16[4,4,16,1152]{3,2,1,0:T(8,128)(2,1)S(1)} async-done(((bf16[4,4,16,1152]{3,2,1,0:T(8,128)(2,1)}), bf16[4,4,16,1152]{3,2,1,0:T(8,128)(2,1)S(1)}, u32[]{:S(2)}, u32[]{:S(2)}) %all-to-all-start.1) | async-done | bytes 589856 | tf_op jit(solution)/shard_map/gather_keys/all_to_all | solution.py:213
  34.6 1.6 %collective-permute-start.3 = (bf16[256,1152]{1,0:T(8,128)(2,1)S(1)}, bf16[256,1152]{1,0:T(8,128)(2,1)S(1)}, u32[]{:S(2)}, u32[]{:S(2)}) collective-permute-start(bf16[256,1152]{1,0:T(8,128)(2,1)S(1)} %bitcast.11), channel_id=1, source_target_pairs={{0,1},{1,2},{2,3},{3,0},{4,5},{5,6},{6,7},{7,4},{8,9},{9,10},{10,1... | collective-permute-start | bytes 1769480 | tf_op jit(solution)/shard_map/gather_keys/ppermute | solution.py:202
  36.2 3.3 %collective-permute-start.4 = (bf16[256,1152]{1,0:T(8,128)(2,1)S(1)}, bf16[256,1152]{1,0:T(8,128)(2,1)S(1)}, u32[]{:S(2)}, u32[]{:S(2)}) collective-permute-start(bf16[256,1152]{1,0:T(8,128)(2,1)S(1)} %bitcast.12), channel_id=1, source_target_pairs={{0,2},{1,3},{2,0},{3,1},{4,6},{5,7},{6,4},{7,5},{8,10},{9,11},{10,... | collective-permute-start | bytes 1769480 | tf_op jit(solution)/shard_map/gather_keys/ppermute | solution.py:202
  39.5 1.8 %collective-permute-start.5 = (bf16[256,1152]{1,0:T(8,128)(2,1)S(1)}, bf16[256,1152]{1,0:T(8,128)(2,1)S(1)}, u32[]{:S(2)}, u32[]{:S(2)}) collective-permute-start(bf16[256,1152]{1,0:T(8,128)(2,1)S(1)} %bitcast.13), channel_id=1, source_target_pairs={{0,3},{1,0},{2,1},{3,2},{4,7},{5,4},{6,5},{7,6},{8,11},{9,8},{10,9... | collective-permute-start | bytes 1769480 | tf_op jit(solution)/shard_map/gather_keys/ppermute | solution.py:202
  42.1 3.8 %collective-permute-done.3.kv1 = bf16[256,1152]{1,0:T(8,128)(2,1)S(1)} collective-permute-done((bf16[256,1152]{1,0:T(8,128)(2,1)S(1)}, bf16[256,1152]{1,0:T(8,128)(2,1)S(1)}, u32[]{:S(2)}, u32[]{:S(2)}) %collective-permute-start.3) | collective-permute-done | bytes 589856 | tf_op jit(solution)/shard_map/gather_keys/ppermute | solution.py:202
  45.9 7.8 %collective-permute-done.4.kv2 = bf16[256,1152]{1,0:T(8,128)(2,1)S(1)} collective-permute-done((bf16[256,1152]{1,0:T(8,128)(2,1)S(1)}, bf16[256,1152]{1,0:T(8,128)(2,1)S(1)}, u32[]{:S(2)}, u32[]{:S(2)}) %collective-permute-start.4) | collective-permute-done | bytes 589856 | tf_op jit(solution)/shard_map/gather_keys/ppermute | solution.py:202
  53.7 24.0 %attention_backward.1 = (f32[256,3072]{1,0:T(8,128)}, f32[256,1536]{1,0:T(8,128)}, f32[4,2,4,2,16,256]{5,4,3,2,1,0:T(8,128)}, bf16[4,2,4,2,16,256]{5,4,3,2,1,0:T...) custom-call(s32[3]{0:T(128)S(1)} %pad_add_fusion.meta, ...), custom_call_target="tpu_custom_call" | custom-call | flops 8000000000 | bytes 16777216 | tf_op jit(solution)/shard_map/attention_backward/pallas_call | solution.py:123
  77.7 0.8 copy-done
  78.5 1.4 %collective-permute-start.6 = (bf16[4,2,4,2,16,256]{5,4,3,2,1,0:T(8,128)(2,1)}, bf16[4,2,4,2,16,256]{5,4,3,2,1,0:T(8,128)(2,1)S(1)}, u32[]{:S(2)}, u32[]{:S(2)}) collective-permute-start(bf16[4,2,4,2,16,256]{5,4,3,2,1,0:T(8,128)(2,1)} %copy-done), channel_id=1, source_target_pairs={{0,1},{1,2},{2,3},{3,0},{4,5},{5,6},{6,7},{7,4},{8,9},{9,10},{10,1... | collective-permute-start | bytes 1572872 | tf_op jit(solution)/shard_map/scatter_grads/ppermute | solution.py:202
  79.9 2.1 %collective-permute-start.8 = (bf16[4,2,4,2,16,256]{5,4,3,2,1,0:T(8,128)(2,1)S(1)}, bf16[4,2,4,2,16,256]{5,4,3,2,1,0:T(8,128)(2,1)S(1)}, u32[]{:S(2)}, u32[]{:S(2)}) collective-permute-start(bf16[4,2,4,2,16,256]{5,4,3,2,1,0:T(8,128)(2,1)S(1)} %get-tuple-element.19), channel_id=1, source_target_pairs={{0,2},{1,3},{2,0},{3,1},{4,6},{5,7},{6,4},{7,5},{8,10},{9,11},{10,... | collective-permute-start | bytes 1572872 | tf_op jit(solution)/shard_map/scatter_grads/ppermute | solution.py:202
  82.0 2.5 %collective-permute-start.9 = (bf16[4,2,4,2,16,256]{5,4,3,2,1,0:T(8,128)(2,1)S(1)}, bf16[4,2,4,2,16,256]{5,4,3,2,1,0:T(8,128)(2,1)S(1)}, u32[]{:S(2)}, u32[]{:S(2)}) collective-permute-start(bf16[4,2,4,2,16,256]{5,4,3,2,1,0:T(8,128)(2,1)S(1)} %get-tuple-element.20), channel_id=1, source_target_pairs={{0,3},{1,0},{2,1},{3,2},{4,7},{5,4},{6,5},{7,6},{8,11},{9,8},{10,9... | collective-permute-start | bytes 1572872 | tf_op jit(solution)/shard_map/scatter_grads/ppermute | solution.py:202
  84.5 0.9 slice_dynamic-update-slice_fusion.1
  85.4 0.9 slice_dynamic-update-slice_fusion
  86.3 2.8 %collective-permute-done.6 = bf16[4,2,4,2,16,256]{5,4,3,2,1,0:T(8,128)(2,1)S(1)} collective-permute-done((bf16[4,2,4,2,16,256]{5,4,3,2,1,0:T(8,128)(2,1)}, bf16[4,2,4,2,16,256]{5,4,3,2,1,0:T(8,128)(2,1)S(1)}, u32[]{:S(2)}, u32[]{:S(2)}) %collective-permute-start.6) | collective-permute-done | bytes 524320 | tf_op jit(solution)/shard_map/scatter_grads/ppermute | solution.py:202
  89.1 5.9 %collective-permute-done.8 = bf16[4,2,4,2,16,256]{5,4,3,2,1,0:T(8,128)(2,1)S(1)} collective-permute-done((bf16[4,2,4,2,16,256]{5,4,3,2,1,0:T(8,128)(2,1)S(1)}, bf16[4,2,4,2,16,256]{5,4,3,2,1,0:T(8,128)(2,1)S(1)}, u32[]{:S(2)}, u32[]{:S(2)}) %collective-permute-start.8) | collective-permute-done | bytes 524320 | tf_op jit(solution)/shard_map/scatter_grads/ppermute | solution.py:202
  95.8 10.5 %all_to_all.21 = bf16[4,2,4,2,16,256]{5,4,3,2,1,0:T(8,128)(2,1)S(1)} all-to-all(bf16[4,2,4,2,16,256]{5,4,3,2,1,0:T(8,128)(2,1)S(1)} %add_convert_fusion), channel_id=1, replica_groups={{0,4,8,12},{1,5,9,13},{2,6,10,14},{3,7,11,15},{64,65,66,67},{68,69,70,7..., dimensions={0} | all-to-all | bytes 1048576 | tf_op jit(solution)/shard_map/scatter_grads/all_to_all | solution.py:213
  106.3 12.3 %all_to_all.22.got = bf16[8,2,16,256]{3,2,1,0:T(8,128)(2,1)} all-to-all(bf16[8,2,16,256]{3,2,1,0:T(8,128)(2,1)S(1)} %bitcast.15), channel_id=1, replica_groups=mesh['zl'=2,'core'=2,'zh'=4,'x'=4,'y'=4] {'zl','zh'}, dimensions={0} | all-to-all | bytes 262144 | tf_op jit(solution)/shard_map/scatter_grads/all_to_all | solution.py:262
  118.7 1.5 %add_last.1 = (f32[16,256]{1,0:T(8,128)}, f32[16,256]{1,0:T(8,128)}) custom-call(bf16[8,2,16,256]{3,2,1,0:T(8,128)(2,1)} %all_to_all.22.got), custom_call_target="tpu_custom_call" | custom-call | tf_op jit(solution)/shard_map/scatter_grads/add_last/pallas_call | solution.py:192
  (19 shorter events, 1.1 us)
Async XLA Ops:
  0.6 25.5 %copy-start.2 = (f32[1,24,256]{2,1,0:T(8,128)S(1)}, f32[1,24,256]{2,1,0:T(8,128)}, u32[]{:S(2)}) copy-start(f32[1,24,256]{2,1,0:T(8,128)} %param.9) | copy-start | bytes 73732
  0.6 53.1 %collective-permute-start = (bf16[256,3072]{1,0:T(8,128)(2,1)}, bf16[256,3072]{1,0:T(8,128)(2,1)}, u32[]{:S(2)}, u32[]{:S(2)}) collective-permute-start(bf16[256,3072]{1,0:T(8,128)(2,1)} %bitcast.18), channel_id=1, source_target_pairs={{0,64},{64,0},{1,65},{65,1},{2,66},{66,2},{3,67},{67,3},{4,68},{68... | collective-permute-start | bytes 4718600 | tf_op jit(solution)/shard_map/swap_queries/ppermute | solution.py:224
  0.7 53.0 %collective-permute-start.1 = (bf16[256,3072]{1,0:T(8,128)(2,1)}, bf16[256,3072]{1,0:T(8,128)(2,1)}, u32[]{:S(2)}, u32[]{:S(2)}) collective-permute-start(bf16[256,3072]{1,0:T(8,128)(2,1)} %bitcast.20), channel_id=1, source_target_pairs={{0,64},{64,0},{1,65},{65,1},{2,66},{66,2},{3,67},{67,3},{4,68},{68... | collective-permute-start | bytes 4718600 | tf_op jit(solution)/shard_map/swap_queries/ppermute | solution.py:224
  21.9 12.7 %all-to-all-start.1 = ((bf16[4,4,16,1152]{3,2,1,0:T(8,128)(2,1)}), bf16[4,4,16,1152]{3,2,1,0:T(8,128)(2,1)S(1)}, u32[]{:S(2)}, u32[]{:S(2)}) async-start(bf16[4,4,16,1152]{3,2,1,0:T(8,128)(2,1)} %broadcast_in_dim.6), calls=%async_computation.1 | async-start | bytes 1179648 | tf_op jit(solution)/shard_map/gather_keys/all_to_all | solution.py:213
  26.2 13.3 %collective-permute-start.2 = (f32[24,256]{1,0:T(8,128)S(1)}, f32[24,256]{1,0:T(8,128)S(1)}, u32[]{:S(2)}, u32[]{:S(2)}) collective-permute-start(f32[24,256]{1,0:T(8,128)S(1)} %bitcast.16), channel_id=1, source_target_pairs={{0,64},{64,0},{1,65},{65,1},{2,66},{66,2},{3,67},{67,3},{4,68},{68... | collective-permute-start | bytes 73736 | tf_op jit(solution)/shard_map/swap_queries/ppermute | solution.py:224
  34.6 11.3 %collective-permute-start.3 = (bf16[256,1152]{1,0:T(8,128)(2,1)S(1)}, bf16[256,1152]{1,0:T(8,128)(2,1)S(1)}, u32[]{:S(2)}, u32[]{:S(2)}) collective-permute-start(bf16[256,1152]{1,0:T(8,128)(2,1)S(1)} %bitcast.11), channel_id=1, source_target_pairs={{0,1},{1,2},{2,3},{3,0},{4,5},{5,6},{6,7},{7,4},{8,9},{9,10},{10,1... | collective-permute-start | bytes 1769480 | tf_op jit(solution)/shard_map/gather_keys/ppermute | solution.py:202
  36.2 17.4 %collective-permute-start.4 = (bf16[256,1152]{1,0:T(8,128)(2,1)S(1)}, bf16[256,1152]{1,0:T(8,128)(2,1)S(1)}, u32[]{:S(2)}, u32[]{:S(2)}) collective-permute-start(bf16[256,1152]{1,0:T(8,128)(2,1)S(1)} %bitcast.12), channel_id=1, source_target_pairs={{0,2},{1,3},{2,0},{3,1},{4,6},{5,7},{6,4},{7,5},{8,10},{9,11},{10,... | collective-permute-start | bytes 1769480 | tf_op jit(solution)/shard_map/gather_keys/ppermute | solution.py:202
  39.5 14.2 %collective-permute-start.5 = (bf16[256,1152]{1,0:T(8,128)(2,1)S(1)}, bf16[256,1152]{1,0:T(8,128)(2,1)S(1)}, u32[]{:S(2)}, u32[]{:S(2)}) collective-permute-start(bf16[256,1152]{1,0:T(8,128)(2,1)S(1)} %bitcast.13), channel_id=1, source_target_pairs={{0,3},{1,0},{2,1},{3,2},{4,7},{5,4},{6,5},{7,6},{8,11},{9,8},{10,9... | collective-permute-start | bytes 1769480 | tf_op jit(solution)/shard_map/gather_keys/ppermute | solution.py:202
  77.7 0.8 copy-start
  78.5 6.0 %collective-permute-start.7 = (f32[256,1536]{1,0:T(8,128)}, f32[256,1536]{1,0:T(8,128)S(1)}, u32[]{:S(2)}, u32[]{:S(2)}) collective-permute-start(f32[256,1536]{1,0:T(8,128)} %get-tuple-element.15), channel_id=1, source_target_pairs={{0,64},{64,0},{1,65},{65,1},{2,66},{66,2},{3,67},{67,3},{4,68},{68... | collective-permute-start | bytes 4718600 | tf_op jit(solution)/shard_map/swap_query_grads/ppermute | solution.py:224
  78.5 10.6 %collective-permute-start.6 = (bf16[4,2,4,2,16,256]{5,4,3,2,1,0:T(8,128)(2,1)}, bf16[4,2,4,2,16,256]{5,4,3,2,1,0:T(8,128)(2,1)S(1)}, u32[]{:S(2)}, u32[]{:S(2)}) collective-permute-start(bf16[4,2,4,2,16,256]{5,4,3,2,1,0:T(8,128)(2,1)} %copy-done), channel_id=1, source_target_pairs={{0,1},{1,2},{2,3},{3,0},{4,5},{5,6},{6,7},{7,4},{8,9},{9,10},{10,1... | collective-permute-start | bytes 1572872 | tf_op jit(solution)/shard_map/scatter_grads/ppermute | solution.py:202
  79.9 15.1 %collective-permute-start.8 = (bf16[4,2,4,2,16,256]{5,4,3,2,1,0:T(8,128)(2,1)S(1)}, bf16[4,2,4,2,16,256]{5,4,3,2,1,0:T(8,128)(2,1)S(1)}, u32[]{:S(2)}, u32[]{:S(2)}) collective-permute-start(bf16[4,2,4,2,16,256]{5,4,3,2,1,0:T(8,128)(2,1)S(1)} %get-tuple-element.19), channel_id=1, source_target_pairs={{0,2},{1,3},{2,0},{3,1},{4,6},{5,7},{6,4},{7,5},{8,10},{9,11},{10,... | collective-permute-start | bytes 1572872 | tf_op jit(solution)/shard_map/scatter_grads/ppermute | solution.py:202
  82.0 13.4 %collective-permute-start.9 = (bf16[4,2,4,2,16,256]{5,4,3,2,1,0:T(8,128)(2,1)S(1)}, bf16[4,2,4,2,16,256]{5,4,3,2,1,0:T(8,128)(2,1)S(1)}, u32[]{:S(2)}, u32[]{:S(2)}) collective-permute-start(bf16[4,2,4,2,16,256]{5,4,3,2,1,0:T(8,128)(2,1)S(1)} %get-tuple-element.20), channel_id=1, source_target_pairs={{0,3},{1,0},{2,1},{3,2},{4,7},{5,4},{6,5},{7,6},{8,11},{9,8},{10,9... | collective-permute-start | bytes 1572872 | tf_op jit(solution)/shard_map/scatter_grads/ppermute | solution.py:202
  84.5 10.9 %copy-start.1 = (f32[4,2,4,2,16,256]{5,4,3,2,1,0:T(8,128)S(1)}, f32[4,2,4,2,16,256]{5,4,3,2,1,0:T(8,128)}, u32[]{:S(2)}) copy-start(f32[4,2,4,2,16,256]{5,4,3,2,1,0:T(8,128)} %get-tuple-element.17) | copy-start | bytes 3145732

commit v3 on v2

--- a/solution.py
+++ b/solution.py
@@ -14,18 +14,24 @@
 SCALE = HEAD_DIM**-0.5
 LOG2E = 1.4426950408889634
 WIDE = GROUP * ROWS
-MINE = KV_HEADS // 2
-COLS = MINE * HEAD_DIM
+PAIR = 2
+COLS = PAIR * HEAD_DIM
+PAYLOAD = 2 * COLS + 128
 KEYS = 1024
 BLOCK = 256
 AXES = ("zl", "core", "zh", "x", "y")
 
 
+SMALL = pltpu.CompilerParams(vmem_limit_bytes=8 * 2**20)
+
+
 def attention_kernel(
-    meta, q_own, g_own, lse_own, q_oth, g_oth, lse_oth, kv0, kv1, kv2, kv3,
-    dq_own, dq_oth, out0, out1, out2, out3,
-    key_s, val_s, pos_s, rows_q, rows_g, prob_s, gp_s, half_s, ds_s, dk_s, dv_s,
+    meta, q_own, g_own, lse_own, q_oth, g_oth, lse_oth, kv0, kv1, kv2, kv3, *rest
 ):
+    (
+        dq_own, dq_oth, out0, out1, out2, out3,
+        key_s, val_s, pos_s, rows_q, rows_g, prob_s, gp_s, half_s, ds_s, dk_s, dv_s,
+    ) = rest[-17:]
     step = pl.program_id(0)
     core, a0, first = (meta[i] for i in range(3))
     a_step = jnp.where(core == 0, 1, 4)
@@ -40,7 +46,7 @@
                     slab = z * 16 + ((a0 - a) & 3) * a_step + b * b_step
                     src = pl.ds((b * 4 + z) * SLAB, SLAB)
                     dst = pl.ds(pl.multiple_of(slab * SLAB, SLAB), SLAB)
-                    for h in range(MINE):
+                    for h in range(PAIR):
                         key_s[h, dst, :] = piece[src, h * 128:(h + 1) * 128]
                         val_s[h, dst, :] = piece[src, COLS + h * 128:COLS + (h + 1) * 128]
                     pos_s[dst, :] = (
@@ -102,34 +108,36 @@
             for z in range(4):
                 slab = z * 16 + ((a0 + a) & 3) * a_step + b * b_step
                 src = pl.ds(pl.multiple_of(slab * SLAB, SLAB), SLAB)
-                out[b, 0, z, 0] = dk_s[src, :].astype(out.dtype)
-                out[b, 0, z, 1] = dv_s[src, :].astype(out.dtype)
-
-
-def attention(meta, q_own, g_own, lse_own, q_oth, g_oth, lse_oth, kv):
+                out[b, z, 0] = dk_s[src, :].astype(out.dtype)
+                out[b, z, 1] = dv_s[src, :].astype(out.dtype)
+
+
+def attention(chunk, meta, q_own, g_own, lse_own, q_oth, g_oth, lse_oth, kv, partly):
     def head(g, m):
-        return (g // 2) * 4 + m[0] * 2 + g % 2
-
+        return chunk * 4 + m[0] * 2 + g
+
+    q_own, g_own, q_oth, g_oth = (
+        pltpu.with_memory_space_constraint(v, pltpu.HBM) for v in (q_own, g_own, q_oth, g_oth)
+    )
     f32, bf16 = jnp.float32, jnp.bfloat16
     width = GROUP * HEAD_DIM
     own = pl.BlockSpec((ROWS, width), lambda g, m: (0, head(g, m)))
-    back = pl.BlockSpec((ROWS, width), lambda g, m: (0, g))
-    part = pl.BlockSpec((BLOCK, kv[0].shape[1]), lambda g, m: (0, 0))
+    back = pl.BlockSpec((ROWS, width), lambda g, m: (0, chunk * 2 + g))
+    part = pl.BlockSpec((BLOCK, PAYLOAD), lambda g, m: (0, 0))
     lse = pl.BlockSpec((1, 1, WIDE), lambda g, m: (head(g, m), 0, 0))
-    out_dims = (4, 2, 4, 2, SLAB, 2 * HEAD_DIM)
-    out = pl.BlockSpec(
-        (4, 1, 4, 2, SLAB, HEAD_DIM), lambda g, m: (0, g // 2, 0, 0, 0, g % 2)
-    )
+    out_dims = (4, 4, 2, SLAB, PAIR * HEAD_DIM)
+    out = pl.BlockSpec((4, 4, 2, SLAB, HEAD_DIM), lambda g, m: (0, 0, 0, 0, g))
     return pl.pallas_call(
         attention_kernel,
         grid_spec=pltpu.PrefetchScalarGridSpec(
             num_scalar_prefetch=1,
-            grid=(MINE,),
-            in_specs=[own, own, lse, own, own, lse, part, part, part, part],
+            grid=(PAIR,),
+            in_specs=[own, own, lse, own, own, lse, part, part, part, part]
+            + [pl.BlockSpec(memory_space=pl.ANY)] * len(partly),
             out_specs=[own, back, out, out, out, out],
             scratch_shapes=[
-                pltpu.VMEM((MINE, KEYS, HEAD_DIM), bf16),
-                pltpu.VMEM((MINE, KEYS, HEAD_DIM), bf16),
+                pltpu.VMEM((PAIR, KEYS, HEAD_DIM), bf16),
+                pltpu.VMEM((PAIR, KEYS, HEAD_DIM), bf16),
                 pltpu.VMEM((KEYS, 128), f32),
                 pltpu.VMEM((2, WIDE, HEAD_DIM), bf16),
                 pltpu.VMEM((2, WIDE, HEAD_DIM), bf16),
@@ -142,30 +150,33 @@
             ],
         ),
         out_shape=[
-            jax.ShapeDtypeStruct((ROWS, KV_HEADS * width), f32),
-            jax.ShapeDtypeStruct((ROWS, MINE * width), f32),
-            jax.ShapeDtypeStruct(out_dims, f32),
-        ] + [jax.ShapeDtypeStruct(out_dims, bf16)] * 3,
-        compiler_params=pltpu.CompilerParams(vmem_limit_bytes=50 * 2**20),
+            pltpu.HBM((ROWS, KV_HEADS * width), f32),
+            pltpu.HBM((ROWS, KV_HEADS // 2 * width), f32),
+            pltpu.HBM(out_dims, f32),
+        ] + [pltpu.HBM(out_dims, bf16)] * 3,
+        input_output_aliases={11 + n: n for n in range(len(partly))},
+        compiler_params=pltpu.CompilerParams(vmem_limit_bytes=36 * 2**20),
         cost_estimate=pl.CostEstimate(
-            flops=8 * 10**9, bytes_accessed=16 * 2**20, transcendentals=6 * 10**6
+            flops=8 * 10**9, bytes_accessed=8 * 2**20, transcendentals=3 * 10**6
         ),
         name="attention_backward",
-    )(meta, q_own, g_own, lse_own, q_oth, g_oth, lse_oth, *kv)
-
-
-def pack_kernel(meta, keys, values, out):
-    core, offset = meta[0], meta[1]
+    )(meta, q_own, g_own, lse_own, q_oth, g_oth, lse_oth, *kv, *partly)
+
+
+def pack_kernel(starts, keys, values, out):
+    core, zh, x, y = (lax.axis_index(n) for n in ("core", "zh", "x", "y"))
+    offset = starts[0] - (zh * 16 + x * 4 + y) * 256
     tail = jnp.full((SLAB, 128), offset, jnp.int32).astype(jnp.float32).astype(jnp.bfloat16)
-    cols = [pl.ds(pl.multiple_of(n * 512 + core * 256, 128), 256) for n in range(2)]
-    for to in range(4):
-        for n in range(2):
-            out[to, :, n * 256:(n + 1) * 256] = keys[:, cols[n]]
-            out[to, :, COLS + n * 256:COLS + (n + 1) * 256] = values[:, cols[n]]
-        out[to, :, 2 * COLS:] = tail
-
-
-def pack(meta, keys, values):
+    for chunk in range(2):
+        cols = pl.ds(pl.multiple_of(chunk * 512 + core * COLS, 128), COLS)
+        for to in range(4):
+            out[to, chunk, :, :COLS] = keys[:, cols]
+            out[to, chunk, :, COLS:2 * COLS] = values[:, cols]
+            out[to, chunk, :, 2 * COLS:] = tail
+
+
+def pack(starts, keys, values):
+    keys, values = (pltpu.with_memory_space_constraint(v, pltpu.HBM) for v in (keys, values))
     return pl.pallas_call(
         pack_kernel,
         in_specs=[
@@ -174,9 +185,33 @@
             pl.BlockSpec(memory_space=pltpu.VMEM),
         ],
         out_specs=pl.BlockSpec(memory_space=pltpu.VMEM),
-        out_shape=jax.ShapeDtypeStruct((4, SLAB, 2 * COLS + 128), jnp.bfloat16),
+        out_shape=jax.ShapeDtypeStruct((4, 2, SLAB, PAYLOAD), jnp.bfloat16),
+        compiler_params=SMALL,
         name="pack_keys_values",
-    )(meta, keys, values)
+    )(starts, keys, values)
+
+
+def join_kernel(*refs):
+    out = refs[-1]
+    total = refs[0][...]
+    for ref in refs[1:4]:
+        total = total + ref[...].astype(jnp.float32)
+    out[:, 0] = total.astype(jnp.bfloat16)
+
+
+def join(chunk, terms, partly):
+    dims = terms[0].shape
+    whole = pl.BlockSpec(dims, lambda i: (0,) * 5)
+    return pl.pallas_call(
+        join_kernel,
+        grid=(1,),
+        in_specs=[whole] * 4 + [pl.BlockSpec(memory_space=pl.ANY)] * len(partly),
+        out_specs=pl.BlockSpec((dims[0], 1, *dims[1:]), lambda i: (0, chunk, 0, 0, 0, 0)),
+        out_shape=jax.ShapeDtypeStruct((dims[0], 2, *dims[1:]), jnp.bfloat16),
+        input_output_aliases={4: 0} if partly else {},
+        compiler_params=SMALL,
+        name="add_first",
+    )(*terms, *partly)
 
 
 def finish_kernel(got, dk, dv):
@@ -189,7 +224,7 @@
 
 def finish(got):
     shape = jax.ShapeDtypeStruct((SLAB, 2 * HEAD_DIM), jnp.float32)
-    return pl.pallas_call(finish_kernel, out_shape=[shape, shape], name="add_last")(got)
+    return pl.pallas_call(finish_kernel, out_shape=[shape, shape], compiler_params=SMALL, name="add_last")(got)
 
 
 def plane_shift(value, by, x_core):
@@ -227,37 +262,48 @@
 def per_device(
     queries, out_grads, logsumexp, shared_keys, shared_values, query_starts, slab_starts
 ):
-    core, zh, x, y = (lax.axis_index(n) for n in ("core", "zh", "x", "y"))
+    core, x, y = (lax.axis_index(n) for n in ("core", "x", "y"))
     other = 1 - core
-    seq = zh * 16 + x * 4 + y
     queries, out_grads, lse = queries[0], out_grads[0], logsumexp[0]
 
     with jax.named_scope("gather_keys"):
-        offset = slab_starts[0] - seq * 256
-        payload = pack(jnp.stack([core, offset]).astype(jnp.int32), shared_keys, shared_values)
+        payload = pack(slab_starts, shared_keys, shared_values)
         block = lax.all_to_all(payload, "zh", 0, 0)
         block = plane_exchange(jnp.broadcast_to(block, (4, *block.shape)), 0)
-        block = block.reshape(BLOCK, 2 * COLS + 128)
-        pieces = [block] + [plane_shift(block, r, 1) for r in (1, 2, 3)]
+        pieces = []
+        for chunk in range(2):
+            piece = block[:, :, chunk].reshape(BLOCK, PAYLOAD)
+            pieces.append([piece] + [plane_shift(piece, r, 1) for r in (1, 2, 3)])
     with jax.named_scope("swap_queries"):
         q_oth, g_oth, lse_oth = (swap(v) for v in (queries, out_grads, lse))
 
     a0 = jnp.where(core == 0, y, x)
     meta = jnp.stack([core, a0, query_starts[0]]).astype(jnp.int32)
     wide = (KV_HEADS, 1, WIDE)
-    dq, dq_oth, part0, *parts = attention(
-        meta, queries, out_grads, lse.reshape(wide), q_oth, g_oth, lse_oth.reshape(wide), pieces
-    )
-
-    with jax.named_scope("scatter_grads"):
-        parts = [plane_shift(part, r + 1, 1) for r, part in enumerate(parts)]
+    lse, lse_oth = lse.reshape(wide), lse_oth.reshape(wide)
+    partly, sums = [], []
+    for chunk in range(2):
+        *partly, part0, part1, part2, part3 = attention(
+            chunk, meta, queries, out_grads, lse, q_oth, g_oth, lse_oth, pieces[chunk], partly
+        )
+        with jax.named_scope("scatter_grads"):
+            if sums:
+                part0, part1, part2, part3, partly, sums = lax.optimization_barrier(
+                    (part0, part1, part2, part3, partly, sums)
+                )
+            parts = [plane_shift(p, r, 1) for r, p in ((1, part1), (2, part2), (3, part3))]
+        sums.append([part0, *parts])
+
+    dq, dq_oth = partly
     with jax.named_scope("swap_query_grads"):
         back = swap(dq_oth)
         dq = lax.dynamic_update_slice(dq, back[:, :768], (0, other * 768))
         dq = lax.dynamic_update_slice(dq, back[:, 768:], (0, (2 + other) * 768))
     with jax.named_scope("scatter_grads"):
-        parts[0], dq = lax.optimization_barrier((parts[0], dq))
-        got = plane_exchange(add([part0, *parts]), 0)
+        sums[1][1], dq = lax.optimization_barrier((sums[1][1], dq))
+        total = join(0, sums[0], [])
+        total = join(1, sums[1], [total])
+        got = plane_exchange(total, 0)
         small = add([got[i] for i in range(4)]).reshape(8, 2, SLAB, 2 * HEAD_DIM)
         dk, dv = finish(lax.all_to_all(small, ("zl", "zh"), 0, 0))
     return dq[None], dk, dv

time: 121 us -> 117 us (0.967)
  waiting for transfers between devices: 29 us -> 15 us
  starting transfers between devices: 17.6 us -> 28 us
  Pallas kernels: 27 us -> 28.3 us
  blocking collectives: 39.8 us -> 38.5 us
    ppermute x6 -> x12, waiting for transfers between devices: 20.6 us -> 6.19 us  [plane_shift(): return lax.ppermute(value, ('core', 'x', 'y'), pairs)]
    ppermute x6 -> x12, starting transfers between devices: 12.7 us -> 23 us  [plane_shift(): return lax.ppermute(value, ('core', 'x', 'y'), pairs)]
    pallas_call x1 -> x2, Pallas kernels: 24 us -> 26.6 us  [attention(): pl.pallas_call(attention_kernel, grid_spec=pltpu.PrefetchScalarGridSpec(n...]
    all_to_all x1, blocking collectives: 12.3 us -> 11 us  [per_device(): dk, dv = finish(lax.all_to_all(small, ('zl', 'zh'), 0, 0))]
  transfers between devices with their start and end apart: 11 -> 17, of which waited for: 6 -> 4; matrix products, arithmetic and copies ran while one was open for 3% -> 3% of each run, Pallas kernels for 1% -> 24%
where the time goes in v3:
time: 117 us; the launch traced here: 116 us
  blocking collectives  38.5 us (33%)
  Pallas kernels  28.3 us (24%)
  starting transfers between devices  28 us (24%)
  waiting for transfers between devices  15 us (13%)
  local copies, waits for them, and re-layouts  4.06 us (3%)
  between operations  2.09 us (2%)
    pallas_call x2, Pallas kernels, attention(): pl.pallas_call(attention_kernel, grid_spec=pltpu.PrefetchScalarGridSpec(n...  26.6 us
    ppermute x12, starting transfers between devices, plane_shift(): return lax.ppermute(value, ('core', 'x', 'y'), pairs)  23 us
    all_to_all x1, blocking collectives, per_device(): block = lax.all_to_all(payload, 'zh', 0, 0)  17 us
    all_to_all x1, blocking collectives, per_device(): dk, dv = finish(lax.all_to_all(small, ('zl', 'zh'), 0, 0))  11 us
    all_to_all x1, blocking collectives, plane_exchange(): lax.all_to_all(value, ('core', 'x', 'y'), 0, 0, axis_index_groups=groups)  10.5 us
    all_to_all x1, waiting for transfers between devices, plane_exchange(): lax.all_to_all(value, ('core', 'x', 'y'), 0, 0, axis_index_groups=groups)  8.78 us
    ppermute x12, waiting for transfers between devices, plane_shift(): return lax.ppermute(value, ('core', 'x', 'y'), pairs)  6.19 us
    all_to_all x1, starting transfers between devices, plane_exchange(): lax.all_to_all(value, ('core', 'x', 'y'), 0, 0, axis_index_groups=groups)  4.29 us
  transfers between devices with their start and end apart: 17, of which 4 were waited for; matrix products, arithmetic and copies ran while one was open for 3% of the time, Pallas kernels for 24%

profile of v3, /device:TPU:32, one launch (start us, length us, event | category | flops | bytes accessed | tf_op | source)
XLA Modules:
  0.0 116.0 jit_solution(4527573229449188318)
XLA Ops:
  2.7 17.0 %all_to_all.20 = bf16[4,2,16,640]{3,2,1,0:T(8,128)(2,1)S(1)} all-to-all(bf16[4,2,16,640]{3,2,1,0:T(8,128)(2,1)S(1)} %pack_keys_values.1), channel_id=1, replica_groups=mesh['zl'=2,'core'=2,'zh'=4,'x'=4,'y'=4] {'zh'}, dimensions={0} | all-to-all | bytes 327680 | tf_op jit(solution)/shard_map/gather_keys/all_to_all | solution.py:271
  19.7 0.9 broadcast_in_dim.6
  20.6 4.3 %all-to-all-start.1 = ((bf16[4,4,2,16,640]{4,3,1,2,0:T(8,128)(2,1)}), bf16[4,4,2,16,640]{4,3,1,2,0:T(8,128)(2,1)S(1)}, u32[]{:S(2)}, u32[]{:S(2)}) async-start(bf16[4,4,2,16,640]{4,3,1,2,0:T(8,128)(2,1)} %broadcast_in_dim.6), calls=%async_computation.1 | async-start | bytes 1310720 | tf_op jit(solution)/shard_map/gather_keys/all_to_all | solution.py:248
  24.9 8.8 %all-to-all-done.1 = bf16[4,4,2,16,640]{4,3,1,2,0:T(8,128)(2,1)S(1)} async-done(((bf16[4,4,2,16,640]{4,3,1,2,0:T(8,128)(2,1)}), bf16[4,4,2,16,640]{4,3,1,2,0:T(8,128)(2,1)S(1)}, u32[]{:S(2)}, u32[]{:S(2)}) %all-to-all-start.1) | async-done | bytes 655392 | tf_op jit(solution)/shard_map/gather_keys/all_to_all | solution.py:248
  33.8 1.7 %collective-permute-start.6 = (bf16[256,640]{1,0:T(8,128)(2,1)S(1)}, bf16[256,640]{1,0:T(8,128)(2,1)S(1)}, u32[]{:S(2)}, u32[]{:S(2)}) collective-permute-start(bf16[256,640]{1,0:T(8,128)(2,1)S(1)} %bitcast.13), channel_id=1, source_target_pairs={{0,1},{1,2},{2,3},{3,0},{4,5},{5,6},{6,7},{7,4},{8,9},{9,10},{10,1... | collective-permute-start | bytes 983048 | tf_op jit(solution)/shard_map/gather_keys/ppermute | solution.py:237
  35.5 3.3 %collective-permute-start.7 = (bf16[256,640]{1,0:T(8,128)(2,1)S(1)}, bf16[256,640]{1,0:T(8,128)(2,1)S(1)}, u32[]{:S(2)}, u32[]{:S(2)}) collective-permute-start(bf16[256,640]{1,0:T(8,128)(2,1)S(1)} %bitcast.14), channel_id=1, source_target_pairs={{0,2},{1,3},{2,0},{3,1},{4,6},{5,7},{6,4},{7,5},{8,10},{9,11},{10,... | collective-permute-start | bytes 983048 | tf_op jit(solution)/shard_map/gather_keys/ppermute | solution.py:237
  38.8 1.8 %collective-permute-start.8 = (bf16[256,640]{1,0:T(8,128)(2,1)S(1)}, bf16[256,640]{1,0:T(8,128)(2,1)S(1)}, u32[]{:S(2)}, u32[]{:S(2)}) collective-permute-start(bf16[256,640]{1,0:T(8,128)(2,1)S(1)} %bitcast.15), channel_id=1, source_target_pairs={{0,3},{1,0},{2,1},{3,2},{4,7},{5,4},{6,5},{7,6},{8,11},{9,8},{10,9... | collective-permute-start | bytes 983048 | tf_op jit(solution)/shard_map/gather_keys/ppermute | solution.py:237
  41.5 0.9 collective-permute-done.6.kv1
  42.4 3.7 %collective-permute-start.3 = (bf16[256,640]{1,0:T(8,128)(2,1)S(1)}, bf16[256,640]{1,0:T(8,128)(2,1)S(1)}, u32[]{:S(2)}, u32[]{:S(2)}) collective-permute-start(bf16[256,640]{1,0:T(8,128)(2,1)S(1)} %bitcast.9), channel_id=1, source_target_pairs={{0,1},{1,2},{2,3},{3,0},{4,5},{5,6},{6,7},{7,4},{8,9},{9,10},{10,1... | collective-permute-start | bytes 983048 | tf_op jit(solution)/shard_map/gather_keys/ppermute | solution.py:237
  46.1 1.3 %collective-permute-done.7.kv2 = bf16[256,640]{1,0:T(8,128)(2,1)S(1)} collective-permute-done((bf16[256,640]{1,0:T(8,128)(2,1)S(1)}, bf16[256,640]{1,0:T(8,128)(2,1)S(1)}, u32[]{:S(2)}, u32[]{:S(2)}) %collective-permute-start.7) | collective-permute-done | bytes 327712 | tf_op jit(solution)/shard_map/gather_keys/ppermute | solution.py:237
  47.4 1.2 %collective-permute-start.4 = (bf16[256,640]{1,0:T(8,128)(2,1)S(1)}, bf16[256,640]{1,0:T(8,128)(2,1)S(1)}, u32[]{:S(2)}, u32[]{:S(2)}) collective-permute-start(bf16[256,640]{1,0:T(8,128)(2,1)S(1)} %bitcast.10), channel_id=1, source_target_pairs={{0,2},{1,3},{2,0},{3,1},{4,6},{5,7},{6,4},{7,5},{8,10},{9,11},{10,... | collective-permute-start | bytes 983048 | tf_op jit(solution)/shard_map/gather_keys/ppermute | solution.py:237
  48.7 2.6 %collective-permute-start.5 = (bf16[256,640]{1,0:T(8,128)(2,1)S(1)}, bf16[256,640]{1,0:T(8,128)(2,1)S(1)}, u32[]{:S(2)}, u32[]{:S(2)}) collective-permute-start(bf16[256,640]{1,0:T(8,128)(2,1)S(1)} %bitcast.11), channel_id=1, source_target_pairs={{0,3},{1,0},{2,1},{3,2},{4,7},{5,4},{6,5},{7,6},{8,11},{9,8},{10,9... | collective-permute-start | bytes 983048 | tf_op jit(solution)/shard_map/gather_keys/ppermute | solution.py:237
  51.3 1.2 %copy-done.3 = bf16[256,3072]{1,0:T(8,128)(2,1)} copy-done((bf16[256,3072]{1,0:T(8,128)(2,1)}, bf16[256,3072]{1,0:T(8,128)(2,1)S(1)}, u32[]{:S(2)}) %copy-start.3) | copy-done | bytes 1572888
  52.5 13.3 %attention_backward.2 = (f32[256,3072]{1,0:T(8,128)}, f32[256,1536]{1,0:T(8,128)}, f32[4,4,2,16,256]{4,3,2,1,0:T(8,128)}, bf16[4,4,2,16,256]{4,3,2,1,0:T(8,128)(...) custom-call(s32[3]{0:T(128)S(1)} %pad_add_fusion.meta, bf16[256,3072]{1,0:T(8,128)(2,1)} %bitcast.21, ...), custom_call_target="tpu_custom_call" | custom-call | flops 8000000000 | bytes 8388608 | tf_op jit(solution)/shard_map/attention_backward/pallas_call | solution.py:130
  66.0 2.1 %collective-permute-start.11 = (bf16[4,4,2,16,256]{4,3,2,1,0:T(8,128)(2,1)}, bf16[4,4,2,16,256]{4,3,2,1,0:T(8,128)(2,1)S(1)}, u32[]{:S(2)}, u32[]{:S(2)}) collective-permute-start(bf16[4,4,2,16,256]{4,3,2,1,0:T(8,128)(2,1)} %get-tuple-element.40), channel_id=1, source_target_pairs={{0,3},{1,0},{2,1},{3,2},{4,7},{5,4},{6,5},{7,6},{8,11},{9,8},{10,9... | collective-permute-start | bytes 786440 | tf_op jit(solution)/shard_map/scatter_grads/ppermute | solution.py:237
  68.1 13.3 %attention_backward.3 = (f32[256,3072]{1,0:T(8,128)}, f32[256,1536]{1,0:T(8,128)}, f32[4,4,2,16,256]{4,3,2,1,0:T(8,128)}, bf16[4,4,2,16,256]{4,3,2,1,0:T(8,128)(...) custom-call(s32[3]{0:T(128)S(1)} %pad_add_fusion.meta, ...), custom_call_target="tpu_custom_call", output_to_operand_aliasing={{0}: (11, {}), {1}: (12, {})} | custom-call | flops 8000000000 | bytes 8388608 | tf_op jit(solution)/shard_map/attention_backward/pallas_call | solution.py:130
  81.6 1.5 %collective-permute-start.12 = (bf16[4,4,2,16,256]{4,3,2,1,0:T(8,128)(2,1)}, bf16[4,4,2,16,256]{4,3,2,1,0:T(8,128)(2,1)S(1)}, u32[]{:S(2)}, u32[]{:S(2)}) collective-permute-start(bf16[4,4,2,16,256]{4,3,2,1,0:T(8,128)(2,1)} %get-tuple-element.41), channel_id=1, source_target_pairs={{0,1},{1,2},{2,3},{3,0},{4,5},{5,6},{6,7},{7,4},{8,9},{9,10},{10,1... | collective-permute-start | bytes 786440 | tf_op jit(solution)/shard_map/scatter_grads/ppermute | solution.py:237
  83.1 3.3 %collective-permute-start.14 = (bf16[4,4,2,16,256]{4,3,2,1,0:T(8,128)(2,1)}, bf16[4,4,2,16,256]{4,3,2,1,0:T(8,128)(2,1)S(1)}, u32[]{:S(2)}, u32[]{:S(2)}) collective-permute-start(bf16[4,4,2,16,256]{4,3,2,1,0:T(8,128)(2,1)} %get-tuple-element.47), channel_id=1, source_target_pairs={{0,2},{1,3},{2,0},{3,1},{4,6},{5,7},{6,4},{7,5},{8,10},{9,11},{10,... | collective-permute-start | bytes 786440 | tf_op jit(solution)/shard_map/scatter_grads/ppermute | solution.py:237
  86.4 1.4 %collective-permute-start.15 = (bf16[4,4,2,16,256]{4,3,2,1,0:T(8,128)(2,1)}, bf16[4,4,2,16,256]{4,3,2,1,0:T(8,128)(2,1)S(1)}, u32[]{:S(2)}, u32[]{:S(2)}) collective-permute-start(bf16[4,4,2,16,256]{4,3,2,1,0:T(8,128)(2,1)} %get-tuple-element.48), channel_id=1, source_target_pairs={{0,3},{1,0},{2,1},{3,2},{4,7},{5,4},{6,5},{7,6},{8,11},{9,8},{10,9... | collective-permute-start | bytes 786440 | tf_op jit(solution)/shard_map/scatter_grads/ppermute | solution.py:237
  87.9 0.9 slice_dynamic-update-slice_fusion.1
  88.9 0.9 slice_dynamic-update-slice_fusion
  89.8 3.9 %collective-permute-done.14.refs_2_ = bf16[4,4,2,16,256]{4,3,2,1,0:T(8,128)(2,1)S(1)} collective-permute-done((bf16[4,4,2,16,256]{4,3,2,1,0:T(8,128)(2,1)}, bf16[4,4,2,16,256]{4,3,2,1,0:T(8,128)(2,1)S(1)}, u32[]{:S(2)}, u32[]{:S(2)}) %collective-permute-start.14) | collective-permute-done | bytes 262176 | tf_op jit(solution)/shard_map/scatter_grads/ppermute | solution.py:237
  93.8 10.5 %all_to_all.21 = bf16[4,2,4,2,16,256]{5,4,3,2,1,0:T(8,128)(2,1)S(1)} all-to-all(bf16[4,2,4,2,16,256]{5,4,3,2,1,0:T(8,128)(2,1)S(1)} %add_first.3), channel_id=1, replica_groups={{0,4,8,12},{1,5,9,13},{2,6,10,14},{3,7,11,15},{64,65,66,67},{68,69,70,7..., dimensions={0} | all-to-all | bytes 1048576 | tf_op jit(solution)/shard_map/scatter_grads/all_to_all | solution.py:248
  104.4 11.0 %all_to_all.22.got = bf16[8,2,16,256]{3,2,1,0:T(8,128)(2,1)S(1)} all-to-all(bf16[8,2,16,256]{3,2,1,0:T(8,128)(2,1)S(1)} %bitcast.17), channel_id=1, replica_groups=mesh['zl'=2,'core'=2,'zh'=4,'x'=4,'y'=4] {'zl','zh'}, dimensions={0} | all-to-all | bytes 262144 | tf_op jit(solution)/shard_map/scatter_grads/all_to_all | solution.py:308
  (36 shorter events, 3.0 us)
Async XLA Ops:
  0.6 24.3 %copy-start.2 = (f32[1,24,256]{2,1,0:T(8,128)S(1)}, f32[1,24,256]{2,1,0:T(8,128)}, u32[]{:S(2)}) copy-start(f32[1,24,256]{2,1,0:T(8,128)} %param.9) | copy-start | bytes 73732
  0.6 50.6 %collective-permute-start = (bf16[256,3072]{1,0:T(8,128)(2,1)}, bf16[256,3072]{1,0:T(8,128)(2,1)S(1)}, u32[]{:S(2)}, u32[]{:S(2)}) collective-permute-start(bf16[256,3072]{1,0:T(8,128)(2,1)} %bitcast.20), channel_id=1, source_target_pairs={{0,64},{64,0},{1,65},{65,1},{2,66},{66,2},{3,67},{67,3},{4,68},{68... | collective-permute-start | bytes 4718600 | tf_op jit(solution)/shard_map/swap_queries/ppermute | solution.py:259
  0.7 50.5 %collective-permute-start.1 = (bf16[256,3072]{1,0:T(8,128)(2,1)}, bf16[256,3072]{1,0:T(8,128)(2,1)}, u32[]{:S(2)}, u32[]{:S(2)}) collective-permute-start(bf16[256,3072]{1,0:T(8,128)(2,1)} %bitcast.23), channel_id=1, source_target_pairs={{0,64},{64,0},{1,65},{65,1},{2,66},{66,2},{3,67},{67,3},{4,68},{68... | collective-permute-start | bytes 4718600 | tf_op jit(solution)/shard_map/swap_queries/ppermute | solution.py:259
  20.6 13.1 %all-to-all-start.1 = ((bf16[4,4,2,16,640]{4,3,1,2,0:T(8,128)(2,1)}), bf16[4,4,2,16,640]{4,3,1,2,0:T(8,128)(2,1)S(1)}, u32[]{:S(2)}, u32[]{:S(2)}) async-start(bf16[4,4,2,16,640]{4,3,1,2,0:T(8,128)(2,1)} %broadcast_in_dim.6), calls=%async_computation.1 | async-start | bytes 1310720 | tf_op jit(solution)/shard_map/gather_keys/all_to_all | solution.py:248
  24.9 13.9 %collective-permute-start.2 = (f32[24,256]{1,0:T(8,128)S(1)}, f32[24,256]{1,0:T(8,128)S(1)}, u32[]{:S(2)}, u32[]{:S(2)}) collective-permute-start(f32[24,256]{1,0:T(8,128)S(1)} %bitcast.18), channel_id=1, source_target_pairs={{0,64},{64,0},{1,65},{65,1},{2,66},{66,2},{3,67},{67,3},{4,68},{68... | collective-permute-start | bytes 73736 | tf_op jit(solution)/shard_map/swap_queries/ppermute | solution.py:259
  33.8 8.7 %collective-permute-start.6 = (bf16[256,640]{1,0:T(8,128)(2,1)S(1)}, bf16[256,640]{1,0:T(8,128)(2,1)S(1)}, u32[]{:S(2)}, u32[]{:S(2)}) collective-permute-start(bf16[256,640]{1,0:T(8,128)(2,1)S(1)} %bitcast.13), channel_id=1, source_target_pairs={{0,1},{1,2},{2,3},{3,0},{4,5},{5,6},{6,7},{7,4},{8,9},{9,10},{10,1... | collective-permute-start | bytes 983048 | tf_op jit(solution)/shard_map/gather_keys/ppermute | solution.py:237
  35.5 11.9 %collective-permute-start.7 = (bf16[256,640]{1,0:T(8,128)(2,1)S(1)}, bf16[256,640]{1,0:T(8,128)(2,1)S(1)}, u32[]{:S(2)}, u32[]{:S(2)}) collective-permute-start(bf16[256,640]{1,0:T(8,128)(2,1)S(1)} %bitcast.14), channel_id=1, source_target_pairs={{0,2},{1,3},{2,0},{3,1},{4,6},{5,7},{6,4},{7,5},{8,10},{9,11},{10,... | collective-permute-start | bytes 983048 | tf_op jit(solution)/shard_map/gather_keys/ppermute | solution.py:237
  38.8 9.8 %collective-permute-start.8 = (bf16[256,640]{1,0:T(8,128)(2,1)S(1)}, bf16[256,640]{1,0:T(8,128)(2,1)S(1)}, u32[]{:S(2)}, u32[]{:S(2)}) collective-permute-start(bf16[256,640]{1,0:T(8,128)(2,1)S(1)} %bitcast.15), channel_id=1, source_target_pairs={{0,3},{1,0},{2,1},{3,2},{4,7},{5,4},{6,5},{7,6},{8,11},{9,8},{10,9... | collective-permute-start | bytes 983048 | tf_op jit(solution)/shard_map/gather_keys/ppermute | solution.py:237
  42.4 25.6 %collective-permute-start.3 = (bf16[256,640]{1,0:T(8,128)(2,1)S(1)}, bf16[256,640]{1,0:T(8,128)(2,1)S(1)}, u32[]{:S(2)}, u32[]{:S(2)}) collective-permute-start(bf16[256,640]{1,0:T(8,128)(2,1)S(1)} %bitcast.9), channel_id=1, source_target_pairs={{0,1},{1,2},{2,3},{3,0},{4,5},{5,6},{6,7},{7,4},{8,9},{9,10},{10,1... | collective-permute-start | bytes 983048 | tf_op jit(solution)/shard_map/gather_keys/ppermute | solution.py:237
  47.4 20.7 %collective-permute-start.4 = (bf16[256,640]{1,0:T(8,128)(2,1)S(1)}, bf16[256,640]{1,0:T(8,128)(2,1)S(1)}, u32[]{:S(2)}, u32[]{:S(2)}) collective-permute-start(bf16[256,640]{1,0:T(8,128)(2,1)S(1)} %bitcast.10), channel_id=1, source_target_pairs={{0,2},{1,3},{2,0},{3,1},{4,6},{5,7},{6,4},{7,5},{8,10},{9,11},{10,... | collective-permute-start | bytes 983048 | tf_op jit(solution)/shard_map/gather_keys/ppermute | solution.py:237
  48.7 19.5 %collective-permute-start.5 = (bf16[256,640]{1,0:T(8,128)(2,1)S(1)}, bf16[256,640]{1,0:T(8,128)(2,1)S(1)}, u32[]{:S(2)}, u32[]{:S(2)}) collective-permute-start(bf16[256,640]{1,0:T(8,128)(2,1)S(1)} %bitcast.11), channel_id=1, source_target_pairs={{0,3},{1,0},{2,1},{3,2},{4,7},{5,4},{6,5},{7,6},{8,11},{9,8},{10,9... | collective-permute-start | bytes 983048 | tf_op jit(solution)/shard_map/gather_keys/ppermute | solution.py:237
  51.3 1.2 %copy-start.3 = (bf16[256,3072]{1,0:T(8,128)(2,1)}, bf16[256,3072]{1,0:T(8,128)(2,1)S(1)}, u32[]{:S(2)}) copy-start(bf16[256,3072]{1,0:T(8,128)(2,1)S(1)} %collective-permute-done.q_oth) | copy-start | bytes 4718596
  65.7 15.8 %collective-permute-start.10 = (bf16[4,4,2,16,256]{4,3,2,1,0:T(8,128)(2,1)}, bf16[4,4,2,16,256]{4,3,2,1,0:T(8,128)(2,1)S(1)}, u32[]{:S(2)}, u32[]{:S(2)}) collective-permute-start(bf16[4,4,2,16,256]{4,3,2,1,0:T(8,128)(2,1)} %get-tuple-element.39), channel_id=1, source_target_pairs={{0,2},{1,3},{2,0},{3,1},{4,6},{5,7},{6,4},{7,5},{8,10},{9,11},{10,... | collective-permute-start | bytes 786440 | tf_op jit(solution)/shard_map/scatter_grads/ppermute | solution.py:237
  66.0 15.5 %collective-permute-start.11 = (bf16[4,4,2,16,256]{4,3,2,1,0:T(8,128)(2,1)}, bf16[4,4,2,16,256]{4,3,2,1,0:T(8,128)(2,1)S(1)}, u32[]{:S(2)}, u32[]{:S(2)}) collective-permute-start(bf16[4,4,2,16,256]{4,3,2,1,0:T(8,128)(2,1)} %get-tuple-element.40), channel_id=1, source_target_pairs={{0,3},{1,0},{2,1},{3,2},{4,7},{5,4},{6,5},{7,6},{8,11},{9,8},{10,9... | collective-permute-start | bytes 786440 | tf_op jit(solution)/shard_map/scatter_grads/ppermute | solution.py:237
  68.1 13.4 %collective-permute-start.9 = (bf16[4,4,2,16,256]{4,3,2,1,0:T(8,128)(2,1)}, bf16[4,4,2,16,256]{4,3,2,1,0:T(8,128)(2,1)S(1)}, u32[]{:S(2)}, u32[]{:S(2)}) collective-permute-start(bf16[4,4,2,16,256]{4,3,2,1,0:T(8,128)(2,1)} %get-tuple-element.38), channel_id=1, source_target_pairs={{0,1},{1,2},{2,3},{3,0},{4,5},{5,6},{6,7},{7,4},{8,9},{9,10},{10,1... | collective-permute-start | bytes 786440 | tf_op jit(solution)/shard_map/scatter_grads/ppermute | solution.py:237
  68.1 19.7 %copy-start = (f32[4,4,2,16,256]{4,3,2,1,0:T(8,128)S(1)}, f32[4,4,2,16,256]{4,3,2,1,0:T(8,128)}, u32[]{:S(2)}) copy-start(f32[4,4,2,16,256]{4,3,2,1,0:T(8,128)} %get-tuple-element.49.refs_0_) | copy-start | bytes 1572868
  81.5 6.4 %collective-permute-start.13 = (f32[256,1536]{1,0:T(8,128)}, f32[256,1536]{1,0:T(8,128)S(1)}, u32[]{:S(2)}, u32[]{:S(2)}) collective-permute-start(f32[256,1536]{1,0:T(8,128)} %get-tuple-element.43), channel_id=1, source_target_pairs={{0,64},{64,0},{1,65},{65,1},{2,66},{66,2},{3,67},{67,3},{4,68},{68... | collective-permute-start | bytes 4718600 | tf_op jit(solution)/shard_map/swap_query_grads/ppermute | solution.py:259
  81.6 8.2 %collective-permute-start.12 = (bf16[4,4,2,16,256]{4,3,2,1,0:T(8,128)(2,1)}, bf16[4,4,2,16,256]{4,3,2,1,0:T(8,128)(2,1)S(1)}, u32[]{:S(2)}, u32[]{:S(2)}) collective-permute-start(bf16[4,4,2,16,256]{4,3,2,1,0:T(8,128)(2,1)} %get-tuple-element.41), channel_id=1, source_target_pairs={{0,1},{1,2},{2,3},{3,0},{4,5},{5,6},{6,7},{7,4},{8,9},{9,10},{10,1... | collective-permute-start | bytes 786440 | tf_op jit(solution)/shard_map/scatter_grads/ppermute | solution.py:237
  83.1 10.6 %collective-permute-start.14 = (bf16[4,4,2,16,256]{4,3,2,1,0:T(8,128)(2,1)}, bf16[4,4,2,16,256]{4,3,2,1,0:T(8,128)(2,1)S(1)}, u32[]{:S(2)}, u32[]{:S(2)}) collective-permute-start(bf16[4,4,2,16,256]{4,3,2,1,0:T(8,128)(2,1)} %get-tuple-element.47), channel_id=1, source_target_pairs={{0,2},{1,3},{2,0},{3,1},{4,6},{5,7},{6,4},{7,5},{8,10},{9,11},{10,... | collective-permute-start | bytes 786440 | tf_op jit(solution)/shard_map/scatter_grads/ppermute | solution.py:237
  86.4 7.4 %collective-permute-start.15 = (bf16[4,4,2,16,256]{4,3,2,1,0:T(8,128)(2,1)}, bf16[4,4,2,16,256]{4,3,2,1,0:T(8,128)(2,1)S(1)}, u32[]{:S(2)}, u32[]{:S(2)}) collective-permute-start(bf16[4,4,2,16,256]{4,3,2,1,0:T(8,128)(2,1)} %get-tuple-element.48), channel_id=1, source_target_pairs={{0,3},{1,0},{2,1},{3,2},{4,7},{5,4},{6,5},{7,6},{8,11},{9,8},{10,9... | collective-permute-start | bytes 786440 | tf_op jit(solution)/shard_map/scatter_grads/ppermute | solution.py:237
  87.9 5.8 %copy-start.1 = (f32[4,4,2,16,256]{4,3,2,1,0:T(8,128)S(1)}, f32[4,4,2,16,256]{4,3,2,1,0:T(8,128)}, u32[]{:S(2)}) copy-start(f32[4,4,2,16,256]{4,3,2,1,0:T(8,128)} %get-tuple-element.45.refs_0_) | copy-start | bytes 1572868

commit v4 on v3

v4 whole, which is shorter than its diff:
```python
import jax
import jax.numpy as jnp
from jax import lax
from jax.experimental import pallas as pl
from jax.experimental.pallas import tpu as pltpu
from jax.sharding import Mesh
from jax.sharding import PartitionSpec as P

KV_HEADS = 8
GROUP = 3
HEAD_DIM = 128
ROWS = 256
SLAB = 16
SCALE = HEAD_DIM**-0.5
LOG2E = 1.4426950408889634
WIDE = GROUP * ROWS
PAIR = 2
COLS = PAIR * HEAD_DIM
PAYLOAD = 2 * COLS + 128
BLOCK = 256
APART = (0, 2, 1, 3)
AXES = ("zl", "core", "zh", "x", "y")


SMALL = pltpu.CompilerParams(vmem_limit_bytes=8 * 2**20)


def matmul(left, right, contract):
    return lax.dot_general(
        left, right, ((contract[:1], contract[1:]), ((), ())), preferred_element_type=jnp.float32
    )


def attention_kernel(
    meta, q_own, g_own, lse_own, q_oth, g_oth, lse_oth, kv0, kv1, kv2, kv3, *rest
):
    (
        dq_own, dq_oth, out0, out1, out2, out3,
        pos_s, key_s, val_s, rows_q, rows_g, prob_s, gp_s, half_s, ds_s,
    ) = rest[-15:]
    step = pl.program_id(0)
    core, a0, first = (meta[i] for i in range(3))
    pieces = (kv0, kv1, kv2, kv3)
    outs = (out0, out1, out2, out3)

    @pl.when(step == 0)
    def _():
        a_step = jnp.where(core == 0, 1, 4)
        b_step = jnp.where(core == 0, 4, 1)
        row = lax.broadcasted_iota(jnp.int32, (BLOCK, 128), 0)
        base = (((row >> 4) & 3) * 16 + (row >> 6) * b_step) * 256 + (row & 15)
        for a, piece in enumerate(pieces):
            slab = (a0 ^ APART[a]) * a_step
            pos_s[a] = piece[:, 2 * COLS:].astype(jnp.float32) + (base + slab * 256).astype(jnp.float32)
            for h in range(PAIR):
                key_s[h, a] = piece[:, h * 128:(h + 1) * 128]
                val_s[h, a] = piece[:, COLS + h * 128:COLS + (h + 1) * 128]

    lane = lax.broadcasted_iota(jnp.int32, (1, 128), 1)
    q_pos = [(first + lane + c * 128).astype(jnp.float32) for c in range(2)]
    sides = ((q_own, g_own, lse_own, dq_own), (q_oth, g_oth, lse_oth, dq_oth))

    for layer, (q_ref, g_ref, _, _) in enumerate(sides):
        for h in range(GROUP):
            rows = slice(layer * WIDE + h * ROWS, layer * WIDE + (h + 1) * ROWS)
            rows_q[rows, :] = q_ref[:, h * 128:(h + 1) * 128]
            rows_g[rows, :] = g_ref[:, h * 128:(h + 1) * 128]

    for layer, (_, _, lse_ref, _) in enumerate(sides):
        rows = slice(layer * WIDE, (layer + 1) * WIDE)
        lse = lse_ref[0] * LOG2E
        delta = jnp.zeros((1, WIDE), jnp.float32)
        for a in range(4):
            score = matmul(key_s[step, a], rows_q[rows, :], (1, 1))
            prob = jnp.exp2(score * (SCALE * LOG2E) - lse)
            seen = jnp.concatenate([pos_s[a] <= q_pos[0], pos_s[a] <= q_pos[1]] * GROUP, axis=1)
            prob = jnp.where(seen, prob, 0.0)
            grad_prob = matmul(val_s[step, a], rows_g[rows, :], (1, 1))
            delta = delta + jnp.sum(prob * grad_prob, axis=0, keepdims=True)
            prob_s[layer, a] = prob
            gp_s[layer, a] = grad_prob
            half_s[a, :, rows] = prob.astype(jnp.bfloat16)
        for a in range(4):
            ds_s[a, :, rows] = (prob_s[layer, a] * (gp_s[layer, a] - delta)).astype(jnp.bfloat16)

    for a, out in enumerate(outs):
        dv = matmul(half_s[a], rows_g[...], (1, 0))
        dk = matmul(ds_s[a], rows_q[...], (1, 0)) * SCALE
        out[:, :, 0] = dk.astype(out.dtype).reshape(4, 4, SLAB, HEAD_DIM)
        out[:, :, 1] = dv.astype(out.dtype).reshape(4, 4, SLAB, HEAD_DIM)

    for layer, (_, _, _, dq_ref) in enumerate(sides):
        rows = slice(layer * WIDE, (layer + 1) * WIDE)
        dq_t = matmul(key_s[step, 0], ds_s[0, :, rows], (0, 0))
        for a in range(1, 4):
            dq_t = dq_t + matmul(key_s[step, a], ds_s[a, :, rows], (0, 0))
        dq_t = dq_t * SCALE
        for h in range(GROUP):
            dq_ref[:, h * 128:(h + 1) * 128] = dq_t[:, h * ROWS:(h + 1) * ROWS].T


def attention(chunk, meta, q_own, g_own, lse_own, q_oth, g_oth, lse_oth, kv, partly):
    def head(g, m):
        return chunk * 4 + m[0] * 2 + g

    q_own, g_own = (pltpu.with_memory_space_constraint(v, pltpu.HBM) for v in (q_own, g_own))
    f32, bf16 = jnp.float32, jnp.bfloat16
    width = GROUP * HEAD_DIM
    own = pl.BlockSpec((ROWS, width), lambda g, m: (0, head(g, m)))
    back = pl.BlockSpec((ROWS, width), lambda g, m: (0, chunk * 2 + g))
    part = pl.BlockSpec((BLOCK, PAYLOAD), lambda g, m: (0, 0))
    lse = pl.BlockSpec((1, 1, WIDE), lambda g, m: (head(g, m), 0, 0))
    out_dims = (4, 4, 2, SLAB, PAIR * HEAD_DIM)
    out = pl.BlockSpec((4, 4, 2, SLAB, HEAD_DIM), lambda g, m: (0, 0, 0, 0, g))
    return pl.pallas_call(
        attention_kernel,
        grid_spec=pltpu.PrefetchScalarGridSpec(
            num_scalar_prefetch=1,
            grid=(PAIR,),
            in_specs=[own, own, lse, own, own, lse, part, part, part, part]
            + [pl.BlockSpec(memory_space=pl.ANY)] * len(partly),
            out_specs=[own, back, out, out, out, out],
            scratch_shapes=[
                pltpu.VMEM((4, BLOCK, 128), f32),
                pltpu.VMEM((PAIR, 4, BLOCK, HEAD_DIM), bf16),
                pltpu.VMEM((PAIR, 4, BLOCK, HEAD_DIM), bf16),
                pltpu.VMEM((2 * WIDE, HEAD_DIM), bf16),
                pltpu.VMEM((2 * WIDE, HEAD_DIM), bf16),
                pltpu.VMEM((2, 4, BLOCK, WIDE), f32),
                pltpu.VMEM((2, 4, BLOCK, WIDE), f32),
                pltpu.VMEM((4, BLOCK, 2 * WIDE), bf16),
                pltpu.VMEM((4, BLOCK, 2 * WIDE), bf16),
            ],
        ),
        out_shape=[
            pltpu.HBM((ROWS, KV_HEADS * width), f32),
            pltpu.HBM((ROWS, KV_HEADS // 2 * width), f32),
            pltpu.HBM(out_dims, f32),
        ] + [pltpu.HBM(out_dims, bf16)] * 3,
        input_output_aliases={11 + n: n for n in range(len(partly))},
        compiler_params=pltpu.CompilerParams(vmem_limit_bytes=36 * 2**20),
        cost_estimate=pl.CostEstimate(
            flops=8 * 10**9, bytes_accessed=8 * 2**20, transcendentals=3 * 10**6
        ),
        name="attention_backward",
    )(meta, q_own, g_own, lse_own, q_oth, g_oth, lse_oth, *kv, *partly)


VMEM = pl.BlockSpec(memory_space=pltpu.VMEM)


def pack_kernel(starts, keys, values, out):
    core, zh, x, y = (lax.axis_index(n) for n in ("core", "zh", "x", "y"))
    offset = starts[0] - (zh * 16 + x * 4 + y) * 256
    tail = jnp.full((SLAB, 128), offset, jnp.int32).astype(jnp.float32).astype(jnp.bfloat16)
    for chunk in range(2):
        cols = pl.ds(pl.multiple_of(chunk * 512 + core * COLS, 128), COLS)
        out[chunk, :, :COLS] = keys[:, cols]
        out[chunk, :, COLS:2 * COLS] = values[:, cols]
        out[chunk, :, 2 * COLS:] = tail


def pack(starts, keys, values):
    keys, values = (pltpu.with_memory_space_constraint(v, pltpu.HBM) for v in (keys, values))
    return pl.pallas_call(
        pack_kernel,
        in_specs=[pl.BlockSpec(memory_space=pltpu.SMEM), VMEM, VMEM],
        out_specs=VMEM,
        out_shape=jax.ShapeDtypeStruct((2, SLAB, PAYLOAD), jnp.bfloat16),
        compiler_params=SMALL,
        name="pack_keys_values",
    )(starts, keys, values)


def line_kernel(own, far, near, next_, out):
    zl, zh = lax.axis_index("zl"), lax.axis_index("zh")
    step = jnp.where(zl == 0, -1, 1)
    for by, block in ((0, own), (2, far), (step, near), (-step, next_)):
        out[:, (zh + by) & 3] = block[...]


def line(blocks):
    return pl.pallas_call(
        line_kernel,
        in_specs=[VMEM] * 4,
        out_specs=VMEM,
        out_shape=jax.ShapeDtypeStruct((2, 4, SLAB, PAYLOAD), jnp.bfloat16),
        compiler_params=SMALL,
        name="join_line",
    )(*blocks)


def plane_place():
    core, x, y = (lax.axis_index(n) for n in ("core", "x", "y"))
    return jnp.where(core == 0, x, y)


def pieces_kernel(*refs):
    b0 = plane_place()
    for r, block in enumerate(refs[:4]):
        for chunk, out in enumerate(refs[4:]):
            out[b0 ^ APART[r]] = block[chunk]


def pieces_of(blocks):
    shape = jax.ShapeDtypeStruct((4, 4, SLAB, PAYLOAD), jnp.bfloat16)
    return pl.pallas_call(
        pieces_kernel,
        in_specs=[VMEM] * 4,
        out_specs=[VMEM, VMEM],
        out_shape=[shape, shape],
        compiler_params=SMALL,
        name="join_pieces",
    )(*blocks)


def share_kernel(*refs):
    b0 = plane_place()
    for r, out in enumerate(refs[-4:]):
        total = refs[0][b0 ^ APART[r]]
        for ref in refs[1:4]:
            total = total + ref[b0 ^ APART[r]].astype(jnp.float32)
        out[0] = total.astype(out.dtype)


def share(chunk, terms, partly):
    dims = terms[0].shape
    whole = pl.BlockSpec(dims, lambda i: (0,) * 5)
    out_dims = (2, *dims[1:])
    return pl.pallas_call(
        share_kernel,
        grid=(1,),
        in_specs=[whole] * 4 + [pl.BlockSpec(memory_space=pl.ANY)] * len(partly),
        out_specs=[pl.BlockSpec((1, *dims[1:]), lambda i: (chunk, 0, 0, 0, 0))] * 4,
        out_shape=[jax.ShapeDtypeStruct(out_dims, jnp.float32)]
        + [jax.ShapeDtypeStruct(out_dims, jnp.bfloat16)] * 3,
        input_output_aliases={4 + n: n for n in range(len(partly))},
        compiler_params=SMALL,
        name="add_first",
    )(*terms, *partly)


def finish_kernel(got, dk, dv):
    for n, out in enumerate((dk, dv)):
        total = got[0, n].astype(jnp.float32)
        for i in range(1, 8):
            total = total + got[i, n].astype(jnp.float32)
        out[...] = total


def finish(got):
    shape = jax.ShapeDtypeStruct((SLAB, 2 * HEAD_DIM), jnp.float32)
    return pl.pallas_call(finish_kernel, out_shape=[shape, shape], compiler_params=SMALL, name="add_last")(got)


def plane_swap(value, by, x_core):
    pairs = []
    for core in range(2):
        for x in range(4):
            for y in range(4):
                to = (x ^ by, y) if core == x_core else (x, y ^ by)
                pairs.append((core * 16 + x * 4 + y, core * 16 + to[0] * 4 + to[1]))
    return lax.ppermute(value, ("core", "x", "y"), pairs)


def plane_swaps(values, x_core):
    return [plane_swap(value, by, x_core) for value, by in zip(values, APART[1:])]


def z_shift(value, by):
    pairs = []
    for z in range(8):
        up = z % 2 == 1
        to = (z + (by if up else -by)) % 8
        pairs.append((z % 2 * 4 + z // 2, to % 2 * 4 + to // 2))
    return lax.ppermute(value, ("zl", "zh"), pairs)


def add(terms):
    total = terms[0].astype(jnp.float32)
    for term in terms[1:]:
        total = total + term.astype(jnp.float32)
    return total.astype(jnp.bfloat16)


def swap(value):
    return lax.ppermute(value, "core", [(0, 1), (1, 0)])


def per_device(
    queries, out_grads, logsumexp, shared_keys, shared_values, query_starts, slab_starts
):
    core, x, y = (lax.axis_index(n) for n in ("core", "x", "y"))
    other = 1 - core
    queries, out_grads, lse = queries[0], out_grads[0], logsumexp[0]

    with jax.named_scope("gather_keys"):
        payload = pack(slab_starts, shared_keys, shared_values)
        block = line([payload] + [z_shift(payload, by) for by in (3, 1, 2)])
        own = pieces_of([block] + plane_swaps([block] * 3, 0))
        pieces = []
        for piece in own:
            piece = piece.reshape(BLOCK, PAYLOAD)
            pieces.append([piece] + plane_swaps([piece] * 3, 1))
    with jax.named_scope("swap_queries"):
        q_oth, g_oth, lse_oth = (swap(v) for v in (queries, out_grads, lse))

    a0 = jnp.where(core == 0, y, x)
    meta = jnp.stack([core, a0, query_starts[0]]).astype(jnp.int32)
    wide = (KV_HEADS, 1, WIDE)
    lse, lse_oth = lse.reshape(wide), lse_oth.reshape(wide)
    partly, sums = [], []
    for chunk in range(2):
        *partly, part0, part1, part2, part3 = attention(
            chunk, meta, queries, out_grads, lse, q_oth, g_oth, lse_oth, pieces[chunk], partly
        )
        with jax.named_scope("scatter_grads"):
            if sums:
                part0, part1, part2, part3, partly, sums = lax.optimization_barrier(
                    (part0, part1, part2, part3, partly, sums)
                )
            sums.append([part0, *plane_swaps([part1, part2, part3], 1)])

    dq, dq_oth = partly
    with jax.named_scope("scatter_grads"):
        mine, *shares = share(1, sums[1], share(0, sums[0], []))
        shares = plane_swaps(shares, 0)
    with jax.named_scope("swap_query_grads"):
        dq_oth, _ = lax.optimization_barrier((dq_oth, mine))
        back = swap(dq_oth)
        dq = lax.dynamic_update_slice(dq, back[:, :768], (0, other * 768))
        dq = lax.dynamic_update_slice(dq, back[:, 768:], (0, (2 + other) * 768))
    with jax.named_scope("scatter_grads"):
        shares[0], dq = lax.optimization_barrier((shares[0], dq))
        small = add([mine, *shares]).reshape(8, 2, SLAB, 2 * HEAD_DIM)
        dk, dv = finish(lax.all_to_all(small, ("zl", "zh"), 0, 0))
    return dq[None], dk, dv


def solution(mesh):
    fine = Mesh(mesh.devices.reshape(2, 2, 4, 4, 4), AXES)
    section, seq = ("zl", "core"), ("zh", "x", "y")
    return jax.shard_map(
        per_device,
        mesh=fine,
        in_specs=(
            P(section, seq, None),
            P(section, seq, None),
            P(section, None, seq),
            P(seq, None),
            P(seq, None),
            P(seq),
            P(seq),
        ),
        out_specs=(P(section, seq, None), P(seq, section), P(seq, section)),
        check_vma=False,
    )
```

time: 117 us -> 106 us (0.906)
  blocking collectives: 38.5 us -> 12.1 us
  waiting for transfers between devices: 15 us -> 25.9 us
  starting transfers between devices: 28 us -> 34.2 us
  local copies, waits for them, and re-layouts: 4.06 us -> 2.66 us
    all_to_all x2 -> x0, blocking collectives: 27.5 us -> none  [the longest x1 17 us: per_device(): block = lax.all_to_all(payload, 'zh', 0, 0)]
    ppermute x12 -> x21, waiting for transfers between devices: 6.19 us -> 25.9 us  [the longest x18 20.3 us: plane_swap(): return lax.ppermute(value, ('core', 'x', 'y'), pairs)]
    ppermute x12 -> x21, starting transfers between devices: 23 us -> 33.5 us  [the longest x18 26.1 us: plane_swap(): return lax.ppermute(value, ('core', 'x', 'y'), pairs)]
    all_to_all x1 -> x0, waiting for transfers between devices: 8.78 us -> none  [plane_exchange(): lax.all_to_all(value, ('core', 'x', 'y'), 0, 0, axis_index_groups=groups)]
    all_to_all x1 -> x0, starting transfers between devices: 4.29 us -> none  [plane_exchange(): lax.all_to_all(value, ('core', 'x', 'y'), 0, 0, axis_index_groups=groups)]
  transfers between devices with their start and end apart: 17 -> 25, of which waited for: 4 -> 13; matrix products, arithmetic and copies ran while one was open for 3% -> 3% of each run, Pallas kernels for 24% -> 27%
where the time goes in v4:
time: 106 us
  starting transfers between devices  34.2 us (32%)
  Pallas kernels  28.8 us (27%)
  waiting for transfers between devices  25.9 us (24%)
  blocking collectives  12.1 us (11%)
  local copies, waits for them, and re-layouts  2.66 us (3%)
  between operations  2.06 us (2%)
    pallas_call x2, Pallas kernels, attention(): pl.pallas_call(attention_kernel, grid_spec=pltpu.PrefetchScalarGridSpec(n...  26.4 us
    ppermute x18, starting transfers between devices, plane_swap(): return lax.ppermute(value, ('core', 'x', 'y'), pairs)  26.1 us
    ppermute x18, waiting for transfers between devices, plane_swap(): return lax.ppermute(value, ('core', 'x', 'y'), pairs)  20.3 us
    all_to_all x1, blocking collectives, per_device(): dk, dv = finish(lax.all_to_all(small, ('zl', 'zh'), 0, 0))  12.1 us
    ppermute x3, starting transfers between devices, z_shift(): return lax.ppermute(value, ('zl', 'zh'), pairs)  7.4 us
    ppermute x3, waiting for transfers between devices, z_shift(): return lax.ppermute(value, ('zl', 'zh'), pairs)  5.66 us
  transfers between devices with their start and end apart: 25, of which 13 were waited for; matrix products, arithmetic and copies ran while one was open for 3% of the time, Pallas kernels for 27%

profile of v4, /device:TPU:32, one launch (start us, length us, event | category | flops | bytes accessed | tf_op | source)
XLA Modules:
  0.0 105.9 jit_solution(9958352963121253194)
XLA Ops:
  2.7 5.9 %collective-permute-start.3 = (bf16[2,16,640]{2,1,0:T(8,128)(2,1)S(1)}, bf16[2,16,640]{2,1,0:T(8,128)(2,1)S(1)}, u32[]{:S(2)}, u32[]{:S(2)}) collective-permute-start(bf16[2,16,640]{2,1,0:T(8,128)(2,1)S(1)} %pack_keys_values.1.own), channel_id=1, source_target_pairs={{0,160},{128,32},{16,176},{144,48},{32,128},{160,0},{48,144},{176,... | collective-permute-start | bytes 122888 | tf_op jit(solution)/shard_map/gather_keys/ppermute | solution.py:276
  10.6 2.2 %collective-permute-done.4.near = bf16[2,16,640]{2,1,0:T(8,128)(2,1)S(1)} collective-permute-done((bf16[2,16,640]{2,1,0:T(8,128)(2,1)S(1)}, bf16[2,16,640]{2,1,0:T(8,128)(2,1)S(1)}, u32[]{:S(2)}, u32[]{:S(2)}) %collective-permute-start.4) | collective-permute-done | bytes 40992 | tf_op jit(solution)/shard_map/gather_keys/ppermute | solution.py:276
  12.8 3.0 %collective-permute-done.5.next_ = bf16[2,16,640]{2,1,0:T(8,128)(2,1)S(1)} collective-permute-done((bf16[2,16,640]{2,1,0:T(8,128)(2,1)S(1)}, bf16[2,16,640]{2,1,0:T(8,128)(2,1)S(1)}, u32[]{:S(2)}, u32[]{:S(2)}) %collective-permute-start.5) | collective-permute-done | bytes 40992 | tf_op jit(solution)/shard_map/gather_keys/ppermute | solution.py:276
  15.8 3.1 %collective-permute-start.6 = (bf16[2,4,16,640]{3,2,1,0:T(8,128)(2,1)S(1)}, bf16[2,4,16,640]{3,2,1,0:T(8,128)(2,1)S(1)}, u32[]{:S(2)}, u32[]{:S(2)}) collective-permute-start(bf16[2,4,16,640]{3,2,1,0:T(8,128)(2,1)S(1)} %join_line.1.refs_0_), channel_id=1, source_target_pairs={{0,8},{1,9},{2,10},{3,11},{4,12},{5,13},{6,14},{7,15},{8,0},{9,1},... | collective-permute-start | bytes 491528 | tf_op jit(solution)/shard_map/gather_keys/ppermute | solution.py:263
  20.0 2.7 %collective-permute-done.6.refs_1_ = bf16[2,4,16,640]{3,2,1,0:T(8,128)(2,1)S(1)} collective-permute-done((bf16[2,4,16,640]{3,2,1,0:T(8,128)(2,1)S(1)}, bf16[2,4,16,640]{3,2,1,0:T(8,128)(2,1)S(1)}, u32[]{:S(2)}, u32[]{:S(2)}) %collective-permute-start.6) | collective-permute-done | bytes 163872 | tf_op jit(solution)/shard_map/gather_keys/ppermute | solution.py:263
  22.7 1.8 %collective-permute-done.7.refs_2_ = bf16[2,4,16,640]{3,2,1,0:T(8,128)(2,1)S(1)} collective-permute-done((bf16[2,4,16,640]{3,2,1,0:T(8,128)(2,1)S(1)}, bf16[2,4,16,640]{3,2,1,0:T(8,128)(2,1)S(1)}, u32[]{:S(2)}, u32[]{:S(2)}) %collective-permute-start.7) | collective-permute-done | bytes 163872 | tf_op jit(solution)/shard_map/gather_keys/ppermute | solution.py:263
  24.5 1.5 %collective-permute-done.8.refs_3_ = bf16[2,4,16,640]{3,2,1,0:T(8,128)(2,1)S(1)} collective-permute-done((bf16[2,4,16,640]{3,2,1,0:T(8,128)(2,1)S(1)}, bf16[2,4,16,640]{3,2,1,0:T(8,128)(2,1)S(1)}, u32[]{:S(2)}, u32[]{:S(2)}) %collective-permute-start.8) | collective-permute-done | bytes 163872 | tf_op jit(solution)/shard_map/gather_keys/ppermute | solution.py:263
  26.8 3.2 %collective-permute-start.12 = (bf16[256,640]{1,0:T(8,128)(2,1)}, bf16[256,640]{1,0:T(8,128)(2,1)}, u32[]{:S(2)}, u32[]{:S(2)}) collective-permute-start(bf16[256,640]{1,0:T(8,128)(2,1)} %bitcast.6.kv0), channel_id=1, source_target_pairs={{0,2},{1,3},{2,0},{3,1},{4,6},{5,7},{6,4},{7,5},{8,10},{9,11},{10,... | collective-permute-start | bytes 983048 | tf_op jit(solution)/shard_map/gather_keys/ppermute | solution.py:263
  32.6 3.1 %collective-permute-done.12.kv1 = bf16[256,640]{1,0:T(8,128)(2,1)} collective-permute-done((bf16[256,640]{1,0:T(8,128)(2,1)}, bf16[256,640]{1,0:T(8,128)(2,1)}, u32[]{:S(2)}, u32[]{:S(2)}) %collective-permute-start.12) | collective-permute-done | bytes 327712 | tf_op jit(solution)/shard_map/gather_keys/ppermute | solution.py:263
  35.7 1.7 %collective-permute-start.10 = (bf16[256,640]{1,0:T(8,128)(2,1)S(1)}, bf16[256,640]{1,0:T(8,128)(2,1)S(1)}, u32[]{:S(2)}, u32[]{:S(2)}) collective-permute-start(bf16[256,640]{1,0:T(8,128)(2,1)S(1)} %bitcast.9), channel_id=1, source_target_pairs={{0,1},{1,0},{2,3},{3,2},{4,5},{5,4},{6,7},{7,6},{8,9},{9,8},{10,11... | collective-permute-start | bytes 983048 | tf_op jit(solution)/shard_map/gather_keys/ppermute | solution.py:263
  37.4 2.2 %collective-permute-done.13.kv2 = bf16[256,640]{1,0:T(8,128)(2,1)} collective-permute-done((bf16[256,640]{1,0:T(8,128)(2,1)}, bf16[256,640]{1,0:T(8,128)(2,1)}, u32[]{:S(2)}, u32[]{:S(2)}) %collective-permute-start.13) | collective-permute-done | bytes 327712 | tf_op jit(solution)/shard_map/gather_keys/ppermute | solution.py:263
  39.8 3.2 %collective-permute-start.9 = (bf16[256,640]{1,0:T(8,128)(2,1)S(1)}, bf16[256,640]{1,0:T(8,128)(2,1)S(1)}, u32[]{:S(2)}, u32[]{:S(2)}) collective-permute-start(bf16[256,640]{1,0:T(8,128)(2,1)S(1)} %bitcast.11), channel_id=1, source_target_pairs={{0,2},{1,3},{2,0},{3,1},{4,6},{5,7},{6,4},{7,5},{8,10},{9,11},{10,... | collective-permute-start | bytes 983048 | tf_op jit(solution)/shard_map/gather_keys/ppermute | solution.py:263
  43.0 13.4 %attention_backward.2 = (f32[256,3072]{1,0:T(8,128)}, f32[256,1536]{1,0:T(8,128)}, f32[4,4,2,16,256]{4,3,2,1,0:T(8,128)}, bf16[4,4,2,16,256]{4,3,2,1,0:T(8,128)(...) custom-call(s32[3]{0:T(128)S(1)} %pad_add_fusion.meta, bf16[256,3072]{1,0:T(8,128)(2,1)} %bitcast.17, ...), custom_call_target="tpu_custom_call" | custom-call | flops 8000000000 | bytes 8388608 | tf_op jit(solution)/shard_map/attention_backward/pallas_call | solution.py:115
  56.8 1.6 %collective-permute-start.16 = (bf16[4,4,2,16,256]{4,3,2,1,0:T(8,128)(2,1)}, bf16[4,4,2,16,256]{4,3,2,1,0:T(8,128)(2,1)S(1)}, u32[]{:S(2)}, u32[]{:S(2)}) collective-permute-start(bf16[4,4,2,16,256]{4,3,2,1,0:T(8,128)(2,1)} %get-tuple-element.52), channel_id=1, source_target_pairs={{0,1},{1,0},{2,3},{3,2},{4,5},{5,4},{6,7},{7,6},{8,9},{9,8},{10,11... | collective-permute-start | bytes 786440 | tf_op jit(solution)/shard_map/scatter_grads/ppermute | solution.py:263
  58.4 2.2 %collective-permute-start.17 = (bf16[4,4,2,16,256]{4,3,2,1,0:T(8,128)(2,1)}, bf16[4,4,2,16,256]{4,3,2,1,0:T(8,128)(2,1)S(1)}, u32[]{:S(2)}, u32[]{:S(2)}) collective-permute-start(bf16[4,4,2,16,256]{4,3,2,1,0:T(8,128)(2,1)} %get-tuple-element.53), channel_id=1, source_target_pairs={{0,3},{1,2},{2,1},{3,0},{4,7},{5,6},{6,5},{7,4},{8,11},{9,10},{10,... | collective-permute-start | bytes 786440 | tf_op jit(solution)/shard_map/scatter_grads/ppermute | solution.py:263
  60.6 12.9 %attention_backward.3 = (f32[256,3072]{1,0:T(8,128)}, f32[256,1536]{1,0:T(8,128)}, f32[4,4,2,16,256]{4,3,2,1,0:T(8,128)}, bf16[4,4,2,16,256]{4,3,2,1,0:T(8,128)(...) custom-call(s32[3]{0:T(128)S(1)} %pad_add_fusion.meta, ...), custom_call_target="tpu_custom_call", output_to_operand_aliasing={{0}: (11, {}), {1}: (12, {})} | custom-call | flops 8000000000 | bytes 8388608 | tf_op jit(solution)/shard_map/attention_backward/pallas_call | solution.py:115
  74.4 1.1 %collective-permute-start.19 = (bf16[4,4,2,16,256]{4,3,2,1,0:T(8,128)(2,1)}, bf16[4,4,2,16,256]{4,3,2,1,0:T(8,128)(2,1)S(1)}, u32[]{:S(2)}, u32[]{:S(2)}) collective-permute-start(bf16[4,4,2,16,256]{4,3,2,1,0:T(8,128)(2,1)} %get-tuple-element.56), channel_id=1, source_target_pairs={{0,1},{1,0},{2,3},{3,2},{4,5},{5,4},{6,7},{7,6},{8,9},{9,8},{10,11... | collective-permute-start | bytes 786440 | tf_op jit(solution)/shard_map/scatter_grads/ppermute | solution.py:263
  75.6 2.2 %collective-permute-start.20 = (bf16[4,4,2,16,256]{4,3,2,1,0:T(8,128)(2,1)}, bf16[4,4,2,16,256]{4,3,2,1,0:T(8,128)(2,1)S(1)}, u32[]{:S(2)}, u32[]{:S(2)}) collective-permute-start(bf16[4,4,2,16,256]{4,3,2,1,0:T(8,128)(2,1)} %get-tuple-element.57), channel_id=1, source_target_pairs={{0,3},{1,2},{2,1},{3,0},{4,7},{5,6},{6,5},{7,4},{8,11},{9,10},{10,... | collective-permute-start | bytes 786440 | tf_op jit(solution)/shard_map/scatter_grads/ppermute | solution.py:263
  77.9 4.0 %collective-permute-done.18.refs_1_ = bf16[4,4,2,16,256]{4,3,2,1,0:T(8,128)(2,1)S(1)} collective-permute-done((bf16[4,4,2,16,256]{4,3,2,1,0:T(8,128)(2,1)}, bf16[4,4,2,16,256]{4,3,2,1,0:T(8,128)(2,1)S(1)}, u32[]{:S(2)}, u32[]{:S(2)}) %collective-permute-start.18) | collective-permute-done | bytes 262176 | tf_op jit(solution)/shard_map/scatter_grads/ppermute | solution.py:263
  82.9 1.7 %collective-permute-done.20.refs_3_ = bf16[4,4,2,16,256]{4,3,2,1,0:T(8,128)(2,1)S(1)} collective-permute-done((bf16[4,4,2,16,256]{4,3,2,1,0:T(8,128)(2,1)}, bf16[4,4,2,16,256]{4,3,2,1,0:T(8,128)(2,1)S(1)}, u32[]{:S(2)}, u32[]{:S(2)}) %collective-permute-start.20) | collective-permute-done | bytes 262176 | tf_op jit(solution)/shard_map/scatter_grads/ppermute | solution.py:263
  84.8 1.5 %collective-permute-start.21 = (bf16[2,4,2,16,256]{4,3,2,1,0:T(8,128)(2,1)S(1)}, bf16[2,4,2,16,256]{4,3,2,1,0:T(8,128)(2,1)S(1)}, u32[]{:S(2)}, u32[]{:S(2)}) collective-permute-start(bf16[2,4,2,16,256]{4,3,2,1,0:T(8,128)(2,1)S(1)} %get-tuple-element.66), channel_id=1, source_target_pairs={{0,8},{1,9},{2,10},{3,11},{4,12},{5,13},{6,14},{7,15},{8,0},{9,1},... | collective-permute-start | bytes 393224 | tf_op jit(solution)/shard_map/scatter_grads/ppermute | solution.py:263
  86.9 2.1 %collective-permute-start.24 = (bf16[2,4,2,16,256]{4,3,2,1,0:T(8,128)(2,1)S(1)}, bf16[2,4,2,16,256]{4,3,2,1,0:T(8,128)(2,1)S(1)}, u32[]{:S(2)}, u32[]{:S(2)}) collective-permute-start(bf16[2,4,2,16,256]{4,3,2,1,0:T(8,128)(2,1)S(1)} %get-tuple-element.74), channel_id=1, source_target_pairs={{0,12},{1,13},{2,14},{3,15},{4,8},{5,9},{6,10},{7,11},{8,4},{9,5},... | collective-permute-start | bytes 393224 | tf_op jit(solution)/shard_map/scatter_grads/ppermute | solution.py:263
  91.4 1.7 %collective-permute-done.24 = bf16[2,4,2,16,256]{4,3,2,1,0:T(8,128)(2,1)S(1)} collective-permute-done((bf16[2,4,2,16,256]{4,3,2,1,0:T(8,128)(2,1)S(1)}, bf16[2,4,2,16,256]{4,3,2,1,0:T(8,128)(2,1)S(1)}, u32[]{:S(2)}, u32[]{:S(2)}) %collective-permute-start.24) | collective-permute-done | bytes 131104 | tf_op jit(solution)/shard_map/scatter_grads/ppermute | solution.py:263
  93.2 12.1 %all_to_all.5.got = bf16[8,2,16,256]{3,2,1,0:T(8,128)(2,1)S(1)} all-to-all(bf16[8,2,16,256]{3,2,1,0:T(8,128)(2,1)S(1)} %bitcast.13), channel_id=1, replica_groups=mesh['zl'=2,'core'=2,'zh'=4,'x'=4,'y'=4] {'zl','zh'}, dimensions={0} | all-to-all | bytes 262144 | tf_op jit(solution)/shard_map/scatter_grads/all_to_all | solution.py:336
  (45 shorter events, 13.7 us)
Async XLA Ops:
  0.6 42.4 %collective-permute-start = (bf16[256,3072]{1,0:T(8,128)(2,1)}, bf16[256,3072]{1,0:T(8,128)(2,1)S(1)}, u32[]{:S(2)}, u32[]{:S(2)}) collective-permute-start(bf16[256,3072]{1,0:T(8,128)(2,1)} %bitcast.16), channel_id=1, source_target_pairs={{0,64},{64,0},{1,65},{65,1},{2,66},{66,2},{3,67},{67,3},{4,68},{68... | collective-permute-start | bytes 4718600 | tf_op jit(solution)/shard_map/swap_queries/ppermute | solution.py:287
  0.7 42.3 %collective-permute-start.1 = (bf16[256,3072]{1,0:T(8,128)(2,1)}, bf16[256,3072]{1,0:T(8,128)(2,1)S(1)}, u32[]{:S(2)}, u32[]{:S(2)}) collective-permute-start(bf16[256,3072]{1,0:T(8,128)(2,1)} %bitcast.19), channel_id=1, source_target_pairs={{0,64},{64,0},{1,65},{65,1},{2,66},{66,2},{3,67},{67,3},{4,68},{68... | collective-permute-start | bytes 4718600 | tf_op jit(solution)/shard_map/swap_queries/ppermute | solution.py:287
  2.7 7.9 %collective-permute-start.3 = (bf16[2,16,640]{2,1,0:T(8,128)(2,1)S(1)}, bf16[2,16,640]{2,1,0:T(8,128)(2,1)S(1)}, u32[]{:S(2)}, u32[]{:S(2)}) collective-permute-start(bf16[2,16,640]{2,1,0:T(8,128)(2,1)S(1)} %pack_keys_values.1.own), channel_id=1, source_target_pairs={{0,160},{128,32},{16,176},{144,48},{32,128},{160,0},{48,144},{176,... | collective-permute-start | bytes 122888 | tf_op jit(solution)/shard_map/gather_keys/ppermute | solution.py:276
  9.6 6.1 %collective-permute-start.5 = (bf16[2,16,640]{2,1,0:T(8,128)(2,1)S(1)}, bf16[2,16,640]{2,1,0:T(8,128)(2,1)S(1)}, u32[]{:S(2)}, u32[]{:S(2)}) collective-permute-start(bf16[2,16,640]{2,1,0:T(8,128)(2,1)S(1)} %pack_keys_values.1.own), channel_id=1, source_target_pairs={{0,48},{128,144},{16,0},{144,160},{32,16},{160,176},{48,32},{176,1... | collective-permute-start | bytes 122888 | tf_op jit(solution)/shard_map/gather_keys/ppermute | solution.py:276
  15.8 6.9 %collective-permute-start.6 = (bf16[2,4,16,640]{3,2,1,0:T(8,128)(2,1)S(1)}, bf16[2,4,16,640]{3,2,1,0:T(8,128)(2,1)S(1)}, u32[]{:S(2)}, u32[]{:S(2)}) collective-permute-start(bf16[2,4,16,640]{3,2,1,0:T(8,128)(2,1)S(1)} %join_line.1.refs_0_), channel_id=1, source_target_pairs={{0,8},{1,9},{2,10},{3,11},{4,12},{5,13},{6,14},{7,15},{8,0},{9,1},... | collective-permute-start | bytes 491528 | tf_op jit(solution)/shard_map/gather_keys/ppermute | solution.py:263
  18.9 5.6 %collective-permute-start.7 = (bf16[2,4,16,640]{3,2,1,0:T(8,128)(2,1)S(1)}, bf16[2,4,16,640]{3,2,1,0:T(8,128)(2,1)S(1)}, u32[]{:S(2)}, u32[]{:S(2)}) collective-permute-start(bf16[2,4,16,640]{3,2,1,0:T(8,128)(2,1)S(1)} %join_line.1.refs_0_), channel_id=1, source_target_pairs={{0,4},{1,5},{2,6},{3,7},{4,0},{5,1},{6,2},{7,3},{8,12},{9,13},{10,... | collective-permute-start | bytes 491528 | tf_op jit(solution)/shard_map/gather_keys/ppermute | solution.py:263
  19.5 6.5 %collective-permute-start.8 = (bf16[2,4,16,640]{3,2,1,0:T(8,128)(2,1)S(1)}, bf16[2,4,16,640]{3,2,1,0:T(8,128)(2,1)S(1)}, u32[]{:S(2)}, u32[]{:S(2)}) collective-permute-start(bf16[2,4,16,640]{3,2,1,0:T(8,128)(2,1)S(1)} %join_line.1.refs_0_), channel_id=1, source_target_pairs={{0,12},{1,13},{2,14},{3,15},{4,8},{5,9},{6,10},{7,11},{8,4},{9,5},... | collective-permute-start | bytes 491528 | tf_op jit(solution)/shard_map/gather_keys/ppermute | solution.py:263
  22.7 8.0 %collective-permute-start.2 = (f32[24,256]{1,0:T(8,128)}, f32[24,256]{1,0:T(8,128)S(1)}, u32[]{:S(2)}, u32[]{:S(2)}) collective-permute-start(f32[24,256]{1,0:T(8,128)} %bitcast.14), channel_id=1, source_target_pairs={{0,64},{64,0},{1,65},{65,1},{2,66},{66,2},{3,67},{67,3},{4,68},{68... | collective-permute-start | bytes 73736 | tf_op jit(solution)/shard_map/swap_queries/ppermute | solution.py:287
  26.8 8.9 %collective-permute-start.12 = (bf16[256,640]{1,0:T(8,128)(2,1)}, bf16[256,640]{1,0:T(8,128)(2,1)}, u32[]{:S(2)}, u32[]{:S(2)}) collective-permute-start(bf16[256,640]{1,0:T(8,128)(2,1)} %bitcast.6.kv0), channel_id=1, source_target_pairs={{0,2},{1,3},{2,0},{3,1},{4,6},{5,7},{6,4},{7,5},{8,10},{9,11},{10,... | collective-permute-start | bytes 983048 | tf_op jit(solution)/shard_map/gather_keys/ppermute | solution.py:263
  30.0 9.6 %collective-permute-start.13 = (bf16[256,640]{1,0:T(8,128)(2,1)}, bf16[256,640]{1,0:T(8,128)(2,1)}, u32[]{:S(2)}, u32[]{:S(2)}) collective-permute-start(bf16[256,640]{1,0:T(8,128)(2,1)} %bitcast.6.kv0), channel_id=1, source_target_pairs={{0,1},{1,0},{2,3},{3,2},{4,5},{5,4},{6,7},{7,6},{8,9},{9,8},{10,11... | collective-permute-start | bytes 983048 | tf_op jit(solution)/shard_map/gather_keys/ppermute | solution.py:263
  30.7 9.1 %collective-permute-start.14 = (bf16[256,640]{1,0:T(8,128)(2,1)}, bf16[256,640]{1,0:T(8,128)(2,1)}, u32[]{:S(2)}, u32[]{:S(2)}) collective-permute-start(bf16[256,640]{1,0:T(8,128)(2,1)} %bitcast.6.kv0), channel_id=1, source_target_pairs={{0,3},{1,2},{2,1},{3,0},{4,7},{5,6},{6,5},{7,4},{8,11},{9,10},{10,... | collective-permute-start | bytes 983048 | tf_op jit(solution)/shard_map/gather_keys/ppermute | solution.py:263
  35.7 22.7 %collective-permute-start.10 = (bf16[256,640]{1,0:T(8,128)(2,1)S(1)}, bf16[256,640]{1,0:T(8,128)(2,1)S(1)}, u32[]{:S(2)}, u32[]{:S(2)}) collective-permute-start(bf16[256,640]{1,0:T(8,128)(2,1)S(1)} %bitcast.9), channel_id=1, source_target_pairs={{0,1},{1,0},{2,3},{3,2},{4,5},{5,4},{6,7},{7,6},{8,9},{9,8},{10,11... | collective-permute-start | bytes 983048 | tf_op jit(solution)/shard_map/gather_keys/ppermute | solution.py:263
  39.6 21.0 %collective-permute-start.11 = (bf16[256,640]{1,0:T(8,128)(2,1)S(1)}, bf16[256,640]{1,0:T(8,128)(2,1)S(1)}, u32[]{:S(2)}, u32[]{:S(2)}) collective-permute-start(bf16[256,640]{1,0:T(8,128)(2,1)S(1)} %bitcast.10), channel_id=1, source_target_pairs={{0,3},{1,2},{2,1},{3,0},{4,7},{5,6},{6,5},{7,4},{8,11},{9,10},{10,... | collective-permute-start | bytes 983048 | tf_op jit(solution)/shard_map/gather_keys/ppermute | solution.py:263
  39.8 20.9 %collective-permute-start.9 = (bf16[256,640]{1,0:T(8,128)(2,1)S(1)}, bf16[256,640]{1,0:T(8,128)(2,1)S(1)}, u32[]{:S(2)}, u32[]{:S(2)}) collective-permute-start(bf16[256,640]{1,0:T(8,128)(2,1)S(1)} %bitcast.11), channel_id=1, source_target_pairs={{0,2},{1,3},{2,0},{3,1},{4,6},{5,7},{6,4},{7,5},{8,10},{9,11},{10,... | collective-permute-start | bytes 983048 | tf_op jit(solution)/shard_map/gather_keys/ppermute | solution.py:263
  56.4 17.2 %collective-permute-start.15 = (bf16[4,4,2,16,256]{4,3,2,1,0:T(8,128)(2,1)}, bf16[4,4,2,16,256]{4,3,2,1,0:T(8,128)(2,1)S(1)}, u32[]{:S(2)}, u32[]{:S(2)}) collective-permute-start(bf16[4,4,2,16,256]{4,3,2,1,0:T(8,128)(2,1)} %get-tuple-element.51), channel_id=1, source_target_pairs={{0,2},{1,3},{2,0},{3,1},{4,6},{5,7},{6,4},{7,5},{8,10},{9,11},{10,... | collective-permute-start | bytes 786440 | tf_op jit(solution)/shard_map/scatter_grads/ppermute | solution.py:263
  56.8 16.8 %collective-permute-start.16 = (bf16[4,4,2,16,256]{4,3,2,1,0:T(8,128)(2,1)}, bf16[4,4,2,16,256]{4,3,2,1,0:T(8,128)(2,1)S(1)}, u32[]{:S(2)}, u32[]{:S(2)}) collective-permute-start(bf16[4,4,2,16,256]{4,3,2,1,0:T(8,128)(2,1)} %get-tuple-element.52), channel_id=1, source_target_pairs={{0,1},{1,0},{2,3},{3,2},{4,5},{5,4},{6,7},{7,6},{8,9},{9,8},{10,11... | collective-permute-start | bytes 786440 | tf_op jit(solution)/shard_map/scatter_grads/ppermute | solution.py:263
  58.4 15.2 %collective-permute-start.17 = (bf16[4,4,2,16,256]{4,3,2,1,0:T(8,128)(2,1)}, bf16[4,4,2,16,256]{4,3,2,1,0:T(8,128)(2,1)S(1)}, u32[]{:S(2)}, u32[]{:S(2)}) collective-permute-start(bf16[4,4,2,16,256]{4,3,2,1,0:T(8,128)(2,1)} %get-tuple-element.53), channel_id=1, source_target_pairs={{0,3},{1,2},{2,1},{3,0},{4,7},{5,6},{6,5},{7,4},{8,11},{9,10},{10,... | collective-permute-start | bytes 786440 | tf_op jit(solution)/shard_map/scatter_grads/ppermute | solution.py:263
  73.6 8.3 %collective-permute-start.18 = (bf16[4,4,2,16,256]{4,3,2,1,0:T(8,128)(2,1)}, bf16[4,4,2,16,256]{4,3,2,1,0:T(8,128)(2,1)S(1)}, u32[]{:S(2)}, u32[]{:S(2)}) collective-permute-start(bf16[4,4,2,16,256]{4,3,2,1,0:T(8,128)(2,1)} %get-tuple-element.55), channel_id=1, source_target_pairs={{0,2},{1,3},{2,0},{3,1},{4,6},{5,7},{6,4},{7,5},{8,10},{9,11},{10,... | collective-permute-start | bytes 786440 | tf_op jit(solution)/shard_map/scatter_grads/ppermute | solution.py:263
  74.4 8.5 %collective-permute-start.19 = (bf16[4,4,2,16,256]{4,3,2,1,0:T(8,128)(2,1)}, bf16[4,4,2,16,256]{4,3,2,1,0:T(8,128)(2,1)S(1)}, u32[]{:S(2)}, u32[]{:S(2)}) collective-permute-start(bf16[4,4,2,16,256]{4,3,2,1,0:T(8,128)(2,1)} %get-tuple-element.56), channel_id=1, source_target_pairs={{0,1},{1,0},{2,3},{3,2},{4,5},{5,4},{6,7},{7,6},{8,9},{9,8},{10,11... | collective-permute-start | bytes 786440 | tf_op jit(solution)/shard_map/scatter_grads/ppermute | solution.py:263
  75.6 9.0 %collective-permute-start.20 = (bf16[4,4,2,16,256]{4,3,2,1,0:T(8,128)(2,1)}, bf16[4,4,2,16,256]{4,3,2,1,0:T(8,128)(2,1)S(1)}, u32[]{:S(2)}, u32[]{:S(2)}) collective-permute-start(bf16[4,4,2,16,256]{4,3,2,1,0:T(8,128)(2,1)} %get-tuple-element.57), channel_id=1, source_target_pairs={{0,3},{1,2},{2,1},{3,0},{4,7},{5,6},{6,5},{7,4},{8,11},{9,10},{10,... | collective-permute-start | bytes 786440 | tf_op jit(solution)/shard_map/scatter_grads/ppermute | solution.py:263
  84.7 4.3 %collective-permute-start.22 = (f32[256,1536]{1,0:T(8,128)}, f32[256,1536]{1,0:T(8,128)S(1)}, u32[]{:S(2)}, u32[]{:S(2)}) collective-permute-start(f32[256,1536]{1,0:T(8,128)} %get-tuple-element.70), channel_id=1, source_target_pairs={{0,64},{64,0},{1,65},{65,1},{2,66},{66,2},{3,67},{67,3},{4,68},{68... | collective-permute-start | bytes 4718600 | tf_op jit(solution)/shard_map/swap_query_grads/ppermute | solution.py:287
  84.8 6.6 %collective-permute-start.21 = (bf16[2,4,2,16,256]{4,3,2,1,0:T(8,128)(2,1)S(1)}, bf16[2,4,2,16,256]{4,3,2,1,0:T(8,128)(2,1)S(1)}, u32[]{:S(2)}, u32[]{:S(2)}) collective-permute-start(bf16[2,4,2,16,256]{4,3,2,1,0:T(8,128)(2,1)S(1)} %get-tuple-element.66), channel_id=1, source_target_pairs={{0,8},{1,9},{2,10},{3,11},{4,12},{5,13},{6,14},{7,15},{8,0},{9,1},... | collective-permute-start | bytes 393224 | tf_op jit(solution)/shard_map/scatter_grads/ppermute | solution.py:263
  86.4 5.0 %collective-permute-start.23 = (bf16[2,4,2,16,256]{4,3,2,1,0:T(8,128)(2,1)S(1)}, bf16[2,4,2,16,256]{4,3,2,1,0:T(8,128)(2,1)S(1)}, u32[]{:S(2)}, u32[]{:S(2)}) collective-permute-start(bf16[2,4,2,16,256]{4,3,2,1,0:T(8,128)(2,1)S(1)} %get-tuple-element.73), channel_id=1, source_target_pairs={{0,4},{1,5},{2,6},{3,7},{4,0},{5,1},{6,2},{7,3},{8,12},{9,13},{10,... | collective-permute-start | bytes 393224 | tf_op jit(solution)/shard_map/scatter_grads/ppermute | solution.py:263
  86.9 6.2 %collective-permute-start.24 = (bf16[2,4,2,16,256]{4,3,2,1,0:T(8,128)(2,1)S(1)}, bf16[2,4,2,16,256]{4,3,2,1,0:T(8,128)(2,1)S(1)}, u32[]{:S(2)}, u32[]{:S(2)}) collective-permute-start(bf16[2,4,2,16,256]{4,3,2,1,0:T(8,128)(2,1)S(1)} %get-tuple-element.74), channel_id=1, source_target_pairs={{0,12},{1,13},{2,14},{3,15},{4,8},{5,9},{6,10},{7,11},{8,4},{9,5},... | collective-permute-start | bytes 393224 | tf_op jit(solution)/shard_map/scatter_grads/ppermute | solution.py:263
  (3 other events, 32.4 us)

commit v5 on v4

--- a/solution.py
+++ b/solution.py
@@ -18,6 +18,7 @@
 COLS = PAIR * HEAD_DIM
 PAYLOAD = 2 * COLS + 128
 BLOCK = 256
+KEYS = 4 * BLOCK
 APART = (0, 2, 1, 3)
 AXES = ("zl", "core", "zh", "x", "y")
 
@@ -51,10 +52,13 @@
         base = (((row >> 4) & 3) * 16 + (row >> 6) * b_step) * 256 + (row & 15)
         for a, piece in enumerate(pieces):
             slab = (a0 ^ APART[a]) * a_step
-            pos_s[a] = piece[:, 2 * COLS:].astype(jnp.float32) + (base + slab * 256).astype(jnp.float32)
+            sl = slice(a * BLOCK, (a + 1) * BLOCK)
+            offset = piece[BLOCK:, :128].astype(jnp.float32).reshape(SLAB, 1, 128)
+            offset = jnp.broadcast_to(offset, (SLAB, SLAB, 128)).reshape(BLOCK, 128)
+            pos_s[sl, :] = offset + (base + slab * 256).astype(jnp.float32)
             for h in range(PAIR):
-                key_s[h, a] = piece[:, h * 128:(h + 1) * 128]
-                val_s[h, a] = piece[:, COLS + h * 128:COLS + (h + 1) * 128]
+                key_s[h, sl, :] = piece[:BLOCK, h * 128:(h + 1) * 128]
+                val_s[h, sl, :] = piece[:BLOCK, COLS + h * 128:COLS + (h + 1) * 128]
 
     lane = lax.broadcasted_iota(jnp.int32, (1, 128), 1)
     q_pos = [(first + lane + c * 128).astype(jnp.float32) for c in range(2)]
@@ -70,31 +74,31 @@
         rows = slice(layer * WIDE, (layer + 1) * WIDE)
         lse = lse_ref[0] * LOG2E
         delta = jnp.zeros((1, WIDE), jnp.float32)
-        for a in range(4):
-            score = matmul(key_s[step, a], rows_q[rows, :], (1, 1))
+        for low in range(0, KEYS, BLOCK):
+            sl = slice(low, low + BLOCK)
+            score = matmul(key_s[step, sl, :], rows_q[rows, :], (1, 1))
             prob = jnp.exp2(score * (SCALE * LOG2E) - lse)
-            seen = jnp.concatenate([pos_s[a] <= q_pos[0], pos_s[a] <= q_pos[1]] * GROUP, axis=1)
+            seen = jnp.concatenate([pos_s[sl, :] <= q_pos[0], pos_s[sl, :] <= q_pos[1]] * GROUP, axis=1)
             prob = jnp.where(seen, prob, 0.0)
-            grad_prob = matmul(val_s[step, a], rows_g[rows, :], (1, 1))
+            grad_prob = matmul(val_s[step, sl, :], rows_g[rows, :], (1, 1))
             delta = delta + jnp.sum(prob * grad_prob, axis=0, keepdims=True)
-            prob_s[layer, a] = prob
-            gp_s[layer, a] = grad_prob
-            half_s[a, :, rows] = prob.astype(jnp.bfloat16)
-        for a in range(4):
-            ds_s[a, :, rows] = (prob_s[layer, a] * (gp_s[layer, a] - delta)).astype(jnp.bfloat16)
-
+            prob_s[layer, sl, :] = prob
+            gp_s[layer, sl, :] = grad_prob
+            half_s[sl, rows] = prob.astype(jnp.bfloat16)
+        for low in range(0, KEYS, BLOCK):
+            sl = slice(low, low + BLOCK)
+            ds_s[sl, rows] = (prob_s[layer, sl, :] * (gp_s[layer, sl, :] - delta)).astype(jnp.bfloat16)
+
+    dv = matmul(half_s[...], rows_g[...], (1, 0))
+    dk = matmul(ds_s[...], rows_q[...], (1, 0)) * SCALE
     for a, out in enumerate(outs):
-        dv = matmul(half_s[a], rows_g[...], (1, 0))
-        dk = matmul(ds_s[a], rows_q[...], (1, 0)) * SCALE
-        out[:, :, 0] = dk.astype(out.dtype).reshape(4, 4, SLAB, HEAD_DIM)
-        out[:, :, 1] = dv.astype(out.dtype).reshape(4, 4, SLAB, HEAD_DIM)
+        sl = slice(a * BLOCK, (a + 1) * BLOCK)
+        out[:, :, 0] = dk[sl].astype(out.dtype).reshape(4, 4, SLAB, HEAD_DIM)
+        out[:, :, 1] = dv[sl].astype(out.dtype).reshape(4, 4, SLAB, HEAD_DIM)
 
     for layer, (_, _, _, dq_ref) in enumerate(sides):
         rows = slice(layer * WIDE, (layer + 1) * WIDE)
-        dq_t = matmul(key_s[step, 0], ds_s[0, :, rows], (0, 0))
-        for a in range(1, 4):
-            dq_t = dq_t + matmul(key_s[step, a], ds_s[a, :, rows], (0, 0))
-        dq_t = dq_t * SCALE
+        dq_t = matmul(key_s[step], ds_s[:, rows], (0, 0)) * SCALE
         for h in range(GROUP):
             dq_ref[:, h * 128:(h + 1) * 128] = dq_t[:, h * ROWS:(h + 1) * ROWS].T
 
@@ -108,7 +112,7 @@
     width = GROUP * HEAD_DIM
     own = pl.BlockSpec((ROWS, width), lambda g, m: (0, head(g, m)))
     back = pl.BlockSpec((ROWS, width), lambda g, m: (0, chunk * 2 + g))
-    part = pl.BlockSpec((BLOCK, PAYLOAD), lambda g, m: (0, 0))
+    part = pl.BlockSpec(kv[0].shape, lambda g, m: (0, 0))
     lse = pl.BlockSpec((1, 1, WIDE), lambda g, m: (head(g, m), 0, 0))
     out_dims = (4, 4, 2, SLAB, PAIR * HEAD_DIM)
     out = pl.BlockSpec((4, 4, 2, SLAB, HEAD_DIM), lambda g, m: (0, 0, 0, 0, g))
@@ -121,15 +125,15 @@
             + [pl.BlockSpec(memory_space=pl.ANY)] * len(partly),
             out_specs=[own, back, out, out, out, out],
             scratch_shapes=[
-                pltpu.VMEM((4, BLOCK, 128), f32),
-                pltpu.VMEM((PAIR, 4, BLOCK, HEAD_DIM), bf16),
-                pltpu.VMEM((PAIR, 4, BLOCK, HEAD_DIM), bf16),
+                pltpu.VMEM((KEYS, 128), f32),
+                pltpu.VMEM((PAIR, KEYS, HEAD_DIM), bf16),
+                pltpu.VMEM((PAIR, KEYS, HEAD_DIM), bf16),
                 pltpu.VMEM((2 * WIDE, HEAD_DIM), bf16),
                 pltpu.VMEM((2 * WIDE, HEAD_DIM), bf16),
-                pltpu.VMEM((2, 4, BLOCK, WIDE), f32),
-                pltpu.VMEM((2, 4, BLOCK, WIDE), f32),
-                pltpu.VMEM((4, BLOCK, 2 * WIDE), bf16),
-                pltpu.VMEM((4, BLOCK, 2 * WIDE), bf16),
+                pltpu.VMEM((2, KEYS, WIDE), f32),
+                pltpu.VMEM((2, KEYS, WIDE), f32),
+                pltpu.VMEM((KEYS, 2 * WIDE), bf16),
+                pltpu.VMEM((KEYS, 2 * WIDE), bf16),
             ],
         ),
         out_shape=[
@@ -197,13 +201,20 @@
 
 def pieces_kernel(*refs):
     b0 = plane_place()
-    for r, block in enumerate(refs[:4]):
-        for chunk, out in enumerate(refs[4:]):
-            out[b0 ^ APART[r]] = block[chunk]
+    row = lax.broadcasted_iota(jnp.int32, (SLAB, 128), 0)
+    for chunk, out in enumerate(refs[4:]):
+        tail = jnp.zeros((SLAB, 128), jnp.float32)
+        for r, block in enumerate(refs[:4]):
+            for z in range(4):
+                place = (b0 ^ APART[r]) * 4 + z
+                out[place] = block[chunk, z, :, :2 * COLS]
+                offset = block[chunk, z, :, 2 * COLS:].astype(jnp.float32)
+                tail = jnp.where(row == place, offset, tail)
+        out[SLAB] = jnp.concatenate([tail] * (2 * COLS // 128), 1).astype(jnp.bfloat16)
 
 
 def pieces_of(blocks):
-    shape = jax.ShapeDtypeStruct((4, 4, SLAB, PAYLOAD), jnp.bfloat16)
+    shape = jax.ShapeDtypeStruct((SLAB + 1, SLAB, 2 * COLS), jnp.bfloat16)
     return pl.pallas_call(
         pieces_kernel,
         in_specs=[VMEM] * 4,
@@ -296,15 +307,15 @@
 
     with jax.named_scope("gather_keys"):
         payload = pack(slab_starts, shared_keys, shared_values)
+        q_sent, g_sent, payload = lax.optimization_barrier((queries, out_grads, payload))
         block = line([payload] + [z_shift(payload, by) for by in (3, 1, 2)])
+        with jax.named_scope("swap_queries"):
+            q_oth, g_oth, lse_oth = (swap(v) for v in (q_sent, g_sent, lse))
         own = pieces_of([block] + plane_swaps([block] * 3, 0))
         pieces = []
         for piece in own:
-            piece = piece.reshape(BLOCK, PAYLOAD)
+            piece = piece.reshape(BLOCK + SLAB, 2 * COLS)
             pieces.append([piece] + plane_swaps([piece] * 3, 1))
-    with jax.named_scope("swap_queries"):
-        q_oth, g_oth, lse_oth = (swap(v) for v in (queries, out_grads, lse))
-
     a0 = jnp.where(core == 0, y, x)
     meta = jnp.stack([core, a0, query_starts[0]]).astype(jnp.int32)
     wide = (KV_HEADS, 1, WIDE)
@@ -323,14 +334,15 @@
 
     dq, dq_oth = partly
     with jax.named_scope("scatter_grads"):
-        mine, *shares = share(1, sums[1], share(0, sums[0], []))
-        shares = plane_swaps(shares, 0)
+        first_shares = share(0, sums[0], [])
     with jax.named_scope("swap_query_grads"):
-        dq_oth, _ = lax.optimization_barrier((dq_oth, mine))
+        dq_oth, first_shares = lax.optimization_barrier((dq_oth, first_shares))
         back = swap(dq_oth)
         dq = lax.dynamic_update_slice(dq, back[:, :768], (0, other * 768))
         dq = lax.dynamic_update_slice(dq, back[:, 768:], (0, (2 + other) * 768))
     with jax.named_scope("scatter_grads"):
+        mine, *shares = share(1, sums[1], first_shares)
+        shares = plane_swaps(shares, 0)
         shares[0], dq = lax.optimization_barrier((shares[0], dq))
         small = add([mine, *shares]).reshape(8, 2, SLAB, 2 * HEAD_DIM)
         dk, dv = finish(lax.all_to_all(small, ("zl", "zh"), 0, 0))

time: 106 us -> 104 us (0.981)
  transfers between devices with their start and end apart: 25 -> 25, of which waited for: 13 -> 13; matrix products, arithmetic and copies ran while one was open for 3% -> 3% of each run, Pallas kernels for 27% -> 25%
where the time goes in v5:
time: 104 us
  starting transfers between devices  34.3 us (33%)
  Pallas kernels  27.8 us (27%)
  waiting for transfers between devices  25 us (24%)
  blocking collectives  12.1 us (12%)
  local copies, waits for them, and re-layouts  2.66 us (3%)
  between operations  2.06 us (2%)
    ppermute x18, starting transfers between devices, plane_swap(): return lax.ppermute(value, ('core', 'x', 'y'), pairs)  26.1 us
    pallas_call x2, Pallas kernels, attention(): pl.pallas_call(attention_kernel, grid_spec=pltpu.PrefetchScalarGridSpec(n...  25.3 us
    ppermute x18, waiting for transfers between devices, plane_swap(): return lax.ppermute(value, ('core', 'x', 'y'), pairs)  19.3 us
    all_to_all x1, blocking collectives, per_device(): dk, dv = finish(lax.all_to_all(small, ('zl', 'zh'), 0, 0))  12.1 us
    ppermute x3, starting transfers between devices, z_shift(): return lax.ppermute(value, ('zl', 'zh'), pairs)  7.31 us
    ppermute x3, waiting for transfers between devices, z_shift(): return lax.ppermute(value, ('zl', 'zh'), pairs)  5.66 us
  transfers between devices with their start and end apart: 25, of which 13 were waited for; matrix products, arithmetic and copies ran while one was open for 3% of the time, Pallas kernels for 25%

profile of v5, /device:TPU:32, one launch (start us, length us, event | category | flops | bytes accessed | tf_op | source)
XLA Modules:
  0.0 104.1 jit_solution(8788528464113174374)
XLA Ops:
  2.7 5.8 %collective-permute-start.3 = (bf16[2,16,640]{2,1,0:T(8,128)(2,1)S(1)}, bf16[2,16,640]{2,1,0:T(8,128)(2,1)S(1)}, u32[]{:S(2)}, u32[]{:S(2)}) collective-permute-start(bf16[2,16,640]{2,1,0:T(8,128)(2,1)S(1)} %pack_keys_values.1.own), channel_id=1, source_target_pairs={{0,160},{128,32},{16,176},{144,48},{32,128},{160,0},{48,144},{176,... | collective-permute-start | bytes 122888 | tf_op jit(solution)/shard_map/gather_keys/ppermute | solution.py:287
  10.5 2.2 %collective-permute-done.4.near = bf16[2,16,640]{2,1,0:T(8,128)(2,1)S(1)} collective-permute-done((bf16[2,16,640]{2,1,0:T(8,128)(2,1)S(1)}, bf16[2,16,640]{2,1,0:T(8,128)(2,1)S(1)}, u32[]{:S(2)}, u32[]{:S(2)}) %collective-permute-start.4) | collective-permute-done | bytes 40992 | tf_op jit(solution)/shard_map/gather_keys/ppermute | solution.py:287
  12.7 3.0 %collective-permute-done.5.next_ = bf16[2,16,640]{2,1,0:T(8,128)(2,1)S(1)} collective-permute-done((bf16[2,16,640]{2,1,0:T(8,128)(2,1)S(1)}, bf16[2,16,640]{2,1,0:T(8,128)(2,1)S(1)}, u32[]{:S(2)}, u32[]{:S(2)}) %collective-permute-start.5) | collective-permute-done | bytes 40992 | tf_op jit(solution)/shard_map/gather_keys/ppermute | solution.py:287
  15.7 3.1 %collective-permute-start.6 = (bf16[2,4,16,640]{3,2,1,0:T(8,128)(2,1)S(1)}, bf16[2,4,16,640]{3,2,1,0:T(8,128)(2,1)S(1)}, u32[]{:S(2)}, u32[]{:S(2)}) collective-permute-start(bf16[2,4,16,640]{3,2,1,0:T(8,128)(2,1)S(1)} %join_line.1.refs_0_), channel_id=1, source_target_pairs={{0,8},{1,9},{2,10},{3,11},{4,12},{5,13},{6,14},{7,15},{8,0},{9,1},... | collective-permute-start | bytes 491528 | tf_op jit(solution)/shard_map/gather_keys/ppermute | solution.py:274
  19.9 2.7 %collective-permute-done.6.refs_1_ = bf16[2,4,16,640]{3,2,1,0:T(8,128)(2,1)S(1)} collective-permute-done((bf16[2,4,16,640]{3,2,1,0:T(8,128)(2,1)S(1)}, bf16[2,4,16,640]{3,2,1,0:T(8,128)(2,1)S(1)}, u32[]{:S(2)}, u32[]{:S(2)}) %collective-permute-start.6) | collective-permute-done | bytes 163872 | tf_op jit(solution)/shard_map/gather_keys/ppermute | solution.py:274
  22.6 1.8 %collective-permute-done.7.refs_2_ = bf16[2,4,16,640]{3,2,1,0:T(8,128)(2,1)S(1)} collective-permute-done((bf16[2,4,16,640]{3,2,1,0:T(8,128)(2,1)S(1)}, bf16[2,4,16,640]{3,2,1,0:T(8,128)(2,1)S(1)}, u32[]{:S(2)}, u32[]{:S(2)}) %collective-permute-start.7) | collective-permute-done | bytes 163872 | tf_op jit(solution)/shard_map/gather_keys/ppermute | solution.py:274
  24.4 1.5 %collective-permute-done.8.refs_3_ = bf16[2,4,16,640]{3,2,1,0:T(8,128)(2,1)S(1)} collective-permute-done((bf16[2,4,16,640]{3,2,1,0:T(8,128)(2,1)S(1)}, bf16[2,4,16,640]{3,2,1,0:T(8,128)(2,1)S(1)}, u32[]{:S(2)}, u32[]{:S(2)}) %collective-permute-start.8) | collective-permute-done | bytes 163872 | tf_op jit(solution)/shard_map/gather_keys/ppermute | solution.py:274
  26.7 3.2 %collective-permute-start.12 = (bf16[272,512]{1,0:T(8,128)(2,1)}, bf16[272,512]{1,0:T(8,128)(2,1)}, u32[]{:S(2)}, u32[]{:S(2)}) collective-permute-start(bf16[272,512]{1,0:T(8,128)(2,1)} %bitcast.6.kv0), channel_id=1, source_target_pairs={{0,2},{1,3},{2,0},{3,1},{4,6},{5,7},{6,4},{7,5},{8,10},{9,11},{10,... | collective-permute-start | bytes 835592 | tf_op jit(solution)/shard_map/gather_keys/ppermute | solution.py:274
  32.5 2.6 %collective-permute-done.12.kv1 = bf16[272,512]{1,0:T(8,128)(2,1)} collective-permute-done((bf16[272,512]{1,0:T(8,128)(2,1)}, bf16[272,512]{1,0:T(8,128)(2,1)}, u32[]{:S(2)}, u32[]{:S(2)}) %collective-permute-start.12) | collective-permute-done | bytes 278560 | tf_op jit(solution)/shard_map/gather_keys/ppermute | solution.py:274
  35.0 1.7 %collective-permute-start.10 = (bf16[272,512]{1,0:T(8,128)(2,1)S(1)}, bf16[272,512]{1,0:T(8,128)(2,1)S(1)}, u32[]{:S(2)}, u32[]{:S(2)}) collective-permute-start(bf16[272,512]{1,0:T(8,128)(2,1)S(1)} %bitcast.9), channel_id=1, source_target_pairs={{0,1},{1,0},{2,3},{3,2},{4,5},{5,4},{6,7},{7,6},{8,9},{9,8},{10,11... | collective-permute-start | bytes 835592 | tf_op jit(solution)/shard_map/gather_keys/ppermute | solution.py:274
  36.7 1.7 %collective-permute-done.13.kv2 = bf16[272,512]{1,0:T(8,128)(2,1)} collective-permute-done((bf16[272,512]{1,0:T(8,128)(2,1)}, bf16[272,512]{1,0:T(8,128)(2,1)}, u32[]{:S(2)}, u32[]{:S(2)}) %collective-permute-start.13) | collective-permute-done | bytes 278560 | tf_op jit(solution)/shard_map/gather_keys/ppermute | solution.py:274
  38.9 2.9 %collective-permute-start.9 = (bf16[272,512]{1,0:T(8,128)(2,1)S(1)}, bf16[272,512]{1,0:T(8,128)(2,1)S(1)}, u32[]{:S(2)}, u32[]{:S(2)}) collective-permute-start(bf16[272,512]{1,0:T(8,128)(2,1)S(1)} %bitcast.11), channel_id=1, source_target_pairs={{0,2},{1,3},{2,0},{3,1},{4,6},{5,7},{6,4},{7,5},{8,10},{9,11},{10,... | collective-permute-start | bytes 835592 | tf_op jit(solution)/shard_map/gather_keys/ppermute | solution.py:274
  41.8 12.9 %attention_backward.2 = (f32[256,3072]{1,0:T(8,128)}, f32[256,1536]{1,0:T(8,128)}, f32[4,4,2,16,256]{4,3,2,1,0:T(8,128)}, bf16[4,4,2,16,256]{4,3,2,1,0:T(8,128)(...) custom-call(s32[3]{0:T(128)S(1)} %pad_add_fusion.meta, bf16[256,3072]{1,0:T(8,128)(2,1)} %bitcast.17, ...), custom_call_target="tpu_custom_call" | custom-call | flops 8000000000 | bytes 8388608 | tf_op jit(solution)/shard_map/attention_backward/pallas_call | solution.py:119
  55.4 1.3 %collective-permute-start.16 = (bf16[4,4,2,16,256]{4,3,2,1,0:T(8,128)(2,1)}, bf16[4,4,2,16,256]{4,3,2,1,0:T(8,128)(2,1)S(1)}, u32[]{:S(2)}, u32[]{:S(2)}) collective-permute-start(bf16[4,4,2,16,256]{4,3,2,1,0:T(8,128)(2,1)} %get-tuple-element.62), channel_id=1, source_target_pairs={{0,1},{1,0},{2,3},{3,2},{4,5},{5,4},{6,7},{7,6},{8,9},{9,8},{10,11... | collective-permute-start | bytes 786440 | tf_op jit(solution)/shard_map/scatter_grads/ppermute | solution.py:274
  56.7 2.2 %collective-permute-start.17 = (bf16[4,4,2,16,256]{4,3,2,1,0:T(8,128)(2,1)}, bf16[4,4,2,16,256]{4,3,2,1,0:T(8,128)(2,1)S(1)}, u32[]{:S(2)}, u32[]{:S(2)}) collective-permute-start(bf16[4,4,2,16,256]{4,3,2,1,0:T(8,128)(2,1)} %get-tuple-element.63), channel_id=1, source_target_pairs={{0,3},{1,2},{2,1},{3,0},{4,7},{5,6},{6,5},{7,4},{8,11},{9,10},{10,... | collective-permute-start | bytes 786440 | tf_op jit(solution)/shard_map/scatter_grads/ppermute | solution.py:274
  58.9 12.4 %attention_backward.3 = (f32[256,3072]{1,0:T(8,128)}, f32[256,1536]{1,0:T(8,128)}, f32[4,4,2,16,256]{4,3,2,1,0:T(8,128)}, bf16[4,4,2,16,256]{4,3,2,1,0:T(8,128)(...) custom-call(s32[3]{0:T(128)S(1)} %pad_add_fusion.meta, ...), custom_call_target="tpu_custom_call", output_to_operand_aliasing={{0}: (11, {}), {1}: (12, {})} | custom-call | flops 8000000000 | bytes 8388608 | tf_op jit(solution)/shard_map/attention_backward/pallas_call | solution.py:119
  72.7 1.1 %collective-permute-start.19 = (bf16[4,4,2,16,256]{4,3,2,1,0:T(8,128)(2,1)}, bf16[4,4,2,16,256]{4,3,2,1,0:T(8,128)(2,1)S(1)}, u32[]{:S(2)}, u32[]{:S(2)}) collective-permute-start(bf16[4,4,2,16,256]{4,3,2,1,0:T(8,128)(2,1)} %get-tuple-element.66), channel_id=1, source_target_pairs={{0,1},{1,0},{2,3},{3,2},{4,5},{5,4},{6,7},{7,6},{8,9},{9,8},{10,11... | collective-permute-start | bytes 786440 | tf_op jit(solution)/shard_map/scatter_grads/ppermute | solution.py:274
  73.8 2.2 %collective-permute-start.20 = (bf16[4,4,2,16,256]{4,3,2,1,0:T(8,128)(2,1)}, bf16[4,4,2,16,256]{4,3,2,1,0:T(8,128)(2,1)S(1)}, u32[]{:S(2)}, u32[]{:S(2)}) collective-permute-start(bf16[4,4,2,16,256]{4,3,2,1,0:T(8,128)(2,1)} %get-tuple-element.67), channel_id=1, source_target_pairs={{0,3},{1,2},{2,1},{3,0},{4,7},{5,6},{6,5},{7,4},{8,11},{9,10},{10,... | collective-permute-start | bytes 786440 | tf_op jit(solution)/shard_map/scatter_grads/ppermute | solution.py:274
  76.1 4.1 %collective-permute-done.18.refs_1_ = bf16[4,4,2,16,256]{4,3,2,1,0:T(8,128)(2,1)S(1)} collective-permute-done((bf16[4,4,2,16,256]{4,3,2,1,0:T(8,128)(2,1)}, bf16[4,4,2,16,256]{4,3,2,1,0:T(8,128)(2,1)S(1)}, u32[]{:S(2)}, u32[]{:S(2)}) %collective-permute-start.18) | collective-permute-done | bytes 262176 | tf_op jit(solution)/shard_map/scatter_grads/ppermute | solution.py:274
  81.2 1.7 %collective-permute-done.20.refs_3_ = bf16[4,4,2,16,256]{4,3,2,1,0:T(8,128)(2,1)S(1)} collective-permute-done((bf16[4,4,2,16,256]{4,3,2,1,0:T(8,128)(2,1)}, bf16[4,4,2,16,256]{4,3,2,1,0:T(8,128)(2,1)S(1)}, u32[]{:S(2)}, u32[]{:S(2)}) %collective-permute-start.20) | collective-permute-done | bytes 262176 | tf_op jit(solution)/shard_map/scatter_grads/ppermute | solution.py:274
  83.0 1.5 %collective-permute-start.21 = (bf16[2,4,2,16,256]{4,3,2,1,0:T(8,128)(2,1)S(1)}, bf16[2,4,2,16,256]{4,3,2,1,0:T(8,128)(2,1)S(1)}, u32[]{:S(2)}, u32[]{:S(2)}) collective-permute-start(bf16[2,4,2,16,256]{4,3,2,1,0:T(8,128)(2,1)S(1)} %get-tuple-element.81), channel_id=1, source_target_pairs={{0,8},{1,9},{2,10},{3,11},{4,12},{5,13},{6,14},{7,15},{8,0},{9,1},... | collective-permute-start | bytes 393224 | tf_op jit(solution)/shard_map/scatter_grads/ppermute | solution.py:274
  85.1 2.0 %collective-permute-start.24 = (bf16[2,4,2,16,256]{4,3,2,1,0:T(8,128)(2,1)S(1)}, bf16[2,4,2,16,256]{4,3,2,1,0:T(8,128)(2,1)S(1)}, u32[]{:S(2)}, u32[]{:S(2)}) collective-permute-start(bf16[2,4,2,16,256]{4,3,2,1,0:T(8,128)(2,1)S(1)} %get-tuple-element.88), channel_id=1, source_target_pairs={{0,12},{1,13},{2,14},{3,15},{4,8},{5,9},{6,10},{7,11},{8,4},{9,5},... | collective-permute-start | bytes 393224 | tf_op jit(solution)/shard_map/scatter_grads/ppermute | solution.py:274
  89.5 1.8 %collective-permute-done.24 = bf16[2,4,2,16,256]{4,3,2,1,0:T(8,128)(2,1)S(1)} collective-permute-done((bf16[2,4,2,16,256]{4,3,2,1,0:T(8,128)(2,1)S(1)}, bf16[2,4,2,16,256]{4,3,2,1,0:T(8,128)(2,1)S(1)}, u32[]{:S(2)}, u32[]{:S(2)}) %collective-permute-start.24) | collective-permute-done | bytes 131104 | tf_op jit(solution)/shard_map/scatter_grads/ppermute | solution.py:274
  91.4 12.1 %all_to_all.5.got = bf16[8,2,16,256]{3,2,1,0:T(8,128)(2,1)S(1)} all-to-all(bf16[8,2,16,256]{3,2,1,0:T(8,128)(2,1)S(1)} %bitcast.13), channel_id=1, replica_groups=mesh['zl'=2,'core'=2,'zh'=4,'x'=4,'y'=4] {'zl','zh'}, dimensions={0} | all-to-all | bytes 262144 | tf_op jit(solution)/shard_map/scatter_grads/all_to_all | solution.py:348
  (45 shorter events, 14.6 us)
Async XLA Ops:
  2.1 39.8 %collective-permute-start = (bf16[256,3072]{1,0:T(8,128)(2,1)}, bf16[256,3072]{1,0:T(8,128)(2,1)S(1)}, u32[]{:S(2)}, u32[]{:S(2)}) collective-permute-start(bf16[256,3072]{1,0:T(8,128)(2,1)} %bitcast.16), channel_id=1, source_target_pairs={{0,64},{64,0},{1,65},{65,1},{2,66},{66,2},{3,67},{67,3},{4,68},{68... | collective-permute-start | bytes 4718600 | tf_op jit(solution)/shard_map/gather_keys/swap_queries/ppermute | solution.py:298
  2.2 39.7 %collective-permute-start.1 = (bf16[256,3072]{1,0:T(8,128)(2,1)}, bf16[256,3072]{1,0:T(8,128)(2,1)S(1)}, u32[]{:S(2)}, u32[]{:S(2)}) collective-permute-start(bf16[256,3072]{1,0:T(8,128)(2,1)} %bitcast.19), channel_id=1, source_target_pairs={{0,64},{64,0},{1,65},{65,1},{2,66},{66,2},{3,67},{67,3},{4,68},{68... | collective-permute-start | bytes 4718600 | tf_op jit(solution)/shard_map/gather_keys/swap_queries/ppermute | solution.py:298
  2.7 7.8 %collective-permute-start.3 = (bf16[2,16,640]{2,1,0:T(8,128)(2,1)S(1)}, bf16[2,16,640]{2,1,0:T(8,128)(2,1)S(1)}, u32[]{:S(2)}, u32[]{:S(2)}) collective-permute-start(bf16[2,16,640]{2,1,0:T(8,128)(2,1)S(1)} %pack_keys_values.1.own), channel_id=1, source_target_pairs={{0,160},{128,32},{16,176},{144,48},{32,128},{160,0},{48,144},{176,... | collective-permute-start | bytes 122888 | tf_op jit(solution)/shard_map/gather_keys/ppermute | solution.py:287
  9.5 6.1 %collective-permute-start.5 = (bf16[2,16,640]{2,1,0:T(8,128)(2,1)S(1)}, bf16[2,16,640]{2,1,0:T(8,128)(2,1)S(1)}, u32[]{:S(2)}, u32[]{:S(2)}) collective-permute-start(bf16[2,16,640]{2,1,0:T(8,128)(2,1)S(1)} %pack_keys_values.1.own), channel_id=1, source_target_pairs={{0,48},{128,144},{16,0},{144,160},{32,16},{160,176},{48,32},{176,1... | collective-permute-start | bytes 122888 | tf_op jit(solution)/shard_map/gather_keys/ppermute | solution.py:287
  15.7 6.9 %collective-permute-start.6 = (bf16[2,4,16,640]{3,2,1,0:T(8,128)(2,1)S(1)}, bf16[2,4,16,640]{3,2,1,0:T(8,128)(2,1)S(1)}, u32[]{:S(2)}, u32[]{:S(2)}) collective-permute-start(bf16[2,4,16,640]{3,2,1,0:T(8,128)(2,1)S(1)} %join_line.1.refs_0_), channel_id=1, source_target_pairs={{0,8},{1,9},{2,10},{3,11},{4,12},{5,13},{6,14},{7,15},{8,0},{9,1},... | collective-permute-start | bytes 491528 | tf_op jit(solution)/shard_map/gather_keys/ppermute | solution.py:274
  18.8 5.6 %collective-permute-start.7 = (bf16[2,4,16,640]{3,2,1,0:T(8,128)(2,1)S(1)}, bf16[2,4,16,640]{3,2,1,0:T(8,128)(2,1)S(1)}, u32[]{:S(2)}, u32[]{:S(2)}) collective-permute-start(bf16[2,4,16,640]{3,2,1,0:T(8,128)(2,1)S(1)} %join_line.1.refs_0_), channel_id=1, source_target_pairs={{0,4},{1,5},{2,6},{3,7},{4,0},{5,1},{6,2},{7,3},{8,12},{9,13},{10,... | collective-permute-start | bytes 491528 | tf_op jit(solution)/shard_map/gather_keys/ppermute | solution.py:274
  19.4 6.5 %collective-permute-start.8 = (bf16[2,4,16,640]{3,2,1,0:T(8,128)(2,1)S(1)}, bf16[2,4,16,640]{3,2,1,0:T(8,128)(2,1)S(1)}, u32[]{:S(2)}, u32[]{:S(2)}) collective-permute-start(bf16[2,4,16,640]{3,2,1,0:T(8,128)(2,1)S(1)} %join_line.1.refs_0_), channel_id=1, source_target_pairs={{0,12},{1,13},{2,14},{3,15},{4,8},{5,9},{6,10},{7,11},{8,4},{9,5},... | collective-permute-start | bytes 491528 | tf_op jit(solution)/shard_map/gather_keys/ppermute | solution.py:274
  22.6 8.0 %collective-permute-start.2 = (f32[24,256]{1,0:T(8,128)}, f32[24,256]{1,0:T(8,128)S(1)}, u32[]{:S(2)}, u32[]{:S(2)}) collective-permute-start(f32[24,256]{1,0:T(8,128)} %bitcast.14), channel_id=1, source_target_pairs={{0,64},{64,0},{1,65},{65,1},{2,66},{66,2},{3,67},{67,3},{4,68},{68... | collective-permute-start | bytes 73736 | tf_op jit(solution)/shard_map/gather_keys/swap_queries/ppermute | solution.py:298
  26.7 8.4 %collective-permute-start.12 = (bf16[272,512]{1,0:T(8,128)(2,1)}, bf16[272,512]{1,0:T(8,128)(2,1)}, u32[]{:S(2)}, u32[]{:S(2)}) collective-permute-start(bf16[272,512]{1,0:T(8,128)(2,1)} %bitcast.6.kv0), channel_id=1, source_target_pairs={{0,2},{1,3},{2,0},{3,1},{4,6},{5,7},{6,4},{7,5},{8,10},{9,11},{10,... | collective-permute-start | bytes 835592 | tf_op jit(solution)/shard_map/gather_keys/ppermute | solution.py:274
  29.9 8.5 %collective-permute-start.13 = (bf16[272,512]{1,0:T(8,128)(2,1)}, bf16[272,512]{1,0:T(8,128)(2,1)}, u32[]{:S(2)}, u32[]{:S(2)}) collective-permute-start(bf16[272,512]{1,0:T(8,128)(2,1)} %bitcast.6.kv0), channel_id=1, source_target_pairs={{0,1},{1,0},{2,3},{3,2},{4,5},{5,4},{6,7},{7,6},{8,9},{9,8},{10,11... | collective-permute-start | bytes 835592 | tf_op jit(solution)/shard_map/gather_keys/ppermute | solution.py:274
  30.5 8.4 %collective-permute-start.14 = (bf16[272,512]{1,0:T(8,128)(2,1)}, bf16[272,512]{1,0:T(8,128)(2,1)}, u32[]{:S(2)}, u32[]{:S(2)}) collective-permute-start(bf16[272,512]{1,0:T(8,128)(2,1)} %bitcast.6.kv0), channel_id=1, source_target_pairs={{0,3},{1,2},{2,1},{3,0},{4,7},{5,6},{6,5},{7,4},{8,11},{9,10},{10,... | collective-permute-start | bytes 835592 | tf_op jit(solution)/shard_map/gather_keys/ppermute | solution.py:274
  35.0 21.7 %collective-permute-start.10 = (bf16[272,512]{1,0:T(8,128)(2,1)S(1)}, bf16[272,512]{1,0:T(8,128)(2,1)S(1)}, u32[]{:S(2)}, u32[]{:S(2)}) collective-permute-start(bf16[272,512]{1,0:T(8,128)(2,1)S(1)} %bitcast.9), channel_id=1, source_target_pairs={{0,1},{1,0},{2,3},{3,2},{4,5},{5,4},{6,7},{7,6},{8,9},{9,8},{10,11... | collective-permute-start | bytes 835592 | tf_op jit(solution)/shard_map/gather_keys/ppermute | solution.py:274
  38.4 20.5 %collective-permute-start.11 = (bf16[272,512]{1,0:T(8,128)(2,1)S(1)}, bf16[272,512]{1,0:T(8,128)(2,1)S(1)}, u32[]{:S(2)}, u32[]{:S(2)}) collective-permute-start(bf16[272,512]{1,0:T(8,128)(2,1)S(1)} %bitcast.10), channel_id=1, source_target_pairs={{0,3},{1,2},{2,1},{3,0},{4,7},{5,6},{6,5},{7,4},{8,11},{9,10},{10,... | collective-permute-start | bytes 835592 | tf_op jit(solution)/shard_map/gather_keys/ppermute | solution.py:274
  38.9 20.0 %collective-permute-start.9 = (bf16[272,512]{1,0:T(8,128)(2,1)S(1)}, bf16[272,512]{1,0:T(8,128)(2,1)S(1)}, u32[]{:S(2)}, u32[]{:S(2)}) collective-permute-start(bf16[272,512]{1,0:T(8,128)(2,1)S(1)} %bitcast.11), channel_id=1, source_target_pairs={{0,2},{1,3},{2,0},{3,1},{4,6},{5,7},{6,4},{7,5},{8,10},{9,11},{10,... | collective-permute-start | bytes 835592 | tf_op jit(solution)/shard_map/gather_keys/ppermute | solution.py:274
  54.7 16.6 %collective-permute-start.15 = (bf16[4,4,2,16,256]{4,3,2,1,0:T(8,128)(2,1)}, bf16[4,4,2,16,256]{4,3,2,1,0:T(8,128)(2,1)S(1)}, u32[]{:S(2)}, u32[]{:S(2)}) collective-permute-start(bf16[4,4,2,16,256]{4,3,2,1,0:T(8,128)(2,1)} %get-tuple-element.61), channel_id=1, source_target_pairs={{0,2},{1,3},{2,0},{3,1},{4,6},{5,7},{6,4},{7,5},{8,10},{9,11},{10,... | collective-permute-start | bytes 786440 | tf_op jit(solution)/shard_map/scatter_grads/ppermute | solution.py:274
  55.4 16.0 %collective-permute-start.16 = (bf16[4,4,2,16,256]{4,3,2,1,0:T(8,128)(2,1)}, bf16[4,4,2,16,256]{4,3,2,1,0:T(8,128)(2,1)S(1)}, u32[]{:S(2)}, u32[]{:S(2)}) collective-permute-start(bf16[4,4,2,16,256]{4,3,2,1,0:T(8,128)(2,1)} %get-tuple-element.62), channel_id=1, source_target_pairs={{0,1},{1,0},{2,3},{3,2},{4,5},{5,4},{6,7},{7,6},{8,9},{9,8},{10,11... | collective-permute-start | bytes 786440 | tf_op jit(solution)/shard_map/scatter_grads/ppermute | solution.py:274
  56.7 14.7 %collective-permute-start.17 = (bf16[4,4,2,16,256]{4,3,2,1,0:T(8,128)(2,1)}, bf16[4,4,2,16,256]{4,3,2,1,0:T(8,128)(2,1)S(1)}, u32[]{:S(2)}, u32[]{:S(2)}) collective-permute-start(bf16[4,4,2,16,256]{4,3,2,1,0:T(8,128)(2,1)} %get-tuple-element.63), channel_id=1, source_target_pairs={{0,3},{1,2},{2,1},{3,0},{4,7},{5,6},{6,5},{7,4},{8,11},{9,10},{10,... | collective-permute-start | bytes 786440 | tf_op jit(solution)/shard_map/scatter_grads/ppermute | solution.py:274
  71.6 15.6 %collective-permute-start.22 = (f32[256,1536]{1,0:T(8,128)}, f32[256,1536]{1,0:T(8,128)S(1)}, u32[]{:S(2)}, u32[]{:S(2)}) collective-permute-start(f32[256,1536]{1,0:T(8,128)} %get-tuple-element.83), channel_id=1, source_target_pairs={{0,64},{64,0},{1,65},{65,1},{2,66},{66,2},{3,67},{67,3},{4,68},{68... | collective-permute-start | bytes 4718600 | tf_op jit(solution)/shard_map/swap_query_grads/ppermute | solution.py:298
  71.9 8.3 %collective-permute-start.18 = (bf16[4,4,2,16,256]{4,3,2,1,0:T(8,128)(2,1)}, bf16[4,4,2,16,256]{4,3,2,1,0:T(8,128)(2,1)S(1)}, u32[]{:S(2)}, u32[]{:S(2)}) collective-permute-start(bf16[4,4,2,16,256]{4,3,2,1,0:T(8,128)(2,1)} %get-tuple-element.65), channel_id=1, source_target_pairs={{0,2},{1,3},{2,0},{3,1},{4,6},{5,7},{6,4},{7,5},{8,10},{9,11},{10,... | collective-permute-start | bytes 786440 | tf_op jit(solution)/shard_map/scatter_grads/ppermute | solution.py:274
  72.7 8.5 %collective-permute-start.19 = (bf16[4,4,2,16,256]{4,3,2,1,0:T(8,128)(2,1)}, bf16[4,4,2,16,256]{4,3,2,1,0:T(8,128)(2,1)S(1)}, u32[]{:S(2)}, u32[]{:S(2)}) collective-permute-start(bf16[4,4,2,16,256]{4,3,2,1,0:T(8,128)(2,1)} %get-tuple-element.66), channel_id=1, source_target_pairs={{0,1},{1,0},{2,3},{3,2},{4,5},{5,4},{6,7},{7,6},{8,9},{9,8},{10,11... | collective-permute-start | bytes 786440 | tf_op jit(solution)/shard_map/scatter_grads/ppermute | solution.py:274
  73.8 9.0 %collective-permute-start.20 = (bf16[4,4,2,16,256]{4,3,2,1,0:T(8,128)(2,1)}, bf16[4,4,2,16,256]{4,3,2,1,0:T(8,128)(2,1)S(1)}, u32[]{:S(2)}, u32[]{:S(2)}) collective-permute-start(bf16[4,4,2,16,256]{4,3,2,1,0:T(8,128)(2,1)} %get-tuple-element.67), channel_id=1, source_target_pairs={{0,3},{1,2},{2,1},{3,0},{4,7},{5,6},{6,5},{7,4},{8,11},{9,10},{10,... | collective-permute-start | bytes 786440 | tf_op jit(solution)/shard_map/scatter_grads/ppermute | solution.py:274
  83.0 6.6 %collective-permute-start.21 = (bf16[2,4,2,16,256]{4,3,2,1,0:T(8,128)(2,1)S(1)}, bf16[2,4,2,16,256]{4,3,2,1,0:T(8,128)(2,1)S(1)}, u32[]{:S(2)}, u32[]{:S(2)}) collective-permute-start(bf16[2,4,2,16,256]{4,3,2,1,0:T(8,128)(2,1)S(1)} %get-tuple-element.81), channel_id=1, source_target_pairs={{0,8},{1,9},{2,10},{3,11},{4,12},{5,13},{6,14},{7,15},{8,0},{9,1},... | collective-permute-start | bytes 393224 | tf_op jit(solution)/shard_map/scatter_grads/ppermute | solution.py:274
  84.5 5.0 %collective-permute-start.23 = (bf16[2,4,2,16,256]{4,3,2,1,0:T(8,128)(2,1)S(1)}, bf16[2,4,2,16,256]{4,3,2,1,0:T(8,128)(2,1)S(1)}, u32[]{:S(2)}, u32[]{:S(2)}) collective-permute-start(bf16[2,4,2,16,256]{4,3,2,1,0:T(8,128)(2,1)S(1)} %get-tuple-element.87), channel_id=1, source_target_pairs={{0,4},{1,5},{2,6},{3,7},{4,0},{5,1},{6,2},{7,3},{8,12},{9,13},{10,... | collective-permute-start | bytes 393224 | tf_op jit(solution)/shard_map/scatter_grads/ppermute | solution.py:274
  85.1 6.2 %collective-permute-start.24 = (bf16[2,4,2,16,256]{4,3,2,1,0:T(8,128)(2,1)S(1)}, bf16[2,4,2,16,256]{4,3,2,1,0:T(8,128)(2,1)S(1)}, u32[]{:S(2)}, u32[]{:S(2)}) collective-permute-start(bf16[2,4,2,16,256]{4,3,2,1,0:T(8,128)(2,1)S(1)} %get-tuple-element.88), channel_id=1, source_target_pairs={{0,12},{1,13},{2,14},{3,15},{4,8},{5,9},{6,10},{7,11},{8,4},{9,5},... | collective-permute-start | bytes 393224 | tf_op jit(solution)/shard_map/scatter_grads/ppermute | solution.py:274
  (3 other events, 28.2 us)

commit v6 on v5

--- a/solution.py
+++ b/solution.py
@@ -311,7 +311,9 @@
         block = line([payload] + [z_shift(payload, by) for by in (3, 1, 2)])
         with jax.named_scope("swap_queries"):
             q_oth, g_oth, lse_oth = (swap(v) for v in (q_sent, g_sent, lse))
-        own = pieces_of([block] + plane_swaps([block] * 3, 0))
+        blocks = [block] + plane_swaps([block] * 3, 0)
+        blocks, q_oth, g_oth = lax.optimization_barrier((blocks, q_oth, g_oth))
+        own = pieces_of(blocks)
         pieces = []
         for piece in own:
             piece = piece.reshape(BLOCK + SLAB, 2 * COLS)

time: 104 us -> 101 us (0.971)
  waiting for transfers between devices: 25 us -> 21.2 us
    ppermute x18, waiting for transfers between devices: 19.3 us -> 15.5 us  [plane_swap(): return lax.ppermute(value, ('core', 'x', 'y'), pairs)]
where the time goes in v6:
time: 101 us
  starting transfers between devices  35.1 us (35%)
  Pallas kernels  27.8 us (28%)
  waiting for transfers between devices  21.2 us (21%)
  blocking collectives  12.1 us (12%)
  local copies, waits for them, and re-layouts  2.66 us (3%)
  between operations  2.07 us (2%)
    ppermute x18, starting transfers between devices, plane_swap(): return lax.ppermute(value, ('core', 'x', 'y'), pairs)  26.9 us
    pallas_call x2, Pallas kernels, attention(): pl.pallas_call(attention_kernel, grid_spec=pltpu.PrefetchScalarGridSpec(n...  25.3 us
    ppermute x18, waiting for transfers between devices, plane_swap(): return lax.ppermute(value, ('core', 'x', 'y'), pairs)  15.5 us
    all_to_all x1, blocking collectives, per_device(): dk, dv = finish(lax.all_to_all(small, ('zl', 'zh'), 0, 0))  12.1 us
    ppermute x3, starting transfers between devices, z_shift(): return lax.ppermute(value, ('zl', 'zh'), pairs)  7.31 us
    ppermute x3, waiting for transfers between devices, z_shift(): return lax.ppermute(value, ('zl', 'zh'), pairs)  5.66 us
  transfers between devices with their start and end apart: 25, of which 13 were waited for; matrix products, arithmetic and copies ran while one was open for 3% of the time, Pallas kernels for 25%

profile of v6, /device:TPU:32, one launch (start us, length us, event | category | flops | bytes accessed | tf_op | source)
XLA Modules:
  0.0 101.1 jit_solution(14531327715340477328)
XLA Ops:
  2.7 5.8 %collective-permute-start = (bf16[2,16,640]{2,1,0:T(8,128)(2,1)S(1)}, bf16[2,16,640]{2,1,0:T(8,128)(2,1)S(1)}, u32[]{:S(2)}, u32[]{:S(2)}) collective-permute-start(bf16[2,16,640]{2,1,0:T(8,128)(2,1)S(1)} %pack_keys_values.1.own), channel_id=1, source_target_pairs={{0,160},{128,32},{16,176},{144,48},{32,128},{160,0},{48,144},{176,... | collective-permute-start | bytes 122888 | tf_op jit(solution)/shard_map/gather_keys/ppermute | solution.py:287
  8.5 1.0 %collective-permute-start.1 = (bf16[2,16,640]{2,1,0:T(8,128)(2,1)S(1)}, bf16[2,16,640]{2,1,0:T(8,128)(2,1)S(1)}, u32[]{:S(2)}, u32[]{:S(2)}) collective-permute-start(bf16[2,16,640]{2,1,0:T(8,128)(2,1)S(1)} %pack_keys_values.1.own), channel_id=1, source_target_pairs={{0,176},{128,16},{16,128},{144,32},{32,144},{160,48},{48,160},{176... | collective-permute-start | bytes 122888 | tf_op jit(solution)/shard_map/gather_keys/ppermute | solution.py:287
  10.5 2.2 %collective-permute-done.1.near = bf16[2,16,640]{2,1,0:T(8,128)(2,1)S(1)} collective-permute-done((bf16[2,16,640]{2,1,0:T(8,128)(2,1)S(1)}, bf16[2,16,640]{2,1,0:T(8,128)(2,1)S(1)}, u32[]{:S(2)}, u32[]{:S(2)}) %collective-permute-start.1) | collective-permute-done | bytes 40992 | tf_op jit(solution)/shard_map/gather_keys/ppermute | solution.py:287
  12.7 3.0 %collective-permute-done.2.next_ = bf16[2,16,640]{2,1,0:T(8,128)(2,1)S(1)} collective-permute-done((bf16[2,16,640]{2,1,0:T(8,128)(2,1)S(1)}, bf16[2,16,640]{2,1,0:T(8,128)(2,1)S(1)}, u32[]{:S(2)}, u32[]{:S(2)}) %collective-permute-start.2) | collective-permute-done | bytes 40992 | tf_op jit(solution)/shard_map/gather_keys/ppermute | solution.py:287
  15.7 3.1 %collective-permute-start.3 = (bf16[2,4,16,640]{3,2,1,0:T(8,128)(2,1)S(1)}, bf16[2,4,16,640]{3,2,1,0:T(8,128)(2,1)S(1)}, u32[]{:S(2)}, u32[]{:S(2)}) collective-permute-start(bf16[2,4,16,640]{3,2,1,0:T(8,128)(2,1)S(1)} %join_line.1.refs_0_), channel_id=1, source_target_pairs={{0,8},{1,9},{2,10},{3,11},{4,12},{5,13},{6,14},{7,15},{8,0},{9,1},... | collective-permute-start | bytes 491528 | tf_op jit(solution)/shard_map/gather_keys/ppermute | solution.py:274
  19.9 2.7 %collective-permute-done.3.refs_1_ = bf16[2,4,16,640]{3,2,1,0:T(8,128)(2,1)S(1)} collective-permute-done((bf16[2,4,16,640]{3,2,1,0:T(8,128)(2,1)S(1)}, bf16[2,4,16,640]{3,2,1,0:T(8,128)(2,1)S(1)}, u32[]{:S(2)}, u32[]{:S(2)}) %collective-permute-start.3) | collective-permute-done | bytes 163872 | tf_op jit(solution)/shard_map/gather_keys/ppermute | solution.py:274
  22.6 1.8 %collective-permute-done.4.refs_2_ = bf16[2,4,16,640]{3,2,1,0:T(8,128)(2,1)S(1)} collective-permute-done((bf16[2,4,16,640]{3,2,1,0:T(8,128)(2,1)S(1)}, bf16[2,4,16,640]{3,2,1,0:T(8,128)(2,1)S(1)}, u32[]{:S(2)}, u32[]{:S(2)}) %collective-permute-start.4) | collective-permute-done | bytes 163872 | tf_op jit(solution)/shard_map/gather_keys/ppermute | solution.py:274
  24.4 1.5 %collective-permute-done.5.refs_3_ = bf16[2,4,16,640]{3,2,1,0:T(8,128)(2,1)S(1)} collective-permute-done((bf16[2,4,16,640]{3,2,1,0:T(8,128)(2,1)S(1)}, bf16[2,4,16,640]{3,2,1,0:T(8,128)(2,1)S(1)}, u32[]{:S(2)}, u32[]{:S(2)}) %collective-permute-start.5) | collective-permute-done | bytes 163872 | tf_op jit(solution)/shard_map/gather_keys/ppermute | solution.py:274
  26.7 3.2 %collective-permute-start.12 = (bf16[272,512]{1,0:T(8,128)(2,1)}, bf16[272,512]{1,0:T(8,128)(2,1)}, u32[]{:S(2)}, u32[]{:S(2)}) collective-permute-start(bf16[272,512]{1,0:T(8,128)(2,1)} %bitcast.6.kv0), channel_id=1, source_target_pairs={{0,2},{1,3},{2,0},{3,1},{4,6},{5,7},{6,4},{7,5},{8,10},{9,11},{10,... | collective-permute-start | bytes 835592 | tf_op jit(solution)/shard_map/gather_keys/ppermute | solution.py:274
  32.5 1.5 %collective-permute-start.10 = (bf16[272,512]{1,0:T(8,128)(2,1)S(1)}, bf16[272,512]{1,0:T(8,128)(2,1)S(1)}, u32[]{:S(2)}, u32[]{:S(2)}) collective-permute-start(bf16[272,512]{1,0:T(8,128)(2,1)S(1)} %bitcast.9), channel_id=1, source_target_pairs={{0,1},{1,0},{2,3},{3,2},{4,5},{5,4},{6,7},{7,6},{8,9},{9,8},{10,11... | collective-permute-start | bytes 835592 | tf_op jit(solution)/shard_map/gather_keys/ppermute | solution.py:274
  34.0 2.2 %collective-permute-start.11 = (bf16[272,512]{1,0:T(8,128)(2,1)S(1)}, bf16[272,512]{1,0:T(8,128)(2,1)S(1)}, u32[]{:S(2)}, u32[]{:S(2)}) collective-permute-start(bf16[272,512]{1,0:T(8,128)(2,1)S(1)} %bitcast.10), channel_id=1, source_target_pairs={{0,3},{1,2},{2,1},{3,0},{4,7},{5,6},{6,5},{7,4},{8,11},{9,10},{10,... | collective-permute-start | bytes 835592 | tf_op jit(solution)/shard_map/gather_keys/ppermute | solution.py:274
  36.2 2.2 %collective-permute-start.9 = (bf16[272,512]{1,0:T(8,128)(2,1)S(1)}, bf16[272,512]{1,0:T(8,128)(2,1)S(1)}, u32[]{:S(2)}, u32[]{:S(2)}) collective-permute-start(bf16[272,512]{1,0:T(8,128)(2,1)S(1)} %bitcast.11), channel_id=1, source_target_pairs={{0,2},{1,3},{2,0},{3,1},{4,6},{5,7},{6,4},{7,5},{8,10},{9,11},{10,... | collective-permute-start | bytes 835592 | tf_op jit(solution)/shard_map/gather_keys/ppermute | solution.py:274
  38.6 12.9 %attention_backward.2 = (f32[256,3072]{1,0:T(8,128)}, f32[256,1536]{1,0:T(8,128)}, f32[4,4,2,16,256]{4,3,2,1,0:T(8,128)}, bf16[4,4,2,16,256]{4,3,2,1,0:T(8,128)(...) custom-call(s32[3]{0:T(128)S(1)} %pad_add_fusion.meta, bf16[256,3072]{1,0:T(8,128)(2,1)} %bitcast.17, ...), custom_call_target="tpu_custom_call" | custom-call | flops 8000000000 | bytes 8388608 | tf_op jit(solution)/shard_map/attention_backward/pallas_call | solution.py:119
  51.5 2.7 %collective-permute-start.15 = (bf16[4,4,2,16,256]{4,3,2,1,0:T(8,128)(2,1)}, bf16[4,4,2,16,256]{4,3,2,1,0:T(8,128)(2,1)S(1)}, u32[]{:S(2)}, u32[]{:S(2)}) collective-permute-start(bf16[4,4,2,16,256]{4,3,2,1,0:T(8,128)(2,1)} %get-tuple-element.73), channel_id=1, source_target_pairs={{0,2},{1,3},{2,0},{3,1},{4,6},{5,7},{6,4},{7,5},{8,10},{9,11},{10,... | collective-permute-start | bytes 786440 | tf_op jit(solution)/shard_map/scatter_grads/ppermute | solution.py:274
  55.7 12.4 %attention_backward.3 = (f32[256,3072]{1,0:T(8,128)}, f32[256,1536]{1,0:T(8,128)}, f32[4,4,2,16,256]{4,3,2,1,0:T(8,128)}, bf16[4,4,2,16,256]{4,3,2,1,0:T(8,128)(...) custom-call(s32[3]{0:T(128)S(1)} %pad_add_fusion.meta, ...), custom_call_target="tpu_custom_call", output_to_operand_aliasing={{0}: (11, {}), {1}: (12, {})} | custom-call | flops 8000000000 | bytes 8388608 | tf_op jit(solution)/shard_map/attention_backward/pallas_call | solution.py:119
  68.7 2.7 %collective-permute-start.18 = (bf16[4,4,2,16,256]{4,3,2,1,0:T(8,128)(2,1)}, bf16[4,4,2,16,256]{4,3,2,1,0:T(8,128)(2,1)S(1)}, u32[]{:S(2)}, u32[]{:S(2)}) collective-permute-start(bf16[4,4,2,16,256]{4,3,2,1,0:T(8,128)(2,1)} %get-tuple-element.77), channel_id=1, source_target_pairs={{0,2},{1,3},{2,0},{3,1},{4,6},{5,7},{6,4},{7,5},{8,10},{9,11},{10,... | collective-permute-start | bytes 786440 | tf_op jit(solution)/shard_map/scatter_grads/ppermute | solution.py:274
  72.9 4.0 %collective-permute-done.18.refs_1_ = bf16[4,4,2,16,256]{4,3,2,1,0:T(8,128)(2,1)S(1)} collective-permute-done((bf16[4,4,2,16,256]{4,3,2,1,0:T(8,128)(2,1)}, bf16[4,4,2,16,256]{4,3,2,1,0:T(8,128)(2,1)S(1)}, u32[]{:S(2)}, u32[]{:S(2)}) %collective-permute-start.18) | collective-permute-done | bytes 262176 | tf_op jit(solution)/shard_map/scatter_grads/ppermute | solution.py:274
  76.8 2.6 %collective-permute-done.19.refs_2_ = bf16[4,4,2,16,256]{4,3,2,1,0:T(8,128)(2,1)S(1)} collective-permute-done((bf16[4,4,2,16,256]{4,3,2,1,0:T(8,128)(2,1)}, bf16[4,4,2,16,256]{4,3,2,1,0:T(8,128)(2,1)S(1)}, u32[]{:S(2)}, u32[]{:S(2)}) %collective-permute-start.19) | collective-permute-done | bytes 262176 | tf_op jit(solution)/shard_map/scatter_grads/ppermute | solution.py:274
  79.9 1.5 %collective-permute-start.21 = (bf16[2,4,2,16,256]{4,3,2,1,0:T(8,128)(2,1)S(1)}, bf16[2,4,2,16,256]{4,3,2,1,0:T(8,128)(2,1)S(1)}, u32[]{:S(2)}, u32[]{:S(2)}) collective-permute-start(bf16[2,4,2,16,256]{4,3,2,1,0:T(8,128)(2,1)S(1)} %get-tuple-element.93), channel_id=1, source_target_pairs={{0,8},{1,9},{2,10},{3,11},{4,12},{5,13},{6,14},{7,15},{8,0},{9,1},... | collective-permute-start | bytes 393224 | tf_op jit(solution)/shard_map/scatter_grads/ppermute | solution.py:274
  82.1 2.0 %collective-permute-start.24 = (bf16[2,4,2,16,256]{4,3,2,1,0:T(8,128)(2,1)S(1)}, bf16[2,4,2,16,256]{4,3,2,1,0:T(8,128)(2,1)S(1)}, u32[]{:S(2)}, u32[]{:S(2)}) collective-permute-start(bf16[2,4,2,16,256]{4,3,2,1,0:T(8,128)(2,1)S(1)} %get-tuple-element.100), channel_id=1, source_target_pairs={{0,12},{1,13},{2,14},{3,15},{4,8},{5,9},{6,10},{7,11},{8,4},{9,5},... | collective-permute-start | bytes 393224 | tf_op jit(solution)/shard_map/scatter_grads/ppermute | solution.py:274
  84.1 0.9 slice_dynamic-update-slice_fusion.1
  85.1 0.9 slice_dynamic-update-slice_fusion
  86.5 1.8 %collective-permute-done.24 = bf16[2,4,2,16,256]{4,3,2,1,0:T(8,128)(2,1)S(1)} collective-permute-done((bf16[2,4,2,16,256]{4,3,2,1,0:T(8,128)(2,1)S(1)}, bf16[2,4,2,16,256]{4,3,2,1,0:T(8,128)(2,1)S(1)}, u32[]{:S(2)}, u32[]{:S(2)}) %collective-permute-start.24) | collective-permute-done | bytes 131104 | tf_op jit(solution)/shard_map/scatter_grads/ppermute | solution.py:274
  88.3 12.1 %all_to_all.5.got = bf16[8,2,16,256]{3,2,1,0:T(8,128)(2,1)S(1)} all-to-all(bf16[8,2,16,256]{3,2,1,0:T(8,128)(2,1)S(1)} %bitcast.13), channel_id=1, replica_groups=mesh['zl'=2,'core'=2,'zh'=4,'x'=4,'y'=4] {'zl','zh'}, dimensions={0} | all-to-all | bytes 262144 | tf_op jit(solution)/shard_map/scatter_grads/all_to_all | solution.py:350
  (45 shorter events, 12.3 us)
Async XLA Ops:
  2.1 23.8 %collective-permute-start.6 = (bf16[256,3072]{1,0:T(8,128)(2,1)}, bf16[256,3072]{1,0:T(8,128)(2,1)S(1)}, u32[]{:S(2)}, u32[]{:S(2)}) collective-permute-start(bf16[256,3072]{1,0:T(8,128)(2,1)} %bitcast.16), channel_id=1, source_target_pairs={{0,64},{64,0},{1,65},{65,1},{2,66},{66,2},{3,67},{67,3},{4,68},{68... | collective-permute-start | bytes 4718600 | tf_op jit(solution)/shard_map/gather_keys/swap_queries/ppermute | solution.py:298
  2.2 23.7 %collective-permute-start.7 = (bf16[256,3072]{1,0:T(8,128)(2,1)}, bf16[256,3072]{1,0:T(8,128)(2,1)S(1)}, u32[]{:S(2)}, u32[]{:S(2)}) collective-permute-start(bf16[256,3072]{1,0:T(8,128)(2,1)} %bitcast.19), channel_id=1, source_target_pairs={{0,64},{64,0},{1,65},{65,1},{2,66},{66,2},{3,67},{67,3},{4,68},{68... | collective-permute-start | bytes 4718600 | tf_op jit(solution)/shard_map/gather_keys/swap_queries/ppermute | solution.py:298
  2.7 7.8 %collective-permute-start = (bf16[2,16,640]{2,1,0:T(8,128)(2,1)S(1)}, bf16[2,16,640]{2,1,0:T(8,128)(2,1)S(1)}, u32[]{:S(2)}, u32[]{:S(2)}) collective-permute-start(bf16[2,16,640]{2,1,0:T(8,128)(2,1)S(1)} %pack_keys_values.1.own), channel_id=1, source_target_pairs={{0,160},{128,32},{16,176},{144,48},{32,128},{160,0},{48,144},{176,... | collective-permute-start | bytes 122888 | tf_op jit(solution)/shard_map/gather_keys/ppermute | solution.py:287
  8.5 4.2 %collective-permute-start.1 = (bf16[2,16,640]{2,1,0:T(8,128)(2,1)S(1)}, bf16[2,16,640]{2,1,0:T(8,128)(2,1)S(1)}, u32[]{:S(2)}, u32[]{:S(2)}) collective-permute-start(bf16[2,16,640]{2,1,0:T(8,128)(2,1)S(1)} %pack_keys_values.1.own), channel_id=1, source_target_pairs={{0,176},{128,16},{16,128},{144,32},{32,144},{160,48},{48,160},{176... | collective-permute-start | bytes 122888 | tf_op jit(solution)/shard_map/gather_keys/ppermute | solution.py:287
  9.5 6.1 %collective-permute-start.2 = (bf16[2,16,640]{2,1,0:T(8,128)(2,1)S(1)}, bf16[2,16,640]{2,1,0:T(8,128)(2,1)S(1)}, u32[]{:S(2)}, u32[]{:S(2)}) collective-permute-start(bf16[2,16,640]{2,1,0:T(8,128)(2,1)S(1)} %pack_keys_values.1.own), channel_id=1, source_target_pairs={{0,48},{128,144},{16,0},{144,160},{32,16},{160,176},{48,32},{176,1... | collective-permute-start | bytes 122888 | tf_op jit(solution)/shard_map/gather_keys/ppermute | solution.py:287
  15.7 6.9 %collective-permute-start.3 = (bf16[2,4,16,640]{3,2,1,0:T(8,128)(2,1)S(1)}, bf16[2,4,16,640]{3,2,1,0:T(8,128)(2,1)S(1)}, u32[]{:S(2)}, u32[]{:S(2)}) collective-permute-start(bf16[2,4,16,640]{3,2,1,0:T(8,128)(2,1)S(1)} %join_line.1.refs_0_), channel_id=1, source_target_pairs={{0,8},{1,9},{2,10},{3,11},{4,12},{5,13},{6,14},{7,15},{8,0},{9,1},... | collective-permute-start | bytes 491528 | tf_op jit(solution)/shard_map/gather_keys/ppermute | solution.py:274
  18.8 5.6 %collective-permute-start.4 = (bf16[2,4,16,640]{3,2,1,0:T(8,128)(2,1)S(1)}, bf16[2,4,16,640]{3,2,1,0:T(8,128)(2,1)S(1)}, u32[]{:S(2)}, u32[]{:S(2)}) collective-permute-start(bf16[2,4,16,640]{3,2,1,0:T(8,128)(2,1)S(1)} %join_line.1.refs_0_), channel_id=1, source_target_pairs={{0,4},{1,5},{2,6},{3,7},{4,0},{5,1},{6,2},{7,3},{8,12},{9,13},{10,... | collective-permute-start | bytes 491528 | tf_op jit(solution)/shard_map/gather_keys/ppermute | solution.py:274
  19.4 6.5 %collective-permute-start.5 = (bf16[2,4,16,640]{3,2,1,0:T(8,128)(2,1)S(1)}, bf16[2,4,16,640]{3,2,1,0:T(8,128)(2,1)S(1)}, u32[]{:S(2)}, u32[]{:S(2)}) collective-permute-start(bf16[2,4,16,640]{3,2,1,0:T(8,128)(2,1)S(1)} %join_line.1.refs_0_), channel_id=1, source_target_pairs={{0,12},{1,13},{2,14},{3,15},{4,8},{5,9},{6,10},{7,11},{8,4},{9,5},... | collective-permute-start | bytes 491528 | tf_op jit(solution)/shard_map/gather_keys/ppermute | solution.py:274
  26.7 9.5 %collective-permute-start.12 = (bf16[272,512]{1,0:T(8,128)(2,1)}, bf16[272,512]{1,0:T(8,128)(2,1)}, u32[]{:S(2)}, u32[]{:S(2)}) collective-permute-start(bf16[272,512]{1,0:T(8,128)(2,1)} %bitcast.6.kv0), channel_id=1, source_target_pairs={{0,2},{1,3},{2,0},{3,1},{4,6},{5,7},{6,4},{7,5},{8,10},{9,11},{10,... | collective-permute-start | bytes 835592 | tf_op jit(solution)/shard_map/gather_keys/ppermute | solution.py:274
  29.9 8.5 %collective-permute-start.13 = (bf16[272,512]{1,0:T(8,128)(2,1)}, bf16[272,512]{1,0:T(8,128)(2,1)}, u32[]{:S(2)}, u32[]{:S(2)}) collective-permute-start(bf16[272,512]{1,0:T(8,128)(2,1)} %bitcast.6.kv0), channel_id=1, source_target_pairs={{0,1},{1,0},{2,3},{3,2},{4,5},{5,4},{6,7},{7,6},{8,9},{9,8},{10,11... | collective-permute-start | bytes 835592 | tf_op jit(solution)/shard_map/gather_keys/ppermute | solution.py:274
  30.6 8.1 %collective-permute-start.14 = (bf16[272,512]{1,0:T(8,128)(2,1)}, bf16[272,512]{1,0:T(8,128)(2,1)}, u32[]{:S(2)}, u32[]{:S(2)}) collective-permute-start(bf16[272,512]{1,0:T(8,128)(2,1)} %bitcast.6.kv0), channel_id=1, source_target_pairs={{0,3},{1,2},{2,1},{3,0},{4,7},{5,6},{6,5},{7,4},{8,11},{9,10},{10,... | collective-permute-start | bytes 835592 | tf_op jit(solution)/shard_map/gather_keys/ppermute | solution.py:274
  32.5 22.4 %collective-permute-start.10 = (bf16[272,512]{1,0:T(8,128)(2,1)S(1)}, bf16[272,512]{1,0:T(8,128)(2,1)S(1)}, u32[]{:S(2)}, u32[]{:S(2)}) collective-permute-start(bf16[272,512]{1,0:T(8,128)(2,1)S(1)} %bitcast.9), channel_id=1, source_target_pairs={{0,1},{1,0},{2,3},{3,2},{4,5},{5,4},{6,7},{7,6},{8,9},{9,8},{10,11... | collective-permute-start | bytes 835592 | tf_op jit(solution)/shard_map/gather_keys/ppermute | solution.py:274
  34.0 21.7 %collective-permute-start.11 = (bf16[272,512]{1,0:T(8,128)(2,1)S(1)}, bf16[272,512]{1,0:T(8,128)(2,1)S(1)}, u32[]{:S(2)}, u32[]{:S(2)}) collective-permute-start(bf16[272,512]{1,0:T(8,128)(2,1)S(1)} %bitcast.10), channel_id=1, source_target_pairs={{0,3},{1,2},{2,1},{3,0},{4,7},{5,6},{6,5},{7,4},{8,11},{9,10},{10,... | collective-permute-start | bytes 835592 | tf_op jit(solution)/shard_map/gather_keys/ppermute | solution.py:274
  36.2 19.5 %collective-permute-start.9 = (bf16[272,512]{1,0:T(8,128)(2,1)S(1)}, bf16[272,512]{1,0:T(8,128)(2,1)S(1)}, u32[]{:S(2)}, u32[]{:S(2)}) collective-permute-start(bf16[272,512]{1,0:T(8,128)(2,1)S(1)} %bitcast.11), channel_id=1, source_target_pairs={{0,2},{1,3},{2,0},{3,1},{4,6},{5,7},{6,4},{7,5},{8,10},{9,11},{10,... | collective-permute-start | bytes 835592 | tf_op jit(solution)/shard_map/gather_keys/ppermute | solution.py:274
  51.5 16.6 %collective-permute-start.15 = (bf16[4,4,2,16,256]{4,3,2,1,0:T(8,128)(2,1)}, bf16[4,4,2,16,256]{4,3,2,1,0:T(8,128)(2,1)S(1)}, u32[]{:S(2)}, u32[]{:S(2)}) collective-permute-start(bf16[4,4,2,16,256]{4,3,2,1,0:T(8,128)(2,1)} %get-tuple-element.73), channel_id=1, source_target_pairs={{0,2},{1,3},{2,0},{3,1},{4,6},{5,7},{6,4},{7,5},{8,10},{9,11},{10,... | collective-permute-start | bytes 786440 | tf_op jit(solution)/shard_map/scatter_grads/ppermute | solution.py:274
  54.2 14.0 %collective-permute-start.16 = (bf16[4,4,2,16,256]{4,3,2,1,0:T(8,128)(2,1)}, bf16[4,4,2,16,256]{4,3,2,1,0:T(8,128)(2,1)S(1)}, u32[]{:S(2)}, u32[]{:S(2)}) collective-permute-start(bf16[4,4,2,16,256]{4,3,2,1,0:T(8,128)(2,1)} %get-tuple-element.74), channel_id=1, source_target_pairs={{0,1},{1,0},{2,3},{3,2},{4,5},{5,4},{6,7},{7,6},{8,9},{9,8},{10,11... | collective-permute-start | bytes 786440 | tf_op jit(solution)/shard_map/scatter_grads/ppermute | solution.py:274
  54.9 13.3 %collective-permute-start.17 = (bf16[4,4,2,16,256]{4,3,2,1,0:T(8,128)(2,1)}, bf16[4,4,2,16,256]{4,3,2,1,0:T(8,128)(2,1)S(1)}, u32[]{:S(2)}, u32[]{:S(2)}) collective-permute-start(bf16[4,4,2,16,256]{4,3,2,1,0:T(8,128)(2,1)} %get-tuple-element.75), channel_id=1, source_target_pairs={{0,3},{1,2},{2,1},{3,0},{4,7},{5,6},{6,5},{7,4},{8,11},{9,10},{10,... | collective-permute-start | bytes 786440 | tf_op jit(solution)/shard_map/scatter_grads/ppermute | solution.py:274
  68.4 15.8 %collective-permute-start.22 = (f32[256,1536]{1,0:T(8,128)}, f32[256,1536]{1,0:T(8,128)S(1)}, u32[]{:S(2)}, u32[]{:S(2)}) collective-permute-start(f32[256,1536]{1,0:T(8,128)} %get-tuple-element.95), channel_id=1, source_target_pairs={{0,64},{64,0},{1,65},{65,1},{2,66},{66,2},{3,67},{67,3},{4,68},{68... | collective-permute-start | bytes 4718600 | tf_op jit(solution)/shard_map/swap_query_grads/ppermute | solution.py:298
  68.7 8.2 %collective-permute-start.18 = (bf16[4,4,2,16,256]{4,3,2,1,0:T(8,128)(2,1)}, bf16[4,4,2,16,256]{4,3,2,1,0:T(8,128)(2,1)S(1)}, u32[]{:S(2)}, u32[]{:S(2)}) collective-permute-start(bf16[4,4,2,16,256]{4,3,2,1,0:T(8,128)(2,1)} %get-tuple-element.77), channel_id=1, source_target_pairs={{0,2},{1,3},{2,0},{3,1},{4,6},{5,7},{6,4},{7,5},{8,10},{9,11},{10,... | collective-permute-start | bytes 786440 | tf_op jit(solution)/shard_map/scatter_grads/ppermute | solution.py:274
  71.4 8.0 %collective-permute-start.19 = (bf16[4,4,2,16,256]{4,3,2,1,0:T(8,128)(2,1)}, bf16[4,4,2,16,256]{4,3,2,1,0:T(8,128)(2,1)S(1)}, u32[]{:S(2)}, u32[]{:S(2)}) collective-permute-start(bf16[4,4,2,16,256]{4,3,2,1,0:T(8,128)(2,1)} %get-tuple-element.78), channel_id=1, source_target_pairs={{0,1},{1,0},{2,3},{3,2},{4,5},{5,4},{6,7},{7,6},{8,9},{9,8},{10,11... | collective-permute-start | bytes 786440 | tf_op jit(solution)/shard_map/scatter_grads/ppermute | solution.py:274
  72.0 7.8 %collective-permute-start.20 = (bf16[4,4,2,16,256]{4,3,2,1,0:T(8,128)(2,1)}, bf16[4,4,2,16,256]{4,3,2,1,0:T(8,128)(2,1)S(1)}, u32[]{:S(2)}, u32[]{:S(2)}) collective-permute-start(bf16[4,4,2,16,256]{4,3,2,1,0:T(8,128)(2,1)} %get-tuple-element.79), channel_id=1, source_target_pairs={{0,3},{1,2},{2,1},{3,0},{4,7},{5,6},{6,5},{7,4},{8,11},{9,10},{10,... | collective-permute-start | bytes 786440 | tf_op jit(solution)/shard_map/scatter_grads/ppermute | solution.py:274
  79.9 6.6 %collective-permute-start.21 = (bf16[2,4,2,16,256]{4,3,2,1,0:T(8,128)(2,1)S(1)}, bf16[2,4,2,16,256]{4,3,2,1,0:T(8,128)(2,1)S(1)}, u32[]{:S(2)}, u32[]{:S(2)}) collective-permute-start(bf16[2,4,2,16,256]{4,3,2,1,0:T(8,128)(2,1)S(1)} %get-tuple-element.93), channel_id=1, source_target_pairs={{0,8},{1,9},{2,10},{3,11},{4,12},{5,13},{6,14},{7,15},{8,0},{9,1},... | collective-permute-start | bytes 393224 | tf_op jit(solution)/shard_map/scatter_grads/ppermute | solution.py:274
  81.5 5.0 %collective-permute-start.23 = (bf16[2,4,2,16,256]{4,3,2,1,0:T(8,128)(2,1)S(1)}, bf16[2,4,2,16,256]{4,3,2,1,0:T(8,128)(2,1)S(1)}, u32[]{:S(2)}, u32[]{:S(2)}) collective-permute-start(bf16[2,4,2,16,256]{4,3,2,1,0:T(8,128)(2,1)S(1)} %get-tuple-element.99), channel_id=1, source_target_pairs={{0,4},{1,5},{2,6},{3,7},{4,0},{5,1},{6,2},{7,3},{8,12},{9,13},{10,... | collective-permute-start | bytes 393224 | tf_op jit(solution)/shard_map/scatter_grads/ppermute | solution.py:274
  82.1 6.2 %collective-permute-start.24 = (bf16[2,4,2,16,256]{4,3,2,1,0:T(8,128)(2,1)S(1)}, bf16[2,4,2,16,256]{4,3,2,1,0:T(8,128)(2,1)S(1)}, u32[]{:S(2)}, u32[]{:S(2)}) collective-permute-start(bf16[2,4,2,16,256]{4,3,2,1,0:T(8,128)(2,1)S(1)} %get-tuple-element.100), channel_id=1, source_target_pairs={{0,12},{1,13},{2,14},{3,15},{4,8},{5,9},{6,10},{7,11},{8,4},{9,5},... | collective-permute-start | bytes 393224 | tf_op jit(solution)/shard_map/scatter_grads/ppermute | solution.py:274
  (3 other events, 25.7 us)

commit v7 on v6

--- a/solution.py
+++ b/solution.py
@@ -312,7 +312,10 @@
         with jax.named_scope("swap_queries"):
             q_oth, g_oth, lse_oth = (swap(v) for v in (q_sent, g_sent, lse))
         blocks = [block] + plane_swaps([block] * 3, 0)
-        blocks, q_oth, g_oth = lax.optimization_barrier((blocks, q_oth, g_oth))
+        wide = (KV_HEADS, 1, WIDE)
+        blocks, q_oth, g_oth, lse, lse_oth = lax.optimization_barrier(
+            (blocks, q_oth, g_oth, lse.reshape(wide), lse_oth.reshape(wide))
+        )
         own = pieces_of(blocks)
         pieces = []
         for piece in own:
@@ -320,8 +323,6 @@
             pieces.append([piece] + plane_swaps([piece] * 3, 1))
     a0 = jnp.where(core == 0, y, x)
     meta = jnp.stack([core, a0, query_starts[0]]).astype(jnp.int32)
-    wide = (KV_HEADS, 1, WIDE)
-    lse, lse_oth = lse.reshape(wide), lse_oth.reshape(wide)
     partly, sums = [], []
     for chunk in range(2):
         *partly, part0, part1, part2, part3 = attention(

time: 101 us -> 100 us (0.990)
  no operation moved by 1% of the time
where the time goes in v7:
time: 100 us; the launch traced here: 99.9 us
  starting transfers between devices  35.7 us (36%)
  Pallas kernels  26.8 us (27%)
  waiting for transfers between devices  20.4 us (20%)
  blocking collectives  12.1 us (12%)
  local copies, waits for them, and re-layouts  2.66 us (3%)
  between operations  2.06 us (2%)
    ppermute x18, starting transfers between devices, plane_swap(): return lax.ppermute(value, ('core', 'x', 'y'), pairs)  27.5 us
    pallas_call x2, Pallas kernels, attention(): pl.pallas_call(attention_kernel, grid_spec=pltpu.PrefetchScalarGridSpec(n...  25.1 us
    ppermute x18, waiting for transfers between devices, plane_swap(): return lax.ppermute(value, ('core', 'x', 'y'), pairs)  14.7 us
    all_to_all x1, blocking collectives, per_device(): dk, dv = finish(lax.all_to_all(small, ('zl', 'zh'), 0, 0))  12.1 us
    ppermute x3, starting transfers between devices, z_shift(): return lax.ppermute(value, ('zl', 'zh'), pairs)  7.31 us
    ppermute x3, waiting for transfers between devices, z_shift(): return lax.ppermute(value, ('zl', 'zh'), pairs)  5.66 us
  transfers between devices with their start and end apart: 25, of which 13 were waited for; matrix products, arithmetic and copies ran while one was open for 3% of the time, Pallas kernels for 25%

profile of v7, /device:TPU:32, one launch (start us, length us, event | category | flops | bytes accessed | tf_op | source)
XLA Modules:
  0.0 99.9 jit_solution(17414959148224243584)
XLA Ops:
  2.7 5.8 %collective-permute-start = (bf16[2,16,640]{2,1,0:T(8,128)(2,1)S(1)}, bf16[2,16,640]{2,1,0:T(8,128)(2,1)S(1)}, u32[]{:S(2)}, u32[]{:S(2)}) collective-permute-start(bf16[2,16,640]{2,1,0:T(8,128)(2,1)S(1)} %pack_keys_values.1.own), channel_id=1, source_target_pairs={{0,160},{128,32},{16,176},{144,48},{32,128},{160,0},{48,144},{176,... | collective-permute-start | bytes 122888 | tf_op jit(solution)/shard_map/gather_keys/ppermute | solution.py:287
  8.5 1.0 %collective-permute-start.1 = (bf16[2,16,640]{2,1,0:T(8,128)(2,1)S(1)}, bf16[2,16,640]{2,1,0:T(8,128)(2,1)S(1)}, u32[]{:S(2)}, u32[]{:S(2)}) collective-permute-start(bf16[2,16,640]{2,1,0:T(8,128)(2,1)S(1)} %pack_keys_values.1.own), channel_id=1, source_target_pairs={{0,176},{128,16},{16,128},{144,32},{32,144},{160,48},{48,160},{176... | collective-permute-start | bytes 122888 | tf_op jit(solution)/shard_map/gather_keys/ppermute | solution.py:287
  10.5 2.2 %collective-permute-done.1.near = bf16[2,16,640]{2,1,0:T(8,128)(2,1)S(1)} collective-permute-done((bf16[2,16,640]{2,1,0:T(8,128)(2,1)S(1)}, bf16[2,16,640]{2,1,0:T(8,128)(2,1)S(1)}, u32[]{:S(2)}, u32[]{:S(2)}) %collective-permute-start.1) | collective-permute-done | bytes 40992 | tf_op jit(solution)/shard_map/gather_keys/ppermute | solution.py:287
  12.7 3.0 %collective-permute-done.2.next_ = bf16[2,16,640]{2,1,0:T(8,128)(2,1)S(1)} collective-permute-done((bf16[2,16,640]{2,1,0:T(8,128)(2,1)S(1)}, bf16[2,16,640]{2,1,0:T(8,128)(2,1)S(1)}, u32[]{:S(2)}, u32[]{:S(2)}) %collective-permute-start.2) | collective-permute-done | bytes 40992 | tf_op jit(solution)/shard_map/gather_keys/ppermute | solution.py:287
  15.7 3.1 %collective-permute-start.3 = (bf16[2,4,16,640]{3,2,1,0:T(8,128)(2,1)S(1)}, bf16[2,4,16,640]{3,2,1,0:T(8,128)(2,1)S(1)}, u32[]{:S(2)}, u32[]{:S(2)}) collective-permute-start(bf16[2,4,16,640]{3,2,1,0:T(8,128)(2,1)S(1)} %join_line.1.refs_0_), channel_id=1, source_target_pairs={{0,8},{1,9},{2,10},{3,11},{4,12},{5,13},{6,14},{7,15},{8,0},{9,1},... | collective-permute-start | bytes 491528 | tf_op jit(solution)/shard_map/gather_keys/ppermute | solution.py:274
  20.7 1.9 %collective-permute-done.3.refs_1_ = bf16[2,4,16,640]{3,2,1,0:T(8,128)(2,1)S(1)} collective-permute-done((bf16[2,4,16,640]{3,2,1,0:T(8,128)(2,1)S(1)}, bf16[2,4,16,640]{3,2,1,0:T(8,128)(2,1)S(1)}, u32[]{:S(2)}, u32[]{:S(2)}) %collective-permute-start.3) | collective-permute-done | bytes 163872 | tf_op jit(solution)/shard_map/gather_keys/ppermute | solution.py:274
  22.6 1.8 %collective-permute-done.4.refs_2_ = bf16[2,4,16,640]{3,2,1,0:T(8,128)(2,1)S(1)} collective-permute-done((bf16[2,4,16,640]{3,2,1,0:T(8,128)(2,1)S(1)}, bf16[2,4,16,640]{3,2,1,0:T(8,128)(2,1)S(1)}, u32[]{:S(2)}, u32[]{:S(2)}) %collective-permute-start.4) | collective-permute-done | bytes 163872 | tf_op jit(solution)/shard_map/gather_keys/ppermute | solution.py:274
  24.4 1.5 %collective-permute-done.5.refs_3_ = bf16[2,4,16,640]{3,2,1,0:T(8,128)(2,1)S(1)} collective-permute-done((bf16[2,4,16,640]{3,2,1,0:T(8,128)(2,1)S(1)}, bf16[2,4,16,640]{3,2,1,0:T(8,128)(2,1)S(1)}, u32[]{:S(2)}, u32[]{:S(2)}) %collective-permute-start.5) | collective-permute-done | bytes 163872 | tf_op jit(solution)/shard_map/gather_keys/ppermute | solution.py:274
  26.0 3.3 %collective-permute-start.12 = (bf16[272,512]{1,0:T(8,128)(2,1)S(1)}, bf16[272,512]{1,0:T(8,128)(2,1)S(1)}, u32[]{:S(2)}, u32[]{:S(2)}) collective-permute-start(bf16[272,512]{1,0:T(8,128)(2,1)S(1)} %bitcast.13), channel_id=1, source_target_pairs={{0,2},{1,3},{2,0},{3,1},{4,6},{5,7},{6,4},{7,5},{8,10},{9,11},{10,... | collective-permute-start | bytes 835592 | tf_op jit(solution)/shard_map/gather_keys/ppermute | solution.py:274
  31.0 1.4 %collective-permute-start.10 = (bf16[272,512]{1,0:T(8,128)(2,1)S(1)}, bf16[272,512]{1,0:T(8,128)(2,1)S(1)}, u32[]{:S(2)}, u32[]{:S(2)}) collective-permute-start(bf16[272,512]{1,0:T(8,128)(2,1)S(1)} %bitcast.9), channel_id=1, source_target_pairs={{0,1},{1,0},{2,3},{3,2},{4,5},{5,4},{6,7},{7,6},{8,9},{9,8},{10,11... | collective-permute-start | bytes 835592 | tf_op jit(solution)/shard_map/gather_keys/ppermute | solution.py:274
  32.5 2.2 %collective-permute-start.11 = (bf16[272,512]{1,0:T(8,128)(2,1)S(1)}, bf16[272,512]{1,0:T(8,128)(2,1)S(1)}, u32[]{:S(2)}, u32[]{:S(2)}) collective-permute-start(bf16[272,512]{1,0:T(8,128)(2,1)S(1)} %bitcast.10), channel_id=1, source_target_pairs={{0,3},{1,2},{2,1},{3,0},{4,7},{5,6},{6,5},{7,4},{8,11},{9,10},{10,... | collective-permute-start | bytes 835592 | tf_op jit(solution)/shard_map/gather_keys/ppermute | solution.py:274
  34.7 2.7 %collective-permute-start.9 = (bf16[272,512]{1,0:T(8,128)(2,1)S(1)}, bf16[272,512]{1,0:T(8,128)(2,1)S(1)}, u32[]{:S(2)}, u32[]{:S(2)}) collective-permute-start(bf16[272,512]{1,0:T(8,128)(2,1)S(1)} %bitcast.11), channel_id=1, source_target_pairs={{0,2},{1,3},{2,0},{3,1},{4,6},{5,7},{6,4},{7,5},{8,10},{9,11},{10,... | collective-permute-start | bytes 835592 | tf_op jit(solution)/shard_map/gather_keys/ppermute | solution.py:274
  37.7 12.5 %attention_backward.2 = (f32[256,3072]{1,0:T(8,128)}, f32[256,1536]{1,0:T(8,128)}, f32[4,4,2,16,256]{4,3,2,1,0:T(8,128)}, bf16[4,4,2,16,256]{4,3,2,1,0:T(8,128)(...) custom-call(s32[3]{0:T(128)S(1)} %pad_add_fusion.meta, bf16[256,3072]{1,0:T(8,128)(2,1)} %bitcast.21, ...), custom_call_target="tpu_custom_call" | custom-call | flops 8000000000 | bytes 8388608 | tf_op jit(solution)/shard_map/attention_backward/pallas_call | solution.py:119
  50.2 2.7 %collective-permute-start.15 = (bf16[4,4,2,16,256]{4,3,2,1,0:T(8,128)(2,1)}, bf16[4,4,2,16,256]{4,3,2,1,0:T(8,128)(2,1)S(1)}, u32[]{:S(2)}, u32[]{:S(2)}) collective-permute-start(bf16[4,4,2,16,256]{4,3,2,1,0:T(8,128)(2,1)} %get-tuple-element.77), channel_id=1, source_target_pairs={{0,2},{1,3},{2,0},{3,1},{4,6},{5,7},{6,4},{7,5},{8,10},{9,11},{10,... | collective-permute-start | bytes 786440 | tf_op jit(solution)/shard_map/scatter_grads/ppermute | solution.py:274
  54.4 12.6 %attention_backward.3 = (f32[256,3072]{1,0:T(8,128)}, f32[256,1536]{1,0:T(8,128)}, f32[4,4,2,16,256]{4,3,2,1,0:T(8,128)}, bf16[4,4,2,16,256]{4,3,2,1,0:T(8,128)(...) custom-call(s32[3]{0:T(128)S(1)} %pad_add_fusion.meta, ...), custom_call_target="tpu_custom_call", output_to_operand_aliasing={{0}: (11, {}), {1}: (12, {})} | custom-call | flops 8000000000 | bytes 8388608 | tf_op jit(solution)/shard_map/attention_backward/pallas_call | solution.py:119
  67.5 2.7 %collective-permute-start.18 = (bf16[4,4,2,16,256]{4,3,2,1,0:T(8,128)(2,1)}, bf16[4,4,2,16,256]{4,3,2,1,0:T(8,128)(2,1)S(1)}, u32[]{:S(2)}, u32[]{:S(2)}) collective-permute-start(bf16[4,4,2,16,256]{4,3,2,1,0:T(8,128)(2,1)} %get-tuple-element.81), channel_id=1, source_target_pairs={{0,2},{1,3},{2,0},{3,1},{4,6},{5,7},{6,4},{7,5},{8,10},{9,11},{10,... | collective-permute-start | bytes 786440 | tf_op jit(solution)/shard_map/scatter_grads/ppermute | solution.py:274
  71.7 4.0 %collective-permute-done.18.refs_1_ = bf16[4,4,2,16,256]{4,3,2,1,0:T(8,128)(2,1)S(1)} collective-permute-done((bf16[4,4,2,16,256]{4,3,2,1,0:T(8,128)(2,1)}, bf16[4,4,2,16,256]{4,3,2,1,0:T(8,128)(2,1)S(1)}, u32[]{:S(2)}, u32[]{:S(2)}) %collective-permute-start.18) | collective-permute-done | bytes 262176 | tf_op jit(solution)/shard_map/scatter_grads/ppermute | solution.py:274
  75.7 2.6 %collective-permute-done.19.refs_2_ = bf16[4,4,2,16,256]{4,3,2,1,0:T(8,128)(2,1)S(1)} collective-permute-done((bf16[4,4,2,16,256]{4,3,2,1,0:T(8,128)(2,1)}, bf16[4,4,2,16,256]{4,3,2,1,0:T(8,128)(2,1)S(1)}, u32[]{:S(2)}, u32[]{:S(2)}) %collective-permute-start.19) | collective-permute-done | bytes 262176 | tf_op jit(solution)/shard_map/scatter_grads/ppermute | solution.py:274
  78.8 1.5 %collective-permute-start.21 = (bf16[2,4,2,16,256]{4,3,2,1,0:T(8,128)(2,1)S(1)}, bf16[2,4,2,16,256]{4,3,2,1,0:T(8,128)(2,1)S(1)}, u32[]{:S(2)}, u32[]{:S(2)}) collective-permute-start(bf16[2,4,2,16,256]{4,3,2,1,0:T(8,128)(2,1)S(1)} %get-tuple-element.97), channel_id=1, source_target_pairs={{0,8},{1,9},{2,10},{3,11},{4,12},{5,13},{6,14},{7,15},{8,0},{9,1},... | collective-permute-start | bytes 393224 | tf_op jit(solution)/shard_map/scatter_grads/ppermute | solution.py:274
  80.9 2.1 %collective-permute-start.24 = (bf16[2,4,2,16,256]{4,3,2,1,0:T(8,128)(2,1)S(1)}, bf16[2,4,2,16,256]{4,3,2,1,0:T(8,128)(2,1)S(1)}, u32[]{:S(2)}, u32[]{:S(2)}) collective-permute-start(bf16[2,4,2,16,256]{4,3,2,1,0:T(8,128)(2,1)S(1)} %get-tuple-element.104), channel_id=1, source_target_pairs={{0,12},{1,13},{2,14},{3,15},{4,8},{5,9},{6,10},{7,11},{8,4},{9,5},... | collective-permute-start | bytes 393224 | tf_op jit(solution)/shard_map/scatter_grads/ppermute | solution.py:274
  83.0 0.9 slice_dynamic-update-slice_fusion.1
  83.9 0.9 slice_dynamic-update-slice_fusion
  85.3 1.7 %collective-permute-done.24 = bf16[2,4,2,16,256]{4,3,2,1,0:T(8,128)(2,1)S(1)} collective-permute-done((bf16[2,4,2,16,256]{4,3,2,1,0:T(8,128)(2,1)S(1)}, bf16[2,4,2,16,256]{4,3,2,1,0:T(8,128)(2,1)S(1)}, u32[]{:S(2)}, u32[]{:S(2)}) %collective-permute-start.24) | collective-permute-done | bytes 131104 | tf_op jit(solution)/shard_map/scatter_grads/ppermute | solution.py:274
  87.2 12.1 %all_to_all.5.got = bf16[8,2,16,256]{3,2,1,0:T(8,128)(2,1)S(1)} all-to-all(bf16[8,2,16,256]{3,2,1,0:T(8,128)(2,1)S(1)} %bitcast.17), channel_id=1, replica_groups=mesh['zl'=2,'core'=2,'zh'=4,'x'=4,'y'=4] {'zl','zh'}, dimensions={0} | all-to-all | bytes 262144 | tf_op jit(solution)/shard_map/scatter_grads/all_to_all | solution.py:351
  (45 shorter events, 11.6 us)
Async XLA Ops:
  2.1 23.8 %collective-permute-start.6 = (bf16[256,3072]{1,0:T(8,128)(2,1)}, bf16[256,3072]{1,0:T(8,128)(2,1)S(1)}, u32[]{:S(2)}, u32[]{:S(2)}) collective-permute-start(bf16[256,3072]{1,0:T(8,128)(2,1)} %bitcast.20), channel_id=1, source_target_pairs={{0,64},{64,0},{1,65},{65,1},{2,66},{66,2},{3,67},{67,3},{4,68},{68... | collective-permute-start | bytes 4718600 | tf_op jit(solution)/shard_map/gather_keys/swap_queries/ppermute | solution.py:298
  2.2 23.7 %collective-permute-start.7 = (bf16[256,3072]{1,0:T(8,128)(2,1)}, bf16[256,3072]{1,0:T(8,128)(2,1)}, u32[]{:S(2)}, u32[]{:S(2)}) collective-permute-start(bf16[256,3072]{1,0:T(8,128)(2,1)} %bitcast.23), channel_id=1, source_target_pairs={{0,64},{64,0},{1,65},{65,1},{2,66},{66,2},{3,67},{67,3},{4,68},{68... | collective-permute-start | bytes 4718600 | tf_op jit(solution)/shard_map/gather_keys/swap_queries/ppermute | solution.py:298
  2.7 7.8 %collective-permute-start = (bf16[2,16,640]{2,1,0:T(8,128)(2,1)S(1)}, bf16[2,16,640]{2,1,0:T(8,128)(2,1)S(1)}, u32[]{:S(2)}, u32[]{:S(2)}) collective-permute-start(bf16[2,16,640]{2,1,0:T(8,128)(2,1)S(1)} %pack_keys_values.1.own), channel_id=1, source_target_pairs={{0,160},{128,32},{16,176},{144,48},{32,128},{160,0},{48,144},{176,... | collective-permute-start | bytes 122888 | tf_op jit(solution)/shard_map/gather_keys/ppermute | solution.py:287
  9.5 6.1 %collective-permute-start.2 = (bf16[2,16,640]{2,1,0:T(8,128)(2,1)S(1)}, bf16[2,16,640]{2,1,0:T(8,128)(2,1)S(1)}, u32[]{:S(2)}, u32[]{:S(2)}) collective-permute-start(bf16[2,16,640]{2,1,0:T(8,128)(2,1)S(1)} %pack_keys_values.1.own), channel_id=1, source_target_pairs={{0,48},{128,144},{16,0},{144,160},{32,16},{160,176},{48,32},{176,1... | collective-permute-start | bytes 122888 | tf_op jit(solution)/shard_map/gather_keys/ppermute | solution.py:287
  10.5 8.9 %collective-permute-start.8 = (f32[24,256]{1,0:T(8,128)}, f32[24,256]{1,0:T(8,128)S(1)}, u32[]{:S(2)}, u32[]{:S(2)}) collective-permute-start(f32[24,256]{1,0:T(8,128)} %bitcast.18), channel_id=1, source_target_pairs={{0,64},{64,0},{1,65},{65,1},{2,66},{66,2},{3,67},{67,3},{4,68},{68... | collective-permute-start | bytes 73736 | tf_op jit(solution)/shard_map/gather_keys/swap_queries/ppermute | solution.py:298
  15.7 6.9 %collective-permute-start.3 = (bf16[2,4,16,640]{3,2,1,0:T(8,128)(2,1)S(1)}, bf16[2,4,16,640]{3,2,1,0:T(8,128)(2,1)S(1)}, u32[]{:S(2)}, u32[]{:S(2)}) collective-permute-start(bf16[2,4,16,640]{3,2,1,0:T(8,128)(2,1)S(1)} %join_line.1.refs_0_), channel_id=1, source_target_pairs={{0,8},{1,9},{2,10},{3,11},{4,12},{5,13},{6,14},{7,15},{8,0},{9,1},... | collective-permute-start | bytes 491528 | tf_op jit(solution)/shard_map/gather_keys/ppermute | solution.py:274
  18.8 5.6 %collective-permute-start.4 = (bf16[2,4,16,640]{3,2,1,0:T(8,128)(2,1)S(1)}, bf16[2,4,16,640]{3,2,1,0:T(8,128)(2,1)S(1)}, u32[]{:S(2)}, u32[]{:S(2)}) collective-permute-start(bf16[2,4,16,640]{3,2,1,0:T(8,128)(2,1)S(1)} %join_line.1.refs_0_), channel_id=1, source_target_pairs={{0,4},{1,5},{2,6},{3,7},{4,0},{5,1},{6,2},{7,3},{8,12},{9,13},{10,... | collective-permute-start | bytes 491528 | tf_op jit(solution)/shard_map/gather_keys/ppermute | solution.py:274
  19.4 6.5 %collective-permute-start.5 = (bf16[2,4,16,640]{3,2,1,0:T(8,128)(2,1)S(1)}, bf16[2,4,16,640]{3,2,1,0:T(8,128)(2,1)S(1)}, u32[]{:S(2)}, u32[]{:S(2)}) collective-permute-start(bf16[2,4,16,640]{3,2,1,0:T(8,128)(2,1)S(1)} %join_line.1.refs_0_), channel_id=1, source_target_pairs={{0,12},{1,13},{2,14},{3,15},{4,8},{5,9},{6,10},{7,11},{8,4},{9,5},... | collective-permute-start | bytes 491528 | tf_op jit(solution)/shard_map/gather_keys/ppermute | solution.py:274
  26.0 8.7 %collective-permute-start.12 = (bf16[272,512]{1,0:T(8,128)(2,1)S(1)}, bf16[272,512]{1,0:T(8,128)(2,1)S(1)}, u32[]{:S(2)}, u32[]{:S(2)}) collective-permute-start(bf16[272,512]{1,0:T(8,128)(2,1)S(1)} %bitcast.13), channel_id=1, source_target_pairs={{0,2},{1,3},{2,0},{3,1},{4,6},{5,7},{6,4},{7,5},{8,10},{9,11},{10,... | collective-permute-start | bytes 835592 | tf_op jit(solution)/shard_map/gather_keys/ppermute | solution.py:274
  29.3 8.2 %collective-permute-start.13 = (bf16[272,512]{1,0:T(8,128)(2,1)S(1)}, bf16[272,512]{1,0:T(8,128)(2,1)S(1)}, u32[]{:S(2)}, u32[]{:S(2)}) collective-permute-start(bf16[272,512]{1,0:T(8,128)(2,1)S(1)} %bitcast.14), channel_id=1, source_target_pairs={{0,1},{1,0},{2,3},{3,2},{4,5},{5,4},{6,7},{7,6},{8,9},{9,8},{10,11... | collective-permute-start | bytes 835592 | tf_op jit(solution)/shard_map/gather_keys/ppermute | solution.py:274
  29.9 7.8 %collective-permute-start.14 = (bf16[272,512]{1,0:T(8,128)(2,1)S(1)}, bf16[272,512]{1,0:T(8,128)(2,1)S(1)}, u32[]{:S(2)}, u32[]{:S(2)}) collective-permute-start(bf16[272,512]{1,0:T(8,128)(2,1)S(1)} %bitcast.15), channel_id=1, source_target_pairs={{0,3},{1,2},{2,1},{3,0},{4,7},{5,6},{6,5},{7,4},{8,11},{9,10},{10,... | collective-permute-start | bytes 835592 | tf_op jit(solution)/shard_map/gather_keys/ppermute | solution.py:274
  31.0 22.5 %collective-permute-start.10 = (bf16[272,512]{1,0:T(8,128)(2,1)S(1)}, bf16[272,512]{1,0:T(8,128)(2,1)S(1)}, u32[]{:S(2)}, u32[]{:S(2)}) collective-permute-start(bf16[272,512]{1,0:T(8,128)(2,1)S(1)} %bitcast.9), channel_id=1, source_target_pairs={{0,1},{1,0},{2,3},{3,2},{4,5},{5,4},{6,7},{7,6},{8,9},{9,8},{10,11... | collective-permute-start | bytes 835592 | tf_op jit(solution)/shard_map/gather_keys/ppermute | solution.py:274
  32.5 21.9 %collective-permute-start.11 = (bf16[272,512]{1,0:T(8,128)(2,1)S(1)}, bf16[272,512]{1,0:T(8,128)(2,1)S(1)}, u32[]{:S(2)}, u32[]{:S(2)}) collective-permute-start(bf16[272,512]{1,0:T(8,128)(2,1)S(1)} %bitcast.10), channel_id=1, source_target_pairs={{0,3},{1,2},{2,1},{3,0},{4,7},{5,6},{6,5},{7,4},{8,11},{9,10},{10,... | collective-permute-start | bytes 835592 | tf_op jit(solution)/shard_map/gather_keys/ppermute | solution.py:274
  34.7 19.7 %collective-permute-start.9 = (bf16[272,512]{1,0:T(8,128)(2,1)S(1)}, bf16[272,512]{1,0:T(8,128)(2,1)S(1)}, u32[]{:S(2)}, u32[]{:S(2)}) collective-permute-start(bf16[272,512]{1,0:T(8,128)(2,1)S(1)} %bitcast.11), channel_id=1, source_target_pairs={{0,2},{1,3},{2,0},{3,1},{4,6},{5,7},{6,4},{7,5},{8,10},{9,11},{10,... | collective-permute-start | bytes 835592 | tf_op jit(solution)/shard_map/gather_keys/ppermute | solution.py:274
  50.2 16.8 %collective-permute-start.15 = (bf16[4,4,2,16,256]{4,3,2,1,0:T(8,128)(2,1)}, bf16[4,4,2,16,256]{4,3,2,1,0:T(8,128)(2,1)S(1)}, u32[]{:S(2)}, u32[]{:S(2)}) collective-permute-start(bf16[4,4,2,16,256]{4,3,2,1,0:T(8,128)(2,1)} %get-tuple-element.77), channel_id=1, source_target_pairs={{0,2},{1,3},{2,0},{3,1},{4,6},{5,7},{6,4},{7,5},{8,10},{9,11},{10,... | collective-permute-start | bytes 786440 | tf_op jit(solution)/shard_map/scatter_grads/ppermute | solution.py:274
  52.9 14.1 %collective-permute-start.16 = (bf16[4,4,2,16,256]{4,3,2,1,0:T(8,128)(2,1)}, bf16[4,4,2,16,256]{4,3,2,1,0:T(8,128)(2,1)S(1)}, u32[]{:S(2)}, u32[]{:S(2)}) collective-permute-start(bf16[4,4,2,16,256]{4,3,2,1,0:T(8,128)(2,1)} %get-tuple-element.78), channel_id=1, source_target_pairs={{0,1},{1,0},{2,3},{3,2},{4,5},{5,4},{6,7},{7,6},{8,9},{9,8},{10,11... | collective-permute-start | bytes 786440 | tf_op jit(solution)/shard_map/scatter_grads/ppermute | solution.py:274
  53.6 13.4 %collective-permute-start.17 = (bf16[4,4,2,16,256]{4,3,2,1,0:T(8,128)(2,1)}, bf16[4,4,2,16,256]{4,3,2,1,0:T(8,128)(2,1)S(1)}, u32[]{:S(2)}, u32[]{:S(2)}) collective-permute-start(bf16[4,4,2,16,256]{4,3,2,1,0:T(8,128)(2,1)} %get-tuple-element.79), channel_id=1, source_target_pairs={{0,3},{1,2},{2,1},{3,0},{4,7},{5,6},{6,5},{7,4},{8,11},{9,10},{10,... | collective-permute-start | bytes 786440 | tf_op jit(solution)/shard_map/scatter_grads/ppermute | solution.py:274
  67.2 15.8 %collective-permute-start.22 = (f32[256,1536]{1,0:T(8,128)}, f32[256,1536]{1,0:T(8,128)S(1)}, u32[]{:S(2)}, u32[]{:S(2)}) collective-permute-start(f32[256,1536]{1,0:T(8,128)} %get-tuple-element.99), channel_id=1, source_target_pairs={{0,64},{64,0},{1,65},{65,1},{2,66},{66,2},{3,67},{67,3},{4,68},{68... | collective-permute-start | bytes 4718600 | tf_op jit(solution)/shard_map/swap_query_grads/ppermute | solution.py:298
  67.5 8.2 %collective-permute-start.18 = (bf16[4,4,2,16,256]{4,3,2,1,0:T(8,128)(2,1)}, bf16[4,4,2,16,256]{4,3,2,1,0:T(8,128)(2,1)S(1)}, u32[]{:S(2)}, u32[]{:S(2)}) collective-permute-start(bf16[4,4,2,16,256]{4,3,2,1,0:T(8,128)(2,1)} %get-tuple-element.81), channel_id=1, source_target_pairs={{0,2},{1,3},{2,0},{3,1},{4,6},{5,7},{6,4},{7,5},{8,10},{9,11},{10,... | collective-permute-start | bytes 786440 | tf_op jit(solution)/shard_map/scatter_grads/ppermute | solution.py:274
  70.2 8.0 %collective-permute-start.19 = (bf16[4,4,2,16,256]{4,3,2,1,0:T(8,128)(2,1)}, bf16[4,4,2,16,256]{4,3,2,1,0:T(8,128)(2,1)S(1)}, u32[]{:S(2)}, u32[]{:S(2)}) collective-permute-start(bf16[4,4,2,16,256]{4,3,2,1,0:T(8,128)(2,1)} %get-tuple-element.82), channel_id=1, source_target_pairs={{0,1},{1,0},{2,3},{3,2},{4,5},{5,4},{6,7},{7,6},{8,9},{9,8},{10,11... | collective-permute-start | bytes 786440 | tf_op jit(solution)/shard_map/scatter_grads/ppermute | solution.py:274
  70.9 7.8 %collective-permute-start.20 = (bf16[4,4,2,16,256]{4,3,2,1,0:T(8,128)(2,1)}, bf16[4,4,2,16,256]{4,3,2,1,0:T(8,128)(2,1)S(1)}, u32[]{:S(2)}, u32[]{:S(2)}) collective-permute-start(bf16[4,4,2,16,256]{4,3,2,1,0:T(8,128)(2,1)} %get-tuple-element.83), channel_id=1, source_target_pairs={{0,3},{1,2},{2,1},{3,0},{4,7},{5,6},{6,5},{7,4},{8,11},{9,10},{10,... | collective-permute-start | bytes 786440 | tf_op jit(solution)/shard_map/scatter_grads/ppermute | solution.py:274
  78.8 6.6 %collective-permute-start.21 = (bf16[2,4,2,16,256]{4,3,2,1,0:T(8,128)(2,1)S(1)}, bf16[2,4,2,16,256]{4,3,2,1,0:T(8,128)(2,1)S(1)}, u32[]{:S(2)}, u32[]{:S(2)}) collective-permute-start(bf16[2,4,2,16,256]{4,3,2,1,0:T(8,128)(2,1)S(1)} %get-tuple-element.97), channel_id=1, source_target_pairs={{0,8},{1,9},{2,10},{3,11},{4,12},{5,13},{6,14},{7,15},{8,0},{9,1},... | collective-permute-start | bytes 393224 | tf_op jit(solution)/shard_map/scatter_grads/ppermute | solution.py:274
  80.3 5.0 %collective-permute-start.23 = (bf16[2,4,2,16,256]{4,3,2,1,0:T(8,128)(2,1)S(1)}, bf16[2,4,2,16,256]{4,3,2,1,0:T(8,128)(2,1)S(1)}, u32[]{:S(2)}, u32[]{:S(2)}) collective-permute-start(bf16[2,4,2,16,256]{4,3,2,1,0:T(8,128)(2,1)S(1)} %get-tuple-element.103), channel_id=1, source_target_pairs={{0,4},{1,5},{2,6},{3,7},{4,0},{5,1},{6,2},{7,3},{8,12},{9,13},{10,... | collective-permute-start | bytes 393224 | tf_op jit(solution)/shard_map/scatter_grads/ppermute | solution.py:274
  80.9 6.2 %collective-permute-start.24 = (bf16[2,4,2,16,256]{4,3,2,1,0:T(8,128)(2,1)S(1)}, bf16[2,4,2,16,256]{4,3,2,1,0:T(8,128)(2,1)S(1)}, u32[]{:S(2)}, u32[]{:S(2)}) collective-permute-start(bf16[2,4,2,16,256]{4,3,2,1,0:T(8,128)(2,1)S(1)} %get-tuple-element.104), channel_id=1, source_target_pairs={{0,12},{1,13},{2,14},{3,15},{4,8},{5,9},{6,10},{7,11},{8,4},{9,5},... | collective-permute-start | bytes 393224 | tf_op jit(solution)/shard_map/scatter_grads/ppermute | solution.py:274
  (3 other events, 28.5 us)
